TPU v7x, 32 devices: a whole 2x2x4 slice. The times are simulated.
32 devices in a mesh: dp: 2 (over x), blk: 4 (over y, core), ulysses: 4 (over z).
Axes of the slice: x: 2, y: 2, z: 4, core: 2. Of those that a mesh axis runs over, the one named last changes fastest.
Arguments:
- tokens: bfloat16 [8192, 2304], P(('dp', 'blk', 'ulysses')), may hold values from -6 to 6
- query_weight: bfloat16 [2304, 2048], P(('dp', 'blk')), may hold values from -0.125 to 0.125
- key_projection: bfloat16 [2304, 1024], P(('dp', 'blk')), may hold values from -0.125 to 0.125
- value_projection: bfloat16 [2304, 1024], P(('dp', 'blk')), may hold values from -0.125 to 0.125
- out_weight: bfloat16 [2048, 2304], P(('dp', 'blk')), may hold values from -0.125 to 0.125
- gate_weight: bfloat16 [2304, 9216], P(('dp', 'blk')), may hold values from -0.125 to 0.125
- up_weight: bfloat16 [2304, 9216], P(('dp', 'blk')), may hold values from -0.125 to 0.125
- down_weight: bfloat16 [9216, 2304], P(('dp', 'blk')), may hold values from -0.0625 to 0.0625
- attn_in_gain: float32 [2304], replicated, may hold values from 0.5 to 1.5
- attn_out_gain: float32 [2304], replicated, may hold values from 0.5 to 1.5
- feed_in_gain: float32 [2304], replicated, may hold values from 0.5 to 1.5
- feed_out_gain: float32 [2304], replicated, may hold values from 0.5 to 1.5
- adapt_heads_in: bfloat16 [8, 3, 16, 2304], replicated, may hold values from -0.125 to 0.125
- adapt_query_out: bfloat16 [8, 16, 2048], replicated, may hold values from -0.75 to 0.75
- adapter_key_value_second: bfloat16 [8, 2, 16, 1024], replicated, may hold values from -0.75 to 0.75
- adapt_mix_in: bfloat16 [8, 16, 2048], replicated, may hold values from -0.125 to 0.125
- adapt_mix_out: bfloat16 [8, 16, 2304], replicated, may hold values from -0.75 to 0.75
- adapt_feed_in: bfloat16 [8, 2, 16, 2304], replicated, may hold values from -0.125 to 0.125
- adapt_feed_out: bfloat16 [8, 2, 16, 9216], replicated, may hold values from -0.75 to 0.75
- adapt_down_in: bfloat16 [8, 16, 9216], replicated, may hold values from -0.0625 to 0.0625
- adapt_down_out: bfloat16 [8, 16, 2304], replicated, may hold values from -0.75 to 0.75
- adapter_ids: int32 [2, 9], P('dp'), may hold values from 0 to 7
- cotangent: bfloat16 [8192, 2304], P(('dp', 'blk', 'ulysses')), may hold values from -6 to 6
Outputs:
- layer_out: bfloat16 [8192, 2304], P(('dp', 'blk', 'ulysses'))
- tokens_grad: float32 [8192, 2304], P(('dp', 'blk', 'ulysses'))
- grad_heads_in: float32 [8, 3, 16, 2304], replicated
- grad_query_out: float32 [8, 16, 2048], replicated
- grad_kv_out: float32 [8, 2, 16, 1024], replicated
- grad_mix_in: float32 [8, 16, 2048], replicated
- grad_mix_out: float32 [8, 16, 2304], replicated
- grad_feed_in: float32 [8, 2, 16, 2304], replicated
- grad_feed_out: float32 [8, 2, 16, 9216], replicated
- grad_down_in: float32 [8, 16, 9216], replicated
- grad_down_out: float32 [8, 16, 2304], replicated
All inputs are finite; a program needn't handle non-finite values.
Results may differ from a plain program's by a relative error of at most 0.025.
Values may be sent and summed in bfloat16 or wider, within the bound.
A program may use at most 384 MiB of HBM per device.

v0:
```python
import jax
import jax.numpy as jnp
from jax import lax
from jax.sharding import PartitionSpec as P

HEADS = 8
KV_HEADS = 4
HEAD = 256
ADAPTER_RANK = 16
ADAPTER_COUNT = 8
PROMPT = 2048
CONT = 256
CONTS = 8
HQ = 2048
KEY_VALUE_WIDTH = 1024


epsilon = 1e-06
soft_cap = 50.0
rope_base = 10000.0
masked_value = -1e30


def gathered_then(share, axis, dim, apply):
    everything = lax.all_gather(share, axis, axis=dim, tiled=True)
    return apply(everything, jnp.int32(0))


def rms_scale(values, gain_row):
    return (
        values * lax.rsqrt(jnp.mean(values * values, axis=-1, keepdims=True) + epsilon) * gain_row
    )


def norm_back(values, gain_row, grad_out):
    _, pullback = jax.vjp(lambda values_in: rms_scale(values_in, gain_row), values)
    return pullback(grad_out)[0]


def segment_of(token_index):
    return jnp.where(token_index >= PROMPT, 1 + (token_index - PROMPT) // CONT, 0)


def position_of(token_index):
    return jnp.where(token_index >= PROMPT, PROMPT + (token_index - PROMPT) % CONT, token_index)


def can_see(query_index, query_segment, key_index, key_segment):
    earlier = key_index <= query_index
    return (key_segment == 0) & ((query_segment > 0) | earlier) | (
        key_segment == query_segment
    ) & earlier


def rotate(head_values, positions):
    half_size = HEAD // 2
    inverse = rope_base ** (-2.0 * jnp.arange(half_size, dtype=jnp.float32) / HEAD)
    angles = positions.astype(jnp.float32)[:, None] * inverse[None, :]
    cosine = jnp.cos(angles)[:, None, :]
    sine_part = jnp.sin(angles)[:, None, :]
    first_half = head_values[..., :half_size]
    second_half = head_values[..., half_size:]
    return jnp.concatenate(
        [
            first_half * cosine - second_half * sine_part,
            second_half * cosine + first_half * sine_part,
        ],
        axis=-1,
    )


def adapter_columns(adapters):
    lane_owner = jnp.arange(ADAPTER_COUNT * ADAPTER_RANK, dtype=jnp.int32) // ADAPTER_RANK
    return (adapters[:, None] == lane_owner[None, :]).astype(jnp.float32)


def flat_table(table):
    return table.reshape(ADAPTER_COUNT * ADAPTER_RANK, table.shape[-1])


def contract_last(former, latter):
    return lax.dot_general(
        former, latter, (((1,), (1,)), ((), ())), preferred_element_type=jnp.float32
    )


def contract_first(former, latter):
    return lax.dot_general(
        former, latter, (((0,), (0,)), ((), ())), preferred_element_type=jnp.float32
    )


def narrow_down(inputs, table_in, columns):
    return (contract_last(inputs, flat_table(table_in)) * columns).astype(jnp.bfloat16)


def widen(narrow, table_out):
    return jnp.dot(narrow, flat_table(table_out), preferred_element_type=jnp.float32)


def low_rank_back(inputs, narrow, grad_out, table_in, table_out, columns):
    back_narrow = (contract_last(grad_out, flat_table(table_out)) * columns).astype(jnp.bfloat16)
    grad_in_table = contract_first(back_narrow, inputs).reshape(table_in.shape)
    grad_out_table = contract_first(narrow, grad_out).reshape(table_out.shape)
    grad_inputs = jnp.dot(back_narrow, flat_table(table_in), preferred_element_type=jnp.float32)
    return (grad_inputs, grad_in_table, grad_out_table)


def shards(
    tokens,
    query_weight,
    key_projection,
    value_projection,
    out_weight,
    gate_weight,
    up_weight,
    down_weight,
    attn_in_gain,
    attn_out_gain,
    feed_in_gain,
    feed_out_gain,
    adapt_heads_in,
    adapt_query_out,
    adapter_key_value_second,
    adapt_mix_in,
    adapt_mix_out,
    adapt_feed_in,
    adapt_feed_out,
    adapt_down_in,
    adapt_down_out,
    adapter_ids,
    cotangent,
):
    sequence_local_rows = tokens.shape[0]
    cycle_count = lax.axis_size("blk")
    swap_count = lax.axis_size("ulysses")
    block_rows = sequence_local_rows * swap_count
    kv_local = KV_HEADS // swap_count
    sharing = HEADS // KV_HEADS
    first_row = (
        lax.axis_index("blk") * swap_count + lax.axis_index("ulysses")
    ) * sequence_local_rows
    token_index = first_row + jnp.arange(sequence_local_rows, dtype=jnp.int32)
    segments = segment_of(token_index)
    positions = position_of(token_index)
    sequence_ids = jnp.arange(CONTS + 1, dtype=jnp.int32)
    adapters = jnp.sum(
        jnp.where(segments[:, None] == sequence_ids[None, :], adapter_ids[0][None, :], 0), axis=1
    )
    columns = adapter_columns(adapters)
    residual = tokens.astype(jnp.float32)
    normed = rms_scale(residual, attn_in_gain).astype(jnp.bfloat16)
    query_full, key_full, value_full, out_full = (
        lax.all_gather(query_weight, ("dp", "blk"), axis=0, tiled=True),
        lax.all_gather(key_projection, ("dp", "blk"), axis=0, tiled=True),
        lax.all_gather(value_projection, ("dp", "blk"), axis=0, tiled=True),
        lax.all_gather(out_weight, ("dp", "blk"), axis=0, tiled=True),
    )
    narrow_query = narrow_down(normed, adapt_heads_in[:, 0], columns)
    narrow_key = narrow_down(normed, adapt_heads_in[:, 1], columns)
    narrow_value = narrow_down(normed, adapt_heads_in[:, 2], columns)
    query_pre = jnp.dot(normed, query_full, preferred_element_type=jnp.float32) + widen(
        narrow_query, adapt_query_out
    )
    key_pre = jnp.dot(normed, key_full, preferred_element_type=jnp.float32) + widen(
        narrow_key, adapter_key_value_second[:, 0]
    )
    value_rows = (
        jnp.dot(normed, value_full, preferred_element_type=jnp.float32)
        + widen(narrow_value, adapter_key_value_second[:, 1])
    ).astype(jnp.bfloat16)
    query_rows = (
        rotate(query_pre.reshape(sequence_local_rows, HEADS, HEAD), positions) * HEAD ** (-0.5)
    ).astype(jnp.bfloat16)
    key_rows = rotate(key_pre.reshape(sequence_local_rows, KV_HEADS, HEAD), positions).astype(
        jnp.bfloat16
    )
    query_swap, key_swap, value_swap = (
        lax.all_to_all(
            query_rows.reshape(sequence_local_rows, swap_count, -1),
            "ulysses",
            split_axis=1,
            concat_axis=0,
            tiled=True,
        ),
        lax.all_to_all(key_rows, "ulysses", split_axis=1, concat_axis=0, tiled=True),
        lax.all_to_all(
            value_rows.reshape(sequence_local_rows, swap_count, -1),
            "ulysses",
            split_axis=1,
            concat_axis=0,
            tiled=True,
        ),
    )
    query_heads = query_swap.reshape(block_rows, kv_local, sharing, HEAD)
    head_index = lax.axis_index("blk") * block_rows + jnp.arange(block_rows, dtype=jnp.int32)
    head_segments = segment_of(head_index)
    key_all, value_all = (
        lax.all_gather(key_swap, "blk", axis=0, tiled=True),
        lax.all_gather(value_swap, "blk", axis=0, tiled=True),
    )
    key_blocks = key_all.reshape(cycle_count, block_rows, kv_local, HEAD)
    value_blocks = value_all.reshape(cycle_count, block_rows, kv_local, HEAD)
    block_index = jnp.arange(cycle_count * block_rows, dtype=jnp.int32).reshape(
        cycle_count, block_rows
    )

    def visible_of(key_index):
        return can_see(
            head_index[:, None],
            head_segments[:, None],
            key_index[None, :],
            segment_of(key_index)[None, :],
        )

    def forward_block(carried, element):
        key_block, value_block, key_index = element
        visible = visible_of(key_index)

        def update(running):
            running_top, running_sum, weighted = running
            scores = jnp.einsum(
                "qngd,knd->ngqk", query_heads, key_block, preferred_element_type=jnp.float32
            )
            capped = jnp.where(visible, soft_cap * jnp.tanh(scores / soft_cap), masked_value)
            new_top = jnp.maximum(running_top, jnp.max(capped, axis=-1))
            shrink = jnp.exp(running_top - new_top)
            exp_scores = jnp.exp(capped - new_top[..., None])
            running_sum = running_sum * shrink + jnp.sum(exp_scores, axis=-1)
            weighted = weighted * jnp.transpose(shrink, (2, 0, 1))[..., None] + jnp.einsum(
                "ngqk,knd->qngd",
                exp_scores.astype(jnp.bfloat16),
                value_block,
                preferred_element_type=jnp.float32,
            )
            return (new_top, running_sum, weighted)

        return (lax.cond(jnp.any(visible), update, lambda running: running, carried), None)

    start_state = (
        jnp.full((kv_local, sharing, block_rows), masked_value, jnp.float32),
        jnp.zeros((kv_local, sharing, block_rows), jnp.float32),
        jnp.zeros((block_rows, kv_local, sharing, HEAD), jnp.float32),
    )
    (running_top, running_sum, weighted), _ = lax.scan(
        forward_block, start_state, (key_blocks, value_blocks, block_index)
    )
    attended = weighted / jnp.transpose(running_sum, (2, 0, 1))[..., None]
    log_total = running_top + jnp.log(running_sum)
    mixed_heads = lax.all_to_all(
        attended.astype(jnp.bfloat16).reshape(block_rows, -1),
        "ulysses",
        split_axis=0,
        concat_axis=1,
        tiled=True,
    )
    narrow_mix = narrow_down(mixed_heads, adapt_mix_in, columns)
    attn_out = jnp.dot(mixed_heads, out_full, preferred_element_type=jnp.float32) + widen(
        narrow_mix, adapt_mix_out
    )
    middle = residual + rms_scale(attn_out, attn_out_gain)
    normed_feed = rms_scale(middle, feed_in_gain).astype(jnp.bfloat16)
    narrow_gate = narrow_down(normed_feed, adapt_feed_in[:, 0], columns)
    narrow_up = narrow_down(normed_feed, adapt_feed_in[:, 1], columns)
    inputs = normed_feed
    gate_pre = jnp.dot(
        inputs,
        lax.all_gather(gate_weight, ("dp", "blk"), axis=0, tiled=True),
        preferred_element_type=jnp.float32,
    )
    up_pre = jnp.dot(
        inputs,
        lax.all_gather(up_weight, ("dp", "blk"), axis=0, tiled=True),
        preferred_element_type=jnp.float32,
    )
    gate_pre = gate_pre + widen(narrow_gate, adapt_feed_out[:, 0])
    up_pre = up_pre + widen(narrow_up, adapt_feed_out[:, 1])
    hidden = (jax.nn.gelu(gate_pre, approximate=True) * up_pre).astype(jnp.bfloat16)
    narrow_hidden = narrow_down(hidden, adapt_down_in, columns)
    inputs = hidden
    branch = jnp.dot(
        inputs,
        lax.all_gather(down_weight, ("dp", "blk"), axis=0, tiled=True),
        preferred_element_type=jnp.float32,
    )
    branch = branch + widen(narrow_hidden, adapt_down_out)
    layer_out = (middle + rms_scale(branch, feed_out_gain)).astype(jnp.bfloat16)
    grad_top = cotangent.astype(jnp.float32)
    grad_branch = norm_back(branch, feed_out_gain, grad_top).astype(jnp.bfloat16)
    lowrank_hidden, grad_down_in, grad_down_out = low_rank_back(
        hidden, narrow_hidden, grad_branch, adapt_down_in, adapt_down_out, columns
    )
    grad_hidden = gathered_then(
        down_weight,
        ("dp", "blk"),
        0,
        lambda weight_rows, row_start: contract_last(grad_branch, weight_rows),
    )
    grad_hidden = grad_hidden + lowrank_hidden
    _, glu_pullback = jax.vjp(
        lambda gate_in, up_in: jax.nn.gelu(gate_in, approximate=True) * up_in, gate_pre, up_pre
    )
    grad_gate, grad_up = glu_pullback(grad_hidden)
    grad_gate = grad_gate.astype(jnp.bfloat16)
    grad_up = grad_up.astype(jnp.bfloat16)
    lowrank_gate, grad_gate_in, grad_gate_out = low_rank_back(
        normed_feed, narrow_gate, grad_gate, adapt_feed_in[:, 0], adapt_feed_out[:, 0], columns
    )
    lowrank_up, grad_up_in, grad_up_out = low_rank_back(
        normed_feed, narrow_up, grad_up, adapt_feed_in[:, 1], adapt_feed_out[:, 1], columns
    )
    grad_feed = gathered_then(
        (gate_weight, up_weight),
        ("dp", "blk"),
        0,
        lambda weight_rows, row_start: contract_last(grad_gate, weight_rows[0])
        + contract_last(grad_up, weight_rows[1]),
    )
    grad_middle = grad_top + norm_back(middle, feed_in_gain, grad_feed + lowrank_gate + lowrank_up)
    grad_attn = norm_back(attn_out, attn_out_gain, grad_middle).astype(jnp.bfloat16)
    query_again, key_again, value_again, out_again = (
        lax.all_gather(query_weight, ("dp", "blk"), axis=0, tiled=True),
        lax.all_gather(key_projection, ("dp", "blk"), axis=0, tiled=True),
        lax.all_gather(value_projection, ("dp", "blk"), axis=0, tiled=True),
        lax.all_gather(out_weight, ("dp", "blk"), axis=0, tiled=True),
    )
    lowrank_mix, grad_mix_in, grad_mix_out = low_rank_back(
        mixed_heads, narrow_mix, grad_attn, adapt_mix_in, adapt_mix_out, columns
    )
    grad_mixed = (contract_last(grad_attn, out_again) + lowrank_mix).astype(jnp.bfloat16)
    grad_heads = lax.all_to_all(
        grad_mixed.reshape(sequence_local_rows, swap_count, -1),
        "ulysses",
        split_axis=1,
        concat_axis=0,
        tiled=True,
    ).reshape(block_rows, kv_local, sharing, HEAD)
    delta_rows = jnp.transpose(
        jnp.sum(grad_heads.astype(jnp.float32) * attended, axis=-1), (1, 2, 0)
    )

    def backward_block(grad_query, element):
        key_block, value_block, key_index = element
        visible = visible_of(key_index)

        def compute(grad_carry):
            scores = jnp.einsum(
                "qngd,knd->ngqk", query_heads, key_block, preferred_element_type=jnp.float32
            )
            tanh_scores = jnp.tanh(scores / soft_cap)
            capped = jnp.where(visible, soft_cap * tanh_scores, masked_value)
            attn_probs = jnp.exp(capped - log_total[..., None])
            grad_value = jnp.einsum(
                "ngqk,qngd->knd",
                attn_probs.astype(jnp.bfloat16),
                grad_heads,
                preferred_element_type=jnp.float32,
            )
            grad_probs = jnp.einsum(
                "qngd,knd->ngqk", grad_heads, value_block, preferred_element_type=jnp.float32
            )
            grad_scores = (
                attn_probs
                * (grad_probs - delta_rows[..., None])
                * (1.0 - tanh_scores * tanh_scores)
            ).astype(jnp.bfloat16)
            grad_carry = grad_carry + jnp.einsum(
                "ngqk,knd->qngd", grad_scores, key_block, preferred_element_type=jnp.float32
            )
            grad_key = jnp.einsum(
                "ngqk,qngd->knd", grad_scores, query_heads, preferred_element_type=jnp.float32
            )
            return (grad_carry, (grad_key, grad_value))

        def skip_block(grad_carry):
            nothing = jnp.zeros((block_rows, kv_local, HEAD), jnp.float32)
            return (grad_carry, (nothing, nothing))

        return lax.cond(jnp.any(visible), compute, skip_block, grad_query)

    grad_query, (grad_key_all, grad_value_all) = lax.scan(
        backward_block,
        jnp.zeros((block_rows, kv_local, sharing, HEAD), jnp.float32),
        (key_blocks, value_blocks, block_index),
    )
    grad_key_own, grad_value_own = (
        lax.psum_scatter(
            grad_key_all.reshape(cycle_count * block_rows, kv_local, HEAD).astype(jnp.bfloat16),
            "blk",
            scatter_dimension=0,
            tiled=True,
        ).astype(jnp.float32),
        lax.psum_scatter(
            grad_value_all.reshape(cycle_count * block_rows, kv_local, HEAD).astype(jnp.bfloat16),
            "blk",
            scatter_dimension=0,
            tiled=True,
        ).astype(jnp.float32),
    )
    grad_query_rows, grad_key_rows, grad_value_rows = (
        lax.all_to_all(
            grad_query.astype(jnp.bfloat16).reshape(block_rows, -1),
            "ulysses",
            split_axis=0,
            concat_axis=1,
            tiled=True,
        ),
        lax.all_to_all(
            grad_key_own.astype(jnp.bfloat16).reshape(block_rows, -1),
            "ulysses",
            split_axis=0,
            concat_axis=1,
            tiled=True,
        ),
        lax.all_to_all(
            grad_value_own.astype(jnp.bfloat16).reshape(block_rows, -1),
            "ulysses",
            split_axis=0,
            concat_axis=1,
            tiled=True,
        ),
    )
    _, query_pullback = jax.vjp(
        lambda head_values: rotate(head_values, positions) * HEAD ** (-0.5),
        query_pre.reshape(sequence_local_rows, HEADS, HEAD),
    )
    grad_query_pre = (
        query_pullback(
            grad_query_rows.astype(jnp.float32).reshape(sequence_local_rows, HEADS, HEAD)
        )[0]
        .reshape(sequence_local_rows, HQ)
        .astype(jnp.bfloat16)
    )
    _, key_pullback = jax.vjp(
        lambda head_values: rotate(head_values, positions),
        key_pre.reshape(sequence_local_rows, KV_HEADS, HEAD),
    )
    grad_key_pre = (
        key_pullback(
            grad_key_rows.astype(jnp.float32).reshape(sequence_local_rows, KV_HEADS, HEAD)
        )[0]
        .reshape(sequence_local_rows, KEY_VALUE_WIDTH)
        .astype(jnp.bfloat16)
    )
    lowrank_query, grad_query_in, grad_query_out = low_rank_back(
        normed, narrow_query, grad_query_pre, adapt_heads_in[:, 0], adapt_query_out, columns
    )
    lowrank_key, grad_key_in, grad_key_out = low_rank_back(
        normed,
        narrow_key,
        grad_key_pre,
        adapt_heads_in[:, 1],
        adapter_key_value_second[:, 0],
        columns,
    )
    lowrank_value, grad_value_in, grad_value_out = low_rank_back(
        normed,
        narrow_value,
        grad_value_rows,
        adapt_heads_in[:, 2],
        adapter_key_value_second[:, 1],
        columns,
    )
    grad_normed = (
        contract_last(grad_query_pre, query_again)
        + contract_last(grad_key_pre, key_again)
        + contract_last(grad_value_rows, value_again)
        + lowrank_query
        + lowrank_key
        + lowrank_value
    )
    tokens_grad = grad_middle + norm_back(residual, attn_in_gain, grad_normed)
    gradients = (
        jnp.stack([grad_query_in, grad_key_in, grad_value_in], axis=1),
        grad_query_out,
        jnp.stack([grad_key_out, grad_value_out], axis=1),
        grad_mix_in,
        grad_mix_out,
        jnp.stack([grad_gate_in, grad_up_in], axis=1),
        jnp.stack([grad_gate_out, grad_up_out], axis=1),
        grad_down_in,
        grad_down_out,
    )
    summed = tuple(
        lax.psum(
            (
                gradients[0],
                gradients[1],
                gradients[2],
                gradients[3],
                gradients[4],
                gradients[5],
                gradients[6],
                gradients[7],
                gradients[8],
            ),
            ("dp", "blk", "ulysses"),
        )
    )
    return (layer_out, tokens_grad) + summed


def solution(mesh):
    placed = (
        P(("dp", "blk", "ulysses"), None),
        P(("dp", "blk"), None),
        P(("dp", "blk"), None),
        P(("dp", "blk"), None),
        P(("dp", "blk"), None),
        P(("dp", "blk"), None),
        P(("dp", "blk"), None),
        P(("dp", "blk"), None),
        P(),
        P(),
        P(),
        P(),
        P(),
        P(),
        P(),
        P(),
        P(),
        P(),
        P(),
        P(),
        P(),
        P("dp", None),
        P(("dp", "blk", "ulysses"), None),
    )
    return jax.shard_map(
        shards,
        mesh=mesh,
        in_specs=placed,
        out_specs=(
            P(("dp", "blk", "ulysses"), None),
            P(("dp", "blk", "ulysses"), None),
            P(),
            P(),
            P(),
            P(),
            P(),
            P(),
            P(),
            P(),
            P(),
        ),
        check_vma=False,
    )
```

profile of v0, /device:TPU:0, one launch (start us, length us, event | category | flops | bytes accessed | tf_op | source)
XLA Modules:
  0.0 1640.5 jit_solution(16184478687395081910)
XLA Ops:
  15.6 36.0 %all-gather.16.cloned.1.call-done = bf16[2304,1024]{1,0:T(8,128)(2,1)} async-done(((bf16[288,1024]{1,0:T(8,128)(2,1)}), bf16[2304,1024]{1,0:T(8,128)(2,1)}) %all-gather.16.cloned.1.call-update) | async-done | bytes 4718608 | tf_op jit(solution)/shard_map/all_gather | solution.py:156
  51.6 3.8 fusion.161
  55.8 19.4 %all_to_all.130 = bf16[256,4,256]{2,0,1:T(8,128)(2,1)} all-to-all(bf16[256,4,256]{2,0,1:T(8,128)(2,1)S(1)} %bitcast.461), channel_id=1, replica_groups=mesh['dp'=2,'blk'=4,'ulysses'=4] {'ulysses'}, dimensions={1} | all-to-all | bytes 1048576 | tf_op jit(solution)/shard_map/all_to_all | solution.py:187
  78.8 13.6 all-gather.10.cloned.1.call-done
  92.4 3.8 fusion.157
  102.9 19.6 %all_to_all.131 = bf16[256,4,256]{2,0,1:T(8,128)(2,1)} all-to-all(bf16[256,4,256]{2,0,1:T(8,128)(2,1)S(1)} %pad_maximum_fusion.4), channel_id=1, replica_groups=mesh['dp'=2,'blk'=4,'ulysses'=4] {'ulysses'}, dimensions={1} | all-to-all | bytes 1048576 | tf_op jit(solution)/shard_map/all_to_all | solution.py:186
  130.9 22.3 %all-gather.14.cloned.1.call-done = bf16[2304,2048]{1,0:T(8,128)(2,1)} async-done(((bf16[288,2048]{1,0:T(8,128)(2,1)}), bf16[2304,2048]{1,0:T(8,128)(2,1)}) %all-gather.14.cloned.1.call-update) | async-done | bytes 9437200 | tf_op jit(solution)/shard_map/all_gather | solution.py:154
  153.2 5.2 fusion.159
  160.3 3.0 copy.250
  166.4 4.8 all-to-all-start.1
  173.5 3.7 all-gather.18.cloned.1.call-done
  177.2 3.9 copy.199
  181.2 16.1 all-to-all-done.1
  202.8 25.7 %while.39 = (s32[]{:T(128)}, f32[1,2,1024]{2,1,0:T(2,128)S(1)}, f32[1,2,1024]{2,1,0:T(2,128)S(1)}, f32[1024,1,2,256]{0,3,2,1:T(8,128)}, s32[4,1024]{1,0:T(4,128)...) while((s32[]{:T(128)}, f32[1,2,1024]{2,1,0:T(2,128)S(1)}, ...), condition=%wide.region_8.9_spmd.clone.clone, body=%wide.region_2.8_spmd.clone.clone.sunk | while | flops 2185300992 | bytes 52602160 | solution.py:245
  206.1 12.6 conditional.8
  206.1 3.6 fusion.10
  212.4 4.9 bitcast_add_fusion
  228.5 4.1 copy.201
  233.7 4.7 fusion.151
  239.9 5.1 all-to-all-start.3
  245.0 5.0 fusion.152
  250.0 11.0 all-to-all-done.3
  263.8 6.7 fusion.163
  276.8 186.3 %all-gather.22.cloned.1.call-done = bf16[2304,9216]{1,0:T(8,128)(2,1)} async-done(((bf16[288,9216]{1,0:T(8,128)(2,1)}), bf16[2304,9216]{1,0:T(8,128)(2,1)}) %all-gather.22.cloned.1.call-update) | async-done | bytes 42467344 | tf_op jit(solution)/shard_map/all_gather | solution.py:268
  463.1 24.9 %fusion.164 = f32[256,9216]{1,0:T(8,128)} fusion(bf16[256,2304]{1,0:T(8,128)(2,1)S(1)} %multiply_convert_fusion.2, bf16[2304,9216]{1,0:T(8,128)(2,1)} %all-gather.22.cloned.1.call-done), kind=kOutput, calls=%fused_computation.299 | convolution fusion | flops 10871635968 | bytes 53084160 | tf_op jit(solution)/shard_map/dot_general | solution.py:266
  488.0 9.6 convolution_add_fusion.2
  497.6 166.8 %all-gather.24.cloned.1.call-done = bf16[2304,9216]{1,0:T(8,128)(2,1)} async-done(((bf16[288,9216]{1,0:T(8,128)(2,1)}), bf16[2304,9216]{1,0:T(8,128)(2,1)}) %all-gather.24.cloned.1.call-update) | async-done | bytes 42467344 | tf_op jit(solution)/shard_map/all_gather | solution.py:273
  664.4 24.8 %fusion.165 = f32[256,9216]{1,0:T(8,128)} fusion(bf16[256,2304]{1,0:T(8,128)(2,1)S(1)} %multiply_convert_fusion.2, bf16[2304,9216]{1,0:T(8,128)(2,1)} %all-gather.24.cloned.1.call-done), kind=kOutput, calls=%fused_computation.300 | convolution fusion | flops 10871635968 | bytes 53084160 | tf_op jit(solution)/shard_map/dot_general | solution.py:271
  689.2 11.6 multiply_convert_fusion.1
  705.3 160.4 %all-gather.26.cloned.1.call-done = bf16[9216,2304]{1,0:T(8,128)(2,1)} async-done(((bf16[1152,2304]{1,0:T(8,128)(2,1)}), bf16[9216,2304]{1,0:T(8,128)(2,1)}) %all-gather.26.cloned.1.call-update) | async-done | bytes 42467344 | tf_op jit(solution)/shard_map/all_gather | solution.py:283
  865.7 21.7 %fusion.166 = f32[256,2304]{1,0:T(8,128)} fusion(bf16[256,9216]{1,0:T(8,128)(2,1)} %copy-done.7, bf16[9216,2304]{1,0:T(8,128)(2,1)} %all-gather.26.cloned.1.call-done), kind=kOutput, calls=%fused_computation.301 | convolution fusion | flops 10871635968 | bytes 49545216 | tf_op jit(solution)/shard_map/dot_general | solution.py:281
  887.4 2.8 fusion.91
  892.9 22.2 %fusion.167 = f32[256,9216]{1,0:T(8,128)} fusion(bf16[256,2304]{1,0:T(8,128)(2,1)S(1)} %get-tuple-element.828, bf16[9216,2304]{1,0:T(8,128)(2,1)} %all-gather.26.cloned.1.call-done), kind=kOutput, calls=%fused_computation.302 | convolution fusion | flops 10871635968 | bytes 53084160 | tf_op jit(solution)/shard_map/dot_general | solution.py:82
  915.1 15.6 multiply_convert_fusion
  937.8 20.7 %fusion.168 = f32[256,2304]{1,0:T(8,128)} fusion(bf16[256,9216]{1,0:T(8,128)(2,1)} %copy-done.22, bf16[2304,9216]{1,0:T(8,128)(2,1)} %all-gather.22.cloned.1.call-done), kind=kOutput, calls=%fused_computation.303 | convolution fusion | flops 10871635968 | bytes 49545216 | tf_op jit(solution)/shard_map/dot_general | solution.py:82
  958.5 19.5 %convolution_add_fusion.10 = f32[256,2304]{1,0:T(8,128)S(1)} fusion(f32[256,2304]{1,0:T(8,128)} %fusion.168, bf16[256,9216]{1,0:T(8,128)(2,1)} %get-tuple-element.824, bf16[2304,9216]{1,0:T(8,128)(2,1)} %all-gather.24.cloned.1.call-done), kind=kOutput, calls=%fused_computation.140 | convolution fusion | flops 10872225792 | bytes 51904512 | tf_op jit(solution)/shard_map/dot_general | solution.py:82
  990.7 4.6 all-to-all-start.4
  995.3 26.1 %all-to-all-done.4 = bf16[256,4,512]{2,0,1:T(8,128)(2,1)S(1)} async-done(((bf16[256,4,512]{2,0,1:T(8,128)(2,1)}), bf16[256,4,512]{2,0,1:T(8,128)(2,1)S(1)}, u32[]{:S(2)}, u32[]{:S(2)}) %all-to-all-start.4) | async-done | bytes 1048608 | tf_op jit(solution)/shard_map/all_to_all | solution.py:331
  1023.0 2.9 multiply_reduce_fusion.5
  1026.3 41.5 %while.40 = (s32[]{:T(128)}, f32[1024,1,2,256]{0,3,2,1:T(8,128)S(1)}, bf16[4,1024,1,256]{3,1,2,0:T(8,128)(2,1)}, bf16[4,1024,1,256]{3,1,2,0:T(8,128)(2,1)}, s32[...) while((s32[]{:T(128)}, ...), condition=%wide.region_20.21_spmd.clone.clone, body=%wide.region_16.20_spmd.clone.clone.sunk | while | flops 5408093184 | bytes 66653000 | solution.py:381
  1027.1 3.4 fusion.298
  1031.2 15.1 conditional.9
  1034.0 5.6 fusion.29
  1048.7 3.4 fusion.298
  1055.4 3.4 fusion.298
  1062.0 3.4 fusion.298
  1067.9 3.1 copy.202
  1076.0 5.4 fusion.180
  1084.3 5.4 fusion.179
  1089.7 3.0 fusion.181
  1094.8 3.6 all-to-all-start.5
  1101.2 9.1 pad_maximum_fusion
  1110.3 4.0 all-to-all-done.5
  1114.5 13.0 reduce-scatter.3.cloned.1.call-done
  1127.5 4.6 all-to-all-start.6
  1135.2 27.0 %reduce-scatter.5.cloned.1.call-done = bf16[1024,1,256]{2,0,1:T(8,128)(2,1)} async-done(((bf16[4096,1,256]{2,0,1:T(8,128)(2,1)}), bf16[1024,1,256]{2,0,1:T(8,128)(2,1)}) %reduce-scatter.5.cloned.1.call-update) | async-done | bytes 524304 | tf_op jit(solution)/shard_map/reduce_scatter | solution.py:393
  1163.0 4.7 all-to-all-start.7
  1171.8 10.4 all-to-all-done.7
  1195.8 6.3 fusion.170
  1202.1 3.8 convolution_add_fusion.12
  1206.0 4.4 convolution_add_fusion.11
  1216.6 396.4 %all-reduce.7.cloned.1.call-done = (f32[8,3,16,2304]{3,2,1,0:T(8,128)}, f32[8,16,2048]{2,1,0:T(8,128)}, f32[8,2,16,1024]{3,2,0,1:T(8,128)}, f32[8,16,2048]{2,1,0...) async-done(((f32[8,3,16,2304]{3,2,1,0:T(8,128)}, ...) | async-done | bytes 25559056 | tf_op jit(solution)/shard_map/psum | solution.py:485
  1615.3 4.2 copy.314
  1625.3 3.7 copy.319
  (455 shorter events, 167.0 us)
Async XLA Ops:
  7.2 693.6 %copy-start = (bf16[8,16,9216]{2,1,0:T(8,128)(2,1)S(1)}, bf16[8,16,9216]{2,1,0:T(8,128)(2,1)}, u32[]{:S(2)}) copy-start(bf16[8,16,9216]{2,1,0:T(8,128)(2,1)} %param.50) | copy-start | bytes 7077892
  7.2 44.4 %all-gather.16.cloned.1.call-start = ((), (), s32[]{:S(2)}) async-start(), calls=%async_computation.13 | async-start | bytes 5308416 | tf_op jit(solution)/shard_map/all_gather | solution.py:156
  8.0 84.5 %all-gather.10.cloned.1.call-start = ((), (), s32[]{:S(2)}) async-start(), calls=%async_computation.10 | async-start | bytes 5308416 | tf_op jit(solution)/shard_map/all_gather | solution.py:155
  8.7 144.5 %all-gather.14.cloned.1.call-start = ((), (), s32[]{:S(2)}) async-start(), calls=%async_computation.12 | async-start | bytes 10616832 | tf_op jit(solution)/shard_map/all_gather | solution.py:154
  9.4 167.8 %all-gather.18.cloned.1.call-start = ((), (), s32[]{:S(2)}) async-start(), calls=%async_computation.14 | async-start | bytes 2621440 | tf_op jit(solution)/shard_map/all_gather | solution.py:200
  9.5 979.5 %copy-start.100 = (s32[128]{0:T(128)}, s32[128]{0:T(128)S(1)}, u32[]{:S(2)}) copy-start(s32[128]{0:T(128)S(1)} %and_select_fusion.3) | copy-start | bytes 1540
  9.6 979.4 %copy-start.91 = (s32[256]{0:T(256)}, s32[256]{0:T(256)S(1)}, u32[]{:S(2)}) copy-start(s32[256]{0:T(256)S(1)} %select_reduce_fusion) | copy-start | bytes 3076
  13.9 139.3 %copy-start.5 = (bf16[256,2304]{1,0:T(8,128)(2,1)}, bf16[256,2304]{1,0:T(8,128)(2,1)S(1)}, u32[]{:S(2)}) copy-start(bf16[256,2304]{1,0:T(8,128)(2,1)S(1)} %fusion.97) | copy-start | bytes 3538948
  75.3 126.0 %all-gather.12.cloned.1.call-start = ((), (), s32[]{:S(2)}) async-start(), calls=%async_computation.11 | async-start | bytes 2621440 | tf_op jit(solution)/shard_map/all_gather | solution.py:199
  122.5 141.3 %all-gather.20.cloned.1.call-start = ((), (), s32[]{:S(2)}) async-start(), calls=%async_computation.15 | async-start | bytes 10616832 | tf_op jit(solution)/shard_map/all_gather | solution.py:157
  123.1 340.1 %all-gather.22.cloned.1.call-start = ((), (), s32[]{:S(2)}) async-start(), calls=%async_computation.16 | async-start | bytes 47775744 | tf_op jit(solution)/shard_map/all_gather | solution.py:268
  123.8 540.6 %all-gather.24.cloned.1.call-start = ((), (), s32[]{:S(2)}) async-start(), calls=%async_computation.17 | async-start | bytes 47775744 | tf_op jit(solution)/shard_map/all_gather | solution.py:273
  124.6 741.1 %all-gather.26.cloned.1.call-start = ((), (), s32[]{:S(2)}) async-start(), calls=%async_computation.18 | async-start | bytes 47775744 | tf_op jit(solution)/shard_map/all_gather | solution.py:283
  153.2 5.2 copy-start.58
  153.2 5.2 copy-start.77
  166.4 30.9 %all-to-all-start.1 = ((bf16[256,4,512]{0,2,1:T(8,128)(2,1)}), bf16[256,4,512]{0,2,1:T(8,128)(2,1)S(1)}, u32[]{:S(2)}, u32[]{:S(2)}) async-start(bf16[256,4,512]{0,2,1:T(8,128)(2,1)} %bitcast.54), calls=%async_computation.1 | async-start | bytes 2097152 | tf_op jit(solution)/shard_map/all_to_all | solution.py:179
  228.5 5.2 copy-start.67
  228.5 5.2 copy-start.89
  228.5 5.2 copy-start.99
  239.9 21.1 %all-to-all-start.3 = ((bf16[4,256,512]{2,1,0:T(8,128)(2,1)}), bf16[4,256,512]{2,1,0:T(8,128)(2,1)S(1)}, u32[]{:S(2)}, u32[]{:S(2)}) async-start(bf16[4,256,512]{2,1,0:T(8,128)(2,1)} %all_to_all.107), calls=%async_computation.3 | async-start | bytes 2097152 | tf_op jit(solution)/shard_map/all_to_all | solution.py:250
  261.0 9.5 copy-start.29
  263.8 6.7 copy-start.81
  263.8 6.7 copy-start.47
  273.6 390.8 %copy-start.15 = (bf16[256,2304]{1,0:T(8,128)(2,1)}, bf16[256,2304]{1,0:T(8,128)(2,1)S(1)}, u32[]{:S(2)}) copy-start(bf16[256,2304]{1,0:T(8,128)(2,1)S(1)} %multiply_convert_fusion.2) | copy-start | bytes 3538948
  705.3 182.1 %copy-start.24 = (bf16[256,2304]{1,0:T(8,128)(2,1)S(1)}, bf16[256,2304]{1,0:T(8,128)(2,1)}, u32[]{:S(2)}) copy-start(bf16[256,2304]{1,0:T(8,128)(2,1)} %param.53) | copy-start | bytes 3538948
  892.4 22.8 %copy-start.25 = (bf16[256,2304]{1,0:T(8,128)(2,1)}, bf16[256,2304]{1,0:T(8,128)(2,1)S(1)}, u32[]{:S(2)}) copy-start(bf16[256,2304]{1,0:T(8,128)(2,1)S(1)} %get-tuple-element.828) | copy-start | bytes 3538948
  892.9 22.2 %copy-start.96 = (bf16[256,128]{0,1:T(8,128)(2,1)}, bf16[256,128]{0,1:T(8,128)(2,1)S(1)}, u32[]{:S(2)}) copy-start(bf16[256,128]{0,1:T(8,128)(2,1)S(1)} %fusion.104) | copy-start | bytes 196612
  915.1 15.6 copy-start.21
  930.7 4.8 copy-start.23
  958.5 19.5 %copy-start.39 = (bf16[8,1,16,2304]{3,2,1,0:T(8,128)(2,1)S(1)}, bf16[8,1,16,2304]{3,2,1,0:T(8,128)(2,1)}, u32[]{:S(2)}) copy-start(bf16[8,1,16,2304]{3,2,1,0:T(8,128)(2,1)} %get-tuple-element.841) | copy-start | bytes 1769476
  958.5 19.5 %copy-start.73 = (bf16[256,128]{0,1:T(8,128)(2,1)S(1)}, bf16[256,128]{0,1:T(8,128)(2,1)}, u32[]{:S(2)}) copy-start(bf16[256,128]{0,1:T(8,128)(2,1)} %fusion.107) | copy-start | bytes 196612
  979.8 6.5 slice-start.4
  981.5 4.9 slice-start.5
  981.5 4.9 slice-start.6
  989.6 5.7 copy-start.68
  989.6 5.7 copy-start.90
  990.7 30.8 %all-to-all-start.4 = ((bf16[256,4,512]{2,0,1:T(8,128)(2,1)}), bf16[256,4,512]{2,0,1:T(8,128)(2,1)S(1)}, u32[]{:S(2)}, u32[]{:S(2)}) async-start(bf16[256,4,512]{2,0,1:T(8,128)(2,1)} %bitcast.384), calls=%async_computation.4 | async-start | bytes 2097152 | tf_op jit(solution)/shard_map/all_to_all | solution.py:331
  995.2 132.2 %reduce-scatter.3.cloned.1.call-start = ((), (), s32[]{:S(2)}) async-start(), calls=%async_computation.19 | async-start | bytes 2621440 | tf_op jit(solution)/shard_map/reduce_scatter | solution.py:387
  1067.8 5.9 copy-start.16
  1067.8 5.9 copy-start.76
  1067.8 94.3 %reduce-scatter.5.cloned.1.call-start = ((), (), s32[]{:S(2)}) async-start(), calls=%async_computation.20 | async-start | bytes 2621440 | tf_op jit(solution)/shard_map/reduce_scatter | solution.py:393
  1076.0 5.4 copy-start.82
  1076.0 13.7 slice-start
  1081.4 8.2 slice-start.1
  1084.3 5.4 copy-start.97
  1093.7 4.8 copy-start.45
  1093.7 4.8 copy-start.98
  1094.8 5.0 copy-start.26
  1094.8 5.0 copy-start.72
  1094.8 19.5 %all-to-all-start.5 = ((bf16[4,256,512]{1,2,0:T(8,128)(2,1)}), bf16[4,256,512]{1,2,0:T(8,128)(2,1)S(1)}, u32[]{:S(2)}, u32[]{:S(2)}) async-start(bf16[4,256,512]{1,2,0:T(8,128)(2,1)} %copy.216), calls=%async_computation.5 | async-start | bytes 2097152 | tf_op jit(solution)/shard_map/all_to_all | solution.py:401
  1110.3 21.8 %copy-start.62 = (f32[256,128]{0,1:T(8,128)S(1)}, f32[256,128]{0,1:T(8,128)}, u32[]{:S(2)}) copy-start(f32[256,128]{0,1:T(8,128)} %copy.194) | copy-start | bytes 393220
  1110.3 21.8 %copy-start.64 = (f32[256,128]{0,1:T(8,128)S(1)}, f32[256,128]{0,1:T(8,128)}, u32[]{:S(2)}) copy-start(f32[256,128]{0,1:T(8,128)} %copy.192) | copy-start | bytes 393220
  1127.5 34.7 %all-to-all-start.6 = ((bf16[4,256,256]{2,1,0:T(8,128)(2,1)}), bf16[4,256,256]{2,1,0:T(8,128)(2,1)S(1)}, u32[]{:S(2)}, u32[]{:S(2)}) async-start(bf16[4,256,256]{2,1,0:T(8,128)(2,1)} %bitcast.469), calls=%async_computation.7 | async-start | bytes 1048576 | tf_op jit(solution)/shard_map/all_to_all | solution.py:408
  1133.4 34.6 %copy-start.95 = (bf16[128,256]{1,0:T(8,128)(2,1)S(1)}, bf16[128,256]{1,0:T(8,128)(2,1)}, u32[]{:S(2)}) copy-start(bf16[128,256]{1,0:T(8,128)(2,1)} %get-tuple-element.850) | copy-start | bytes 196612
  1133.8 28.4 %copy-start.83 = (bf16[256,128]{0,1:T(8,128)(2,1)}, bf16[256,128]{0,1:T(8,128)(2,1)S(1)}, u32[]{:S(2)}) copy-start(bf16[256,128]{0,1:T(8,128)(2,1)S(1)} %fusion.105) | copy-start | bytes 196612
  1163.0 6.6 copy-start.53
  1163.0 6.6 copy-start.54
  1163.0 19.2 %all-to-all-start.7 = ((bf16[4,256,256]{2,1,0:T(8,128)(2,1)}), bf16[4,256,256]{2,1,0:T(8,128)(2,1)S(1)}, u32[]{:S(2)}, u32[]{:S(2)}) async-start(bf16[4,256,256]{2,1,0:T(8,128)(2,1)} %bitcast.468), calls=%async_computation.9 | async-start | bytes 1048576 | tf_op jit(solution)/shard_map/all_to_all | solution.py:415
  1167.7 445.3 %all-reduce.7.cloned.1.call-start = ((), (), s32[]{:S(2)}) async-start(), calls=%async_computation.21 | async-start | bytes 51118080 | tf_op jit(solution)/shard_map/psum | solution.py:485
  1615.3 5.2 copy-start.70
  1615.3 6.1 copy-start.66
  1615.3 7.1 copy-start.49
  1619.5 5.8 copy-start.28
  1622.4 6.6 slice-start.2
  (83 other events, 188.7 us)
Sparse Core Ops, SparseCore 0:
  9.9 41.6 all-gather.15
  53.5 38.9 all-gather.9
  94.3 58.8 all-gather.13
  154.6 22.5 all-gather.17
  178.6 22.5 all-gather.11
  203.0 58.8 all-gather.19
  263.8 199.2 all-gather.21
  465.0 199.3 all-gather.23
  666.3 199.3 all-gather.25
  1067.9 59.4 reduce-scatter.2
  1130.7 31.3 reduce-scatter.4
  1195.9 417.0 all-reduce.6
where the time goes:
time: 1650 us; the launch traced here: 1640 us
  waiting for transfers between devices  1100 us (67%)
  matrix products  289 us (18%)
  local copies, waits for them, and re-layouts  98.8 us (6%)
  other arithmetic  65.9 us (4%)
  blocking collectives  39 us (2%)
  starting transfers between devices  28.1 us (2%)
    psum x1, waiting for transfers between devices, shards(): lax.psum((gradients[0], gradients[1], gradients[2], gradients[3], gradien...  396 us
    all_gather x1, waiting for transfers between devices, shards(): lax.all_gather(gate_weight, ('dp', 'blk'), axis=0, tiled=True)  186 us
    all_gather x1, waiting for transfers between devices, shards(): lax.all_gather(up_weight, ('dp', 'blk'), axis=0, tiled=True)  167 us
    all_gather x1, waiting for transfers between devices, shards(): lax.all_gather(down_weight, ('dp', 'blk'), axis=0, tiled=True)  160 us
    dot_general x21, matrix products, contract_last(): lax.dot_general(former, latter, (((1,), (1,)), ((), ())), preferred_eleme...  100 us
    unnamed x261, local copies, waits for them, and re-layouts  45.3 us
    all_gather x1, waiting for transfers between devices, shards(): lax.all_gather(value_projection, ('dp', 'blk'), axis=0, tiled=True)  36 us
  transfers between devices with their start and end apart: 18, of which 16 were waited for; matrix products, arithmetic and copies ran while one was open for 14% of the time, Pallas kernels for 0%

commit v1 on v0

v1 whole, which is shorter than its diff:
```python
import jax
import jax.numpy as jnp
from jax import lax
from jax.experimental import pallas as pl
from jax.experimental.pallas import tpu as pltpu
from jax.sharding import PartitionSpec as P

HEADS = 8
KV_HEADS = 4
HEAD = 256
RANK = 16
ADAPTERS = 8
LANES = RANK * ADAPTERS
PROMPT = 2048
CONT = 256
CONTS = 8

epsilon = 1e-06
soft_cap = 50.0
rope_base = 10000.0
PLANE = ("dp", "blk")
EVERY = ("dp", "blk", "ulysses")
f32 = jnp.float32
bf16 = jnp.bfloat16


def dot_nn(a, b):
    return jnp.dot(a, b, preferred_element_type=f32)


def dot_nt(a, b):
    return lax.dot_general(a, b, (((1,), (1,)), ((), ())), preferred_element_type=f32)


def dot_tn(a, b):
    return lax.dot_general(a, b, (((0,), (0,)), ((), ())), preferred_element_type=f32)


def rms_scale(values, gain_row):
    return (
        values * lax.rsqrt(jnp.mean(values * values, axis=-1, keepdims=True) + epsilon) * gain_row
    )


def norm_back(values, gain_row, grad_out):
    scale = lax.rsqrt(jnp.mean(values * values, axis=-1, keepdims=True) + epsilon)
    weighted = grad_out * gain_row
    return scale * weighted - values * (
        scale * scale * scale * jnp.mean(values * weighted, axis=-1, keepdims=True)
    )


def shape(dims, dtype):
    return jax.ShapeDtypeStruct(dims, dtype)


VM = pl.BlockSpec(memory_space=pltpu.VMEM)


MESH = pl.DeviceIdType.MESH


def neighbours():
    dp, b, z = lax.axis_index("dp"), lax.axis_index("blk"), lax.axis_index("ulysses")
    across_x = (dp + 1 - 2 * (dp % 2), b, z)
    across_y = (dp, (b + 2) % 4, z)
    sibling = (dp, b + 1 - 2 * (b % 2), z)
    return across_x, across_y, sibling


def greet(peers):
    barrier = pltpu.get_barrier_semaphore()
    for peer in peers:
        pl.semaphore_signal(barrier, inc=1, device_id=peer, device_id_type=MESH)
    pl.semaphore_wait(barrier, len(peers))


def sender(send, recv):
    def copy(index, src, dst, peer):
        return pltpu.make_async_remote_copy(
            src, dst, send.at[index], recv.at[index], device_id=peer, device_id_type=MESH
        )

    return copy


def add_into(target, source, count, step=32):
    @pl.loop(0, count // step)
    def _(i):
        at = pl.ds(pl.multiple_of(i * step, step), step)
        target[at, :] = (target[at, :].astype(f32) + source[at, :].astype(f32)).astype(target.dtype)


class PlaneGather:
    COUNT = 10

    def __init__(self, copy, own, land, rows):
        px, py, pc = neighbours()
        h = rows // 2
        h0, h1 = pl.ds(0, h), pl.ds(h, h)
        near, far = pl.ds(0, rows), pl.ds(rows, rows)
        self.c = [
            copy(0, own, land.at[0, far], pc),
            copy(1, own.at[h0], land.at[1, h0], px),
            copy(2, own.at[h1], land.at[3, h1], py),
            copy(3, own.at[h1], land.at[1, h1], px),
            copy(4, own.at[h0], land.at[3, h0], py),
            copy(5, land.at[1, h0], land.at[2, h0], py),
            copy(6, land.at[3, h1], land.at[2, h1], px),
            copy(7, land.at[1, near], land.at[1, far], pc),
            copy(8, land.at[3, near], land.at[3, far], pc),
            copy(9, land.at[2, near], land.at[2, far], pc),
        ]

    def begin(self):
        for i in range(5):
            self.c[i].start()

    def before(self, i):
        c = self.c

        @pl.when(i == 0)
        def _():
            c[0].wait_recv()

        @pl.when(i == 1)
        def _():
            c[1].wait_recv()
            c[5].start()
            c[2].wait_recv()
            c[6].start()
            c[3].wait_recv()
            c[7].start()
            c[4].wait_recv()
            c[8].start()
            c[7].wait_recv()

        @pl.when(i == 2)
        def _():
            c[5].wait_recv()
            c[6].wait_recv()
            c[9].start()
            c[9].wait_recv()

        @pl.when(i == 3)
        def _():
            c[8].wait_recv()

    def finish(self):
        for c in self.c:
            c.wait_send()


class PlaneReduce:
    COUNT = 10

    def __init__(self, copy, part, odd, from_core, from_x, from_y, diag, rows, first):
        px, py, pc = neighbours()
        h = rows // 2
        self.h = h
        self.rows = rows
        h0, h1 = pl.ds(0, h), pl.ds(h, h)
        self.part, self.from_core = part, from_core
        self.from_x, self.from_y, self.diag = from_x, from_y, diag
        self.core = [
            copy(first + i, odd.at[i % 2], from_core.at[i], pc) for i in range(4)
        ]
        self.d = [
            copy(first + 4, part.at[2, h0], diag.at[h0], px),
            copy(first + 5, part.at[2, h1], diag.at[h1], py),
        ]
        self.e = [
            copy(first + 6, part.at[1, h0], from_x.at[h0], px),
            copy(first + 7, part.at[3, h1], from_y.at[h1], py),
            copy(first + 8, part.at[1, h1], from_x.at[h1], px),
            copy(first + 9, part.at[3, h0], from_y.at[h0], py),
        ]

    def merge(self, i):
        self.core[i].wait_recv()
        add_into(self.part.at[i], self.from_core.at[i], self.rows)

    def before(self, i):
        for k in (2, 3):

            @pl.when(i == k)
            def _(k=k):
                self.core[k - 2].wait_send()

    def after(self, i):
        for k in range(4):

            @pl.when(i == k)
            def _(k=k):
                self.core[k].start()
                if k == 2:
                    self.merge(1)
                    self.e[0].start()
                    self.merge(2)
                    self.d[0].start()
                    self.d[1].start()

    def finish(self, out):
        h, h0, h1 = self.h, pl.ds(0, self.h), pl.ds(self.h, self.h)
        self.merge(3)
        self.e[1].start()
        self.d[0].wait_recv()
        add_into(self.part.at[3, h0], self.diag.at[h0], h)
        self.e[3].start()
        self.d[1].wait_recv()
        add_into(self.part.at[1, h1], self.diag.at[h1], h)
        self.e[2].start()
        self.merge(0)
        for e in self.e:
            e.wait_recv()

        @pl.loop(0, self.rows // 32)
        def _(i):
            at = pl.ds(pl.multiple_of(i * 32, 32), 32)
            out[at, :] = (
                self.part[0, at, :].astype(f32)
                + self.from_x[at, :].astype(f32)
                + self.from_y[at, :].astype(f32)
            ).astype(out.dtype)

        for c in self.core[2:] + self.d + self.e:
            c.wait_send()


GELU_SLOPE = 0.7978845608028654
GELU_CUBE = 0.044715


def span(i, size):
    return pl.ds(pl.multiple_of(i * size, size), size)


def feed_forward_kernel(
    own, feed_in, gate_out, up_out, down_in, down_out, columns, gate_hbm, up_hbm, down_hbm,
    branch, narrow, feed_all, gate_up,
    gate, up, down, land, hidden, saved, part, odd, from_core, from_x, from_y, diag,
    send, recv, load, store,
):
    rows = own.shape[0]
    share = gate.shape[1]
    width = own.shape[1]
    tile = 384
    loads = [
        pltpu.make_async_copy(s, d, load.at[i])
        for i, (s, d) in enumerate(((gate_hbm, gate), (up_hbm, up), (down_hbm, down)))
    ]
    for c in loads:
        c.start()
    greet(neighbours())
    copy = sender(send, recv)
    gather = PlaneGather(copy, own, land, rows)
    reduce = PlaneReduce(
        copy, part, odd, from_core, from_x, from_y, diag, rows, PlaneGather.COUNT
    )
    gather.begin()
    land[0, :rows, :] = own[...]
    for c in loads:
        c.wait()

    def keep(i):
        slot = i % 2
        return (
            pltpu.make_async_copy(saved.at[slot], gate_up.at[i], store.at[slot]),
            pltpu.make_async_copy(land.at[i], feed_all.at[i], store.at[2 + slot]),
        )

    @pl.loop(0, 4)
    def _(i):
        gather.before(i)
        slot = i % 2

        @pl.when(i >= 2)
        def _():
            for c in keep(i - 2):
                c.wait()

        masks = columns[i].astype(f32)
        low = dot_nt(land[i], feed_in[...])
        low_gate = (low[:, :LANES] * masks).astype(bf16)
        low_up = (low[:, LANES:] * masks).astype(bf16)
        narrow[i, 0] = low_gate
        narrow[i, 1] = low_up

        @pl.loop(0, share // tile)
        def _(n):
            at = span(n, tile)
            g = dot_nn(land[i], gate[:, at]) + dot_nn(narrow[i, 0], gate_out[:, at])
            u = dot_nn(land[i], up[:, at]) + dot_nn(narrow[i, 1], up_out[:, at])
            saved[slot, 0, :, at] = g.astype(bf16)
            saved[slot, 1, :, at] = u.astype(bf16)
            th = jnp.tanh(GELU_SLOPE * (g + GELU_CUBE * g * g * g))
            hidden[:, at] = (0.5 * g * (1.0 + th) * u).astype(bf16)

        for c in keep(i):
            c.start()
        narrow[i, 2] = (dot_nt(hidden[...], down_in[...]) * masks).astype(bf16)
        reduce.before(i)

        @pl.loop(0, width // tile)
        def _(n):
            at = span(n, tile)
            got = dot_nn(hidden[...], down[:, at]) + dot_nn(narrow[i, 2], down_out[:, at])
            got = got.astype(bf16)
            part[i, :, at] = got[:rows]
            odd[i % 2, :, at] = got[rows:]

        reduce.after(i)

    reduce.finish(branch)
    gather.finish()
    for i in (2, 3):
        for c in keep(i):
            c.wait()


def feed_backward_kernel(
    own, feed_in, gate_out, up_out, down_in, down_out, columns, narrow,
    gate_hbm, up_hbm, down_hbm, gate_up,
    grad_feed, both, t_feed_out, t_down_in, t_down_out,
    gate, up, down, land, saved, gg, gu, part, odd, from_core, from_x, from_y, diag,
    send, recv, load, fetch,
):
    rows = own.shape[0]
    share = gate.shape[1]
    width = own.shape[1]
    tile = 384
    loads = [
        pltpu.make_async_copy(s, d, load.at[i])
        for i, (s, d) in enumerate(((down_hbm, down), (gate_hbm, gate), (up_hbm, up)))
    ]

    def bring(i):
        return pltpu.make_async_copy(gate_up.at[i], saved, fetch.at[0])

    for c in loads:
        c.start()
    bring(0).start()
    greet(neighbours())
    copy = sender(send, recv)
    gather = PlaneGather(copy, own, land, rows)
    reduce = PlaneReduce(
        copy, part, odd, from_core, from_x, from_y, diag, rows, PlaneGather.COUNT
    )
    gather.begin()
    land[0, :rows, :] = own[...]
    t_feed_out[...] = jnp.zeros_like(t_feed_out)
    t_down_in[...] = jnp.zeros_like(t_down_in)
    t_down_out[...] = jnp.zeros_like(t_down_out)
    for c in loads:
        c.wait()

    @pl.loop(0, 4)
    def _(i):
        gather.before(i)
        bring(i).wait()
        masks = columns[i].astype(f32)
        back = (dot_nt(land[i], down_out[...]) * masks).astype(bf16)

        @pl.loop(0, share // tile)
        def _(n):
            at = span(n, tile)
            gh = dot_nt(land[i], down[at, :]) + dot_nn(back, down_in[:, at])
            g = saved[0, :, at].astype(f32)
            u = saved[1, :, at].astype(f32)
            th = jnp.tanh(GELU_SLOPE * (g + GELU_CUBE * g * g * g))
            gelu = 0.5 * g * (1.0 + th)
            slope = 0.5 * (1.0 + th) + 0.5 * g * (1.0 - th * th) * GELU_SLOPE * (
                1.0 + 3.0 * GELU_CUBE * g * g
            )
            t_down_in[:, at] += dot_tn(back, (gelu * u).astype(bf16))
            gg[:, at] = (gh * u * slope).astype(bf16)
            gu[:, at] = (gh * gelu).astype(bf16)

        @pl.when(i < 3)
        def _():
            bring(i + 1).start()

        back_gate = (dot_nt(gg[...], gate_out[...]) * masks).astype(bf16)
        back_up = (dot_nt(gu[...], up_out[...]) * masks).astype(bf16)
        both[i] = jnp.concatenate([back_gate, back_up], axis=1)
        reduce.before(i)

        @pl.loop(0, width // tile)
        def _(n):
            at = span(n, tile)
            got = (
                dot_nt(gg[...], gate[at, :])
                + dot_nt(gu[...], up[at, :])
                + dot_nn(both[i], feed_in[:, at])
            ).astype(bf16)
            part[i, :, at] = got[:rows]
            odd[i % 2, :, at] = got[rows:]

        reduce.after(i)
        t_feed_out[0] += dot_tn(narrow[i, 0], gg[...])
        t_feed_out[1] += dot_tn(narrow[i, 1], gu[...])
        t_down_out[...] += dot_tn(narrow[i, 2], land[i])

    reduce.finish(grad_feed)
    gather.finish()


def feed_scratch(rows, width):
    return [
        pltpu.VMEM((4, rows, width), bf16),
        pltpu.VMEM((2, rows, width), bf16),
        pltpu.VMEM((4, rows, width), bf16),
        pltpu.VMEM((rows, width), bf16),
        pltpu.VMEM((rows, width), bf16),
        pltpu.VMEM((rows, width), bf16),
        pltpu.SemaphoreType.DMA((PlaneGather.COUNT + PlaneReduce.COUNT,)),
        pltpu.SemaphoreType.DMA((PlaneGather.COUNT + PlaneReduce.COUNT,)),
    ]


ANY = pl.BlockSpec(memory_space=pl.ANY)


def feed_forward(own, feed_in, gate_out, up_out, down_in, down_out, columns, gate, up, down):
    rows, width = own.shape
    share = gate.shape[1]
    return pl.pallas_call(
        feed_forward_kernel,
        out_shape=(
            shape((rows, width), f32),
            shape((4, 3, 2 * rows, LANES), bf16),
            shape((4, 2 * rows, width), bf16),
            shape((4, 2, 2 * rows, share), bf16),
        ),
        in_specs=[VM] * 7 + [ANY] * 3,
        out_specs=(VM, VM, ANY, ANY),
        scratch_shapes=[
            pltpu.VMEM(gate.shape, bf16),
            pltpu.VMEM(up.shape, bf16),
            pltpu.VMEM(down.shape, bf16),
            pltpu.VMEM((4, 2 * rows, width), bf16),
            pltpu.VMEM((2 * rows, share), bf16),
            pltpu.VMEM((2, 2, 2 * rows, share), bf16),
        ]
        + feed_scratch(rows, width)
        + [pltpu.SemaphoreType.DMA((3,)), pltpu.SemaphoreType.DMA((4,))],
        compiler_params=pltpu.CompilerParams(
            collective_id=1, has_side_effects=True, vmem_limit_bytes=62 << 20
        ),
        name="feed_forward",
    )(own, feed_in, gate_out, up_out, down_in, down_out, columns, gate, up, down)


def feed_backward(
    own, feed_in, gate_out, up_out, down_in, down_out, columns, narrow, gate, up, down, gate_up
):
    rows, width = own.shape
    share = gate.shape[1]
    return pl.pallas_call(
        feed_backward_kernel,
        out_shape=(
            shape((rows, width), bf16),
            shape((4, 2 * rows, 2 * LANES), bf16),
            shape((2, LANES, share), f32),
            shape((LANES, share), f32),
            shape((LANES, width), f32),
        ),
        in_specs=[VM] * 8 + [ANY] * 4,
        out_specs=(VM,) * 5,
        scratch_shapes=[
            pltpu.VMEM(gate.shape, bf16),
            pltpu.VMEM(up.shape, bf16),
            pltpu.VMEM(down.shape, bf16),
            pltpu.VMEM((4, 2 * rows, width), bf16),
            pltpu.VMEM((2, 2 * rows, share), bf16),
            pltpu.VMEM((2 * rows, share), bf16),
            pltpu.VMEM((2 * rows, share), bf16),
        ]
        + feed_scratch(rows, width)
        + [pltpu.SemaphoreType.DMA((3,)), pltpu.SemaphoreType.DMA((1,))],
        compiler_params=pltpu.CompilerParams(
            collective_id=2, has_side_effects=True, vmem_limit_bytes=62 << 20
        ),
        name="feed_backward",
    )(
        own, feed_in, gate_out, up_out, down_in, down_out, columns, narrow, gate, up, down, gate_up
    )


def rms_rows(source, gain, target, rows, add=None, keep=None):
    @pl.loop(0, rows // 32)
    def _(i):
        at = span(i, 32)
        v = source[at, :].astype(f32)
        out = v * lax.rsqrt(jnp.mean(v * v, axis=-1, keepdims=True) + epsilon) * gain[...]
        if add is not None:
            out = out + add[at, :].astype(f32)
        target[at, :] = out.astype(target.dtype)


def attention_forward_kernel(
    tokens, attn_in_gain, attn_out_gain, feed_in_gain, heads_in, query_out, key_out, value_out,
    mix_in, mix_out, columns, own_columns, cosine, sine,
    query_hbm, key_hbm, value_hbm, out_hbm, gate_hbm, up_hbm,
    queries, values_prompt, values_cont, attended, sums, narrow, mixed_out, narrow_mix, attn_out,
    middle, normed_feed, normed_out, wall_out, out_out, gate_share, up_share,
    normed_all, wall, wo, kvp, kvc, acc, total, mixed, send, recv, local,
):
    rows, width = tokens.shape
    dp, b, z = lax.axis_index("dp"), lax.axis_index("blk"), lax.axis_index("ulysses")
    planes = lax.axis_size("ulysses")
    x, y, c = dp % 2, b // 2, b % 2
    base = dp - x
    rank = x * 4 + b
    b_c, b_y = b + 1 - 2 * c, (b + 2) % 4
    b_yc = (b_c + 2) % 4
    pc, py, pyc = (dp, b_c, z), (dp, b_y, z), (dp, b_yc, z)
    other = base + 1 - x
    px, pxc, pxy, pxyc = (other, b, z), (other, b_c, z), (other, b_y, z), (other, b_yc, z)
    pz = (dp, b, z + 1 - 2 * (z % 2))
    left, right = (dp, b, z - 1), (dp, b, z + 1)
    depth = query_hbm.shape[0]
    share = gate_share.shape[1]
    part = out_hbm.shape[0]
    copy = sender(send, recv)

    def block(i):
        return span(i, rows)

    def weight_rows(i):
        return pl.ds(pl.multiple_of(i * depth, 16), depth)

    def out_rows(i):
        return span(i, part)

    heads = ((query_hbm, 2 * HEAD, 0), (key_hbm, HEAD, 2 * HEAD), (value_hbm, HEAD, 3 * HEAD))

    def columns_of(ref, target, size):
        return ref.at[:, pl.ds(pl.multiple_of(target * size, 128), size)]

    own_loads = [
        pltpu.make_async_copy(
            columns_of(ref, b, size), wall.at[weight_rows(rank), pl.ds(to, size)], local.at[i]
        )
        for i, (ref, size, to) in enumerate(heads)
    ]
    own_loads.append(pltpu.make_async_copy(out_hbm, wo.at[out_rows(rank)], local.at[3]))
    own_rows = [
        pltpu.make_async_copy(
            columns_of(ref, rank, share), out.at[weight_rows(rank)], local.at[4 + i]
        )
        for i, (ref, out) in enumerate(((gate_hbm, gate_share), (up_hbm, up_share)))
    ]
    for cp in own_loads:
        cp.start()

    barrier = pltpu.get_barrier_semaphore()
    for peer in (pc, py, pyc, px, pxc, pxy, pxyc) + tuple(
        (dp, b, (z + d) % planes) for d in range(1, planes)
    ):
        pl.semaphore_signal(barrier, inc=1, device_id=peer, device_id_type=MESH)

    rms_rows(tokens, attn_in_gain, normed_all.at[block(b)], rows)
    pl.semaphore_wait(barrier, 6 + planes)

    stage = []
    for j, (peer, pb) in enumerate(((py, b_y), (pyc, b_yc), (pc, b_c))):
        for i, (ref, size, to) in enumerate(heads):
            stage.append(
                copy(
                    3 + 3 * j + i,
                    columns_of(ref, pb, size),
                    wall.at[weight_rows(rank), pl.ds(to, size)],
                    peer,
                )
            )
    token_copies = [
        copy(0, normed_all.at[block(b)], normed_all.at[block(b)], py),
        copy(1, normed_all.at[block(b)], normed_all.at[block(b)], pc),
        copy(2, normed_all.at[block(b_y)], normed_all.at[block(b_y)], pc),
    ]
    across = [
        copy(12 + i, wall.at[weight_rows(x * 4 + o)], wall.at[weight_rows(x * 4 + o)], px)
        for i, o in enumerate((b, b_c, b_y, b_yc))
    ]
    for cp in stage[:3]:
        cp.start()
    token_copies[0].start()
    for cp in stage[3:]:
        cp.start()
    token_copies[1].start()
    for cp in own_loads[:3]:
        cp.wait()
    across[0].start()
    for cp in stage[6:]:
        cp.wait_recv()
    across[1].start()
    for cp in stage[:3]:
        cp.wait_recv()
    across[2].start()
    for cp in stage[3:6]:
        cp.wait_recv()
    across[3].start()
    token_copies[0].wait_recv()
    token_copies[2].start()

    half = part // 2
    rx, ry, rxy = (1 - x) * 4 + b, x * 4 + b_y, (1 - x) * 4 + b_y

    def wo_part(r, h):
        return wo.at[pl.ds(pl.multiple_of(r * part + h * half, 16), half)]

    wo_first = [
        (16, wo_part(rank, 0), px),
        (17, wo_part(rank, 1), py),
        (18, wo_part(rank, 1), px),
        (19, wo_part(rank, 0), py),
        (20, wo.at[out_rows(rank)], pc),
    ]
    wo_next = [
        (21, wo_part(rx, 0), py),
        (22, wo_part(ry, 1), px),
        (23, wo.at[out_rows(rx)], pc),
        (24, wo.at[out_rows(ry)], pc),
        (25, wo.at[out_rows(rxy)], pc),
    ]
    wo_first = [copy(i, ref, ref, peer) for i, ref, peer in wo_first]
    wo_next = [copy(i, ref, ref, peer) for i, ref, peer in wo_next]
    own_loads[3].wait()
    for cp in across:
        cp.wait_recv()
    for cp in wo_first:
        cp.start()
    token_copies[1].wait_recv()
    token_copies[2].wait_recv()

    outs = [
        pltpu.make_async_copy(normed_all, normed_out, local.at[6]),
        pltpu.make_async_copy(wall, wall_out, local.at[7]),
        pltpu.make_async_copy(wo, out_out, local.at[8]),
        pltpu.make_async_copy(kvp, values_prompt, local.at[9]),
        pltpu.make_async_copy(kvc, values_cont, local.at[10]),
        pltpu.make_async_copy(mixed, mixed_out, local.at[11]),
    ]
    outs[0].start()
    outs[1].start()

    half_head = HEAD // 2

    @pl.loop(0, 4)
    def _(t):
        at = block(t)
        masks = columns[at, :].astype(f32)
        cos, sin = cosine[at, :], sine[at, :]
        a = normed_all[at, :]
        for i in range(3):
            lanes = slice(i * LANES, (i + 1) * LANES)
            narrow[at, lanes] = (dot_nt(a, heads_in[lanes, :]) * masks).astype(bf16)

        def turned(pre, scale):
            first, second = pre[:, :half_head], pre[:, half_head:]
            one, two = first * cos - second * sin, second * cos + first * sin
            if scale != 1.0:
                one, two = one * scale, two * scale
            return jnp.concatenate([one, two], axis=1).astype(bf16)

        for h in range(2):
            lanes = slice(h * HEAD, (h + 1) * HEAD)
            pre = dot_nn(a, wall[:, lanes]) + dot_nn(narrow[at, :LANES], query_out[:, lanes])
            queries[t, h * rows : (h + 1) * rows, :] = turned(pre, HEAD ** (-0.5))
        pre = dot_nn(a, wall[:, 2 * HEAD : 3 * HEAD]) + dot_nn(
            narrow[at, LANES : 2 * LANES], key_out[...]
        )
        key = turned(pre, 1.0)
        value = (
            dot_nn(a, wall[:, 3 * HEAD :]) + dot_nn(narrow[at, 2 * LANES :], value_out[...])
        ).astype(bf16)

        @pl.when(t < 2)
        def _():
            kvp[z, 0, t] = key
            kvp[z, 1, t] = value

        @pl.when(t >= 2)
        def _():
            kvc[0, t - 2] = key
            kvc[1, t - 2] = value

    def hop(direction, d):
        index = 42 + d if direction > 0 else 45 + d
        zz = z - d * direction
        return copy(index, kvp.at[zz], kvp.at[zz], right if direction > 0 else left)

    def pass_on(direction, d):
        reach = z < planes - 1 if direction > 0 else z > 0

        @pl.when(reach)
        def _():
            hop(direction, d).start()

    pass_on(1, 0)
    pass_on(-1, 0)

    acc[...] = jnp.zeros_like(acc)
    total[...] = jnp.zeros_like(total)
    row = lax.broadcasted_iota(jnp.int32, (2 * rows, rows), 0) % rows
    causal = lax.broadcasted_iota(jnp.int32, (2 * rows, rows), 1) <= row

    def step(t, k, v, masked):
        e = jnp.exp(soft_cap * jnp.tanh(dot_nt(queries[t], k) * (1.0 / soft_cap)))
        if masked:
            e = jnp.where(causal, e, 0.0)
        some = e[:, :128]
        for n in range(128, rows, 128):
            some = some + e[:, n : n + 128]
        total[t] += some
        acc[t] += dot_nn(e.astype(bf16), v)

    step(0, kvp[z, 0, 0], kvp[z, 1, 0], True)
    step(1, kvp[z, 0, 0], kvp[z, 1, 0], False)
    step(1, kvp[z, 0, 1], kvp[z, 1, 1], True)

    @pl.loop(2, 4)
    def _(t):
        step(t, kvc[0, t - 2], kvc[1, t - 2], True)
        step(t, kvp[z, 0, 0], kvp[z, 1, 0], False)
        step(t, kvp[z, 0, 1], kvp[z, 1, 1], False)

    wo_first[0].wait_recv()
    wo_next[0].start()
    wo_first[1].wait_recv()
    wo_next[1].start()

    swaps = []
    at = 26
    for peer, pr in (
        (px, rx), (py, ry), (pxc, (1 - x) * 4 + b_c), (pyc, x * 4 + b_yc), (pc, x * 4 + b_c),
    ):
        for ref, out in ((gate_hbm, gate_share), (up_hbm, up_share)):
            swaps.append(
                copy(at, columns_of(ref, pr, share), out.at[weight_rows(rank)], peer)
            )
            at += 1
    far = []
    for i, (ref, out) in enumerate(((gate_hbm, gate_share), (up_hbm, up_share))):
        for j, (peer, pr) in enumerate(((pxy, rxy), (pxyc, (1 - x) * 4 + b_yc))):
            far.append(
                pltpu.make_async_remote_copy(
                    columns_of(ref, pr, share),
                    out.at[weight_rows(rank)],
                    send.at[36 + 2 * j + i],
                    recv.at[36 + i],
                    device_id=peer,
                    device_id_type=MESH,
                )
            )
    got_rank = (1 - x) * 4 + (1 - y) * 2 + z % 2
    relay = [
        copy(40 + i, out.at[weight_rows(got_rank)], out.at[weight_rows(got_rank)], pz)
        for i, out in enumerate((gate_share, up_share))
    ]

    @pl.when(c == z % 2)
    def _():
        for cp in far:
            cp.start()

    for cp in swaps:
        cp.start()
    for cp in own_rows:
        cp.start()

    @pl.loop(0, 2 * (planes - 1))
    def _(i):
        d = i // 2 + 1
        direction = 1 - 2 * (i % 2)
        zz = z - d * direction

        @pl.when((zz >= 0) & (zz < planes))
        def _():
            index = 42 + 3 * (i % 2) + d - 1
            here = pltpu.make_async_remote_copy(
                kvp.at[zz], kvp.at[zz], send.at[index], recv.at[index], device_id=left,
                device_id_type=MESH,
            )
            here.wait_recv()

            @pl.when((i % 2 == 0) & (z < planes - 1))
            def _():
                pltpu.make_async_remote_copy(
                    kvp.at[zz], kvp.at[zz], send.at[index + 1], recv.at[index + 1],
                    device_id=right, device_id_type=MESH,
                ).start()

            @pl.when((i % 2 == 1) & (z > 0))
            def _():
                pltpu.make_async_remote_copy(
                    kvp.at[zz], kvp.at[zz], send.at[index + 1], recv.at[index + 1],
                    device_id=left, device_id_type=MESH,
                ).start()

            step(1, kvp[zz, 0, 0], kvp[zz, 1, 0], False)

            @pl.when(zz < z)
            def _():
                step(0, kvp[zz, 0, 0], kvp[zz, 1, 0], False)
                step(1, kvp[zz, 0, 1], kvp[zz, 1, 1], False)

            @pl.loop(2, 4)
            def _(t):
                step(t, kvp[zz, 0, 0], kvp[zz, 1, 0], False)
                step(t, kvp[zz, 0, 1], kvp[zz, 1, 1], False)

    outs[3].start()
    outs[4].start()
    ones = jnp.ones((8, 128), f32)

    @pl.loop(0, 4)
    def _(t):
        whole = jnp.sum(total[t], axis=1, keepdims=True)
        got = (acc[t] / whole).astype(bf16)
        attended[t, :, :HEAD] = got[:rows]
        attended[t, :, HEAD:] = got[rows:]
        sums[t] = lax.dot_general(
            ones, total[t], (((1,), (1,)), ((), ())), precision=lax.Precision.HIGHEST,
            preferred_element_type=f32,
        )

    lanes = pl.ds(pl.multiple_of(b * 2 * HEAD, 128), 2 * HEAD)
    mixes = [
        copy(48 + i, attended.at[o], mixed.at[:, lanes], peer)
        for i, (peer, o) in enumerate(((py, b_y), (pyc, b_yc), (pc, b_c)))
    ]
    for cp in mixes:
        cp.start()
    mixed[:, lanes] = attended[b]
    wo_first[2].wait_recv()
    wo_next[2].start()
    wo_first[3].wait_recv()
    wo_next[3].start()
    wo_next[0].wait_recv()
    wo_next[1].wait_recv()
    wo_next[4].start()
    wo_first[4].wait_recv()
    for cp in wo_next[2:]:
        cp.wait_recv()
    for cp in mixes:
        cp.wait_recv()
    outs[2].start()
    outs[5].start()
    narrow_mix[...] = (dot_nt(mixed[...], mix_in[...]) * own_columns[...].astype(f32)).astype(bf16)

    @pl.loop(0, width // 384)
    def _(n):
        at = span(n, 384)
        attn_out[:, at] = dot_nn(mixed[...], wo[:, at]) + dot_nn(narrow_mix[...], mix_out[:, at])

    rms_rows(attn_out, attn_out_gain, middle, rows, add=tokens)
    rms_rows(middle, feed_in_gain, normed_feed, rows)

    for cp in far[:1] + far[2:3]:
        cp.wait_recv()
    for cp in relay:
        cp.start()
    for cp in swaps:
        cp.wait()
    for cp in relay:
        cp.wait()

    @pl.when(c == z % 2)
    def _():
        for cp in far:
            cp.wait_send()

    for cp in own_rows + outs:
        cp.wait()
    for cp in stage + token_copies + across + wo_first + wo_next + mixes:
        cp.wait_send()

    @pl.loop(0, 2 * (planes - 1))
    def _(i):
        d = i // 2
        direction = 1 - 2 * (i % 2)
        zz = z - d * direction
        onward = z + direction

        @pl.when((zz >= 0) & (zz < planes) & (onward >= 0) & (onward < planes))
        def _():
            index = 42 + 3 * (i % 2) + d
            pltpu.make_async_remote_copy(
                kvp.at[zz], kvp.at[zz], send.at[index], recv.at[index], device_id=left,
                device_id_type=MESH,
            ).wait_send()


def attention_forward(
    tokens, gains, tables, columns, own_columns, cosine, sine, weights, share
):
    rows, width = tokens.shape
    planes = lax.axis_size("ulysses")
    return pl.pallas_call(
        attention_forward_kernel,
        out_shape=(
            shape((4, 2 * rows, HEAD), bf16),
            shape((planes, 2, 2, rows, HEAD), bf16),
            shape((2, 2, rows, HEAD), bf16),
            shape((4, rows, 2 * HEAD), bf16),
            shape((4, 8, 2 * rows), f32),
            shape((4 * rows, 3 * LANES), bf16),
            shape((rows, 8 * HEAD), bf16),
            shape((rows, LANES), bf16),
            shape((rows, width), f32),
            shape((rows, width), f32),
            shape((rows, width), bf16),
            shape((4 * rows, width), bf16),
            shape((width, 4 * HEAD), bf16),
            shape((8 * HEAD, width), bf16),
            shape((width, share), bf16),
            shape((width, share), bf16),
        ),
        in_specs=[VM] * 14 + [ANY] * 6,
        out_specs=(VM, ANY, ANY, VM, VM, VM, ANY, VM, VM, VM, VM, ANY, ANY, ANY, ANY, ANY),
        scratch_shapes=[
            pltpu.VMEM((4 * rows, width), bf16),
            pltpu.VMEM((width, 4 * HEAD), bf16),
            pltpu.VMEM((8 * HEAD, width), bf16),
            pltpu.VMEM((planes, 2, 2, rows, HEAD), bf16),
            pltpu.VMEM((2, 2, rows, HEAD), bf16),
            pltpu.VMEM((4, 2 * rows, HEAD), f32),
            pltpu.VMEM((4, 2 * rows, 128), f32),
            pltpu.VMEM((rows, 8 * HEAD), bf16),
            pltpu.SemaphoreType.DMA((51,)),
            pltpu.SemaphoreType.DMA((51,)),
            pltpu.SemaphoreType.DMA((12,)),
        ],
        compiler_params=pltpu.CompilerParams(
            collective_id=3, has_side_effects=True, vmem_limit_bytes=62 << 20
        ),
        name="attention_forward",
    )(tokens, *gains, *tables, columns, own_columns, cosine, sine, *weights)


class Places:
    def __init__(self):
        dp, b, z = lax.axis_index("dp"), lax.axis_index("blk"), lax.axis_index("ulysses")
        self.b, self.z, self.planes = b, z, lax.axis_size("ulysses")
        x, c = dp % 2, b % 2
        self.x, self.y, self.c = x, b // 2, c
        self.b_c, self.b_y = b + 1 - 2 * c, (b + 2) % 4
        self.b_yc = (self.b_c + 2) % 4
        other = dp + 1 - 2 * x
        self.dp, self.other = dp, other
        self.pc, self.py, self.pyc = (dp, self.b_c, z), (dp, self.b_y, z), (dp, self.b_yc, z)
        self.px = (other, b, z)
        self.plane = (
            self.pc, self.py, self.pyc, self.px,
            (other, self.b_c, z), (other, self.b_y, z), (other, self.b_yc, z),
        )
        self.rank = x * 4 + b
        self.near = (x * 4 + b, (1 - x) * 4 + b, (1 - x) * 4 + self.b_y, x * 4 + self.b_y)
        self.far = (x * 4 + self.b_c, (1 - x) * 4 + self.b_c, (1 - x) * 4 + self.b_yc, x * 4 + self.b_yc)

    def along(self, d):
        return (self.z + d) % self.planes

    def up(self, d):
        return (self.dp, self.b, self.along(d))


class TableSpread:
    COUNT = 16

    def __init__(self, place, copy, first, source, arrived, piece, gathered, local):
        self.place, self.source, self.arrived, self.piece = place, source, arrived, piece
        self.gathered = gathered
        n = place.planes
        self.q = piece.shape[0]
        half = n // 2

        def region(rank, h):
            return gathered.at[rank, pl.ds(h * half, half)]

        self.out = [
            copy(first + d - 1, source.at[span(place.along(d), self.q)], arrived.at[d - 1], place.up(d))
            for d in range(1, n)
        ]
        self.own = pltpu.make_async_copy(piece, gathered.at[place.rank, place.z], local)
        self.back = [
            copy(first + 2 + d, piece, gathered.at[place.rank, place.z], place.up(d))
            for d in range(1, n)
        ]
        own, rx, rxy, ry = place.near
        at = first + 6

        def same(i, ref, peer):
            return copy(at + i, ref, ref, peer)

        px, py, pc = place.px, place.py, place.pc
        self.first = [
            same(0, region(own, 0), px),
            same(1, region(own, 1), py),
            same(2, region(own, 1), px),
            same(3, region(own, 0), py),
            same(4, gathered.at[own], pc),
        ]
        self.next = [
            same(5, region(rx, 0), py),
            same(6, region(ry, 1), px),
            same(7, gathered.at[rx], pc),
            same(8, gathered.at[ry], pc),
            same(9, gathered.at[rxy], pc),
        ]

    def scatter(self):
        for c in self.out:
            c.start()

    def gather(self):
        for c in self.out:
            c.wait_recv()
        got = self.source[span(self.place.z, self.q), :].astype(f32)
        for i in range(self.place.planes - 1):
            got = got + self.arrived[i].astype(f32)
        self.piece[...] = got.astype(bf16)
        self.own.start()
        for c in self.back:
            c.start()

    def plane(self):
        for c in self.back:
            c.wait_recv()
        self.own.wait()
        for c in self.first:
            c.start()

    def forward(self):
        self.first[0].wait_recv()
        self.next[0].start()
        self.first[1].wait_recv()
        self.next[1].start()
        self.first[2].wait_recv()
        self.next[2].start()
        self.first[3].wait_recv()
        self.next[3].start()

    def corner(self):
        self.next[0].wait_recv()
        self.next[1].wait_recv()
        self.next[4].start()

    def finish(self):
        self.first[4].wait_recv()
        for c in self.next[2:]:
            c.wait_recv()
        for c in self.out + self.back + self.first + self.next:
            c.wait_send()


class TableReduce:
    COUNT = 10

    def __init__(self, place, copy, first, table, part, from_core, from_x, from_y, diag, total, local):
        self.part, self.from_core, self.from_x, self.from_y = part, from_core, from_x, from_y
        self.diag, self.total = diag, total
        m = total.shape[0]
        self.m, self.h = m, m // 2
        h0, h1 = pl.ds(0, self.h), pl.ds(self.h, self.h)
        self.h0, self.h1 = h0, h1
        self.core = [
            copy(first + i, table.at[place.far[i]], from_core.at[i], place.pc) for i in range(4)
        ]
        self.load = [
            pltpu.make_async_copy(table.at[place.near[i]], part.at[i], local(i)) for i in range(4)
        ]
        self.d = [
            copy(first + 4, part.at[2, h0], diag.at[h0], place.px),
            copy(first + 5, part.at[2, h1], diag.at[h1], place.py),
        ]
        self.e = [
            copy(first + 6, part.at[1, h0], from_x.at[h0], place.px),
            copy(first + 7, part.at[3, h1], from_y.at[h1], place.py),
            copy(first + 8, part.at[1, h1], from_x.at[h1], place.px),
            copy(first + 9, part.at[3, h0], from_y.at[h0], place.py),
        ]

    def begin(self):
        for c in self.core + self.load:
            c.start()

    def merge(self):
        for i in (2, 1, 3, 0):
            self.load[i].wait()
            self.core[i].wait_recv()
            add_into(self.part.at[i], self.from_core.at[i], self.m, 16)
            if i == 2:
                self.d[0].start()
                self.d[1].start()
        self.e[0].start()
        self.e[1].start()

    def corner(self):
        self.d[0].wait_recv()
        add_into(self.part.at[3, self.h0], self.diag.at[self.h0], self.h, 16)
        self.e[3].start()
        self.d[1].wait_recv()
        add_into(self.part.at[1, self.h1], self.diag.at[self.h1], self.h, 16)
        self.e[2].start()

    def finish(self):
        for e in self.e:
            e.wait_recv()

        @pl.loop(0, self.m // 16)
        def _(i):
            at = span(i, 16)
            self.total[at, :] = (
                self.part[0, at, :].astype(f32)
                + self.from_x[at, :].astype(f32)
                + self.from_y[at, :].astype(f32)
            ).astype(bf16)

        for c in self.core + self.d + self.e:
            c.wait_send()


def attention_backward_kernel(
    grad_mixed, queries, kvp, kvc, attended, sums, narrow, heads_in, query_out, key_out, value_out,
    columns, cosine, sine, mix_table,
    normed_hbm, wall_hbm, feed_table, feed_share,
    grad_normed, g_feed_table, g_feed_share, g_head_table, g_head_share,
    normed_all, wall, g, delta, inv, dq, kv_own, kv_far, kv_send, kv_got, grad_pre, back, part,
    from_core, from_y,
    a_part, a_core, a_x, a_y, a_diag, a_total, a_in, a_piece,
    s_in, s_piece,
    h_table, h_part, h_core, h_x, h_y, h_diag, h_total, h_in, h_piece,
    o_table, o_got, o_total, o_in, o_piece,
    send, recv, local,
):
    rows, width = grad_normed.shape
    place = Places()
    b, z, planes = place.b, place.z, place.planes
    copy = sender(send, recv)
    loads = [
        pltpu.make_async_copy(normed_hbm, normed_all, local.at[0]),
        pltpu.make_async_copy(wall_hbm, wall, local.at[1]),
    ]
    for c in loads:
        c.start()
    barrier = pltpu.get_barrier_semaphore()
    peers = list(place.plane) + [place.up(d) for d in range(1, planes)]
    for peer in peers:
        pl.semaphore_signal(barrier, inc=1, device_id=peer, device_id_type=MESH)
    pl.semaphore_wait(barrier, len(peers))

    swaps = []
    for j, (peer, pb) in enumerate(
        ((place.py, place.b_y), (place.pyc, place.b_yc), (place.pc, place.b_c))
    ):
        for h in range(2):
            lanes = pl.ds(pl.multiple_of(pb * 2 * HEAD + h * HEAD, 128), HEAD)
            swaps.append(
                copy(
                    2 * j + h,
                    grad_mixed.at[:, lanes],
                    g.at[b, pl.ds(h * rows, rows)],
                    peer,
                )
            )
    for c in swaps:
        c.start()
    at = 12
    feed_reduce = TableReduce(
        place, copy, at, feed_table, a_part, a_core, a_x, a_y, a_diag, a_total,
        lambda i: local.at[2 + i],
    )
    at += TableReduce.COUNT
    feed_spread = TableSpread(place, copy, at, a_total, a_in, a_piece, g_feed_table, local.at[6])
    at += TableSpread.COUNT
    share_spread = TableSpread(
        place, copy, at, feed_share, s_in, s_piece, g_feed_share, local.at[7]
    )
    at += TableSpread.COUNT
    head_reduce = TableReduce(
        place, copy, at, h_table, h_part, h_core, h_x, h_y, h_diag, h_total,
        lambda i: local.at[8 + i],
    )
    at += TableReduce.COUNT
    head_spread = TableSpread(place, copy, at, h_total, h_in, h_piece, g_head_table, local.at[12])
    at += TableSpread.COUNT
    out_spread = TableSpread(place, copy, at, o_total, o_in, o_piece, g_head_share, local.at[13])
    at += TableSpread.COUNT
    lanes_half = o_total.shape[0]
    out_swap = copy(
        at, o_table.at[span(1 - place.x, lanes_half)], o_got, place.px
    )

    share_spread.scatter()
    feed_reduce.begin()
    for h in range(2):
        lanes = pl.ds(pl.multiple_of(b * 2 * HEAD + h * HEAD, 128), HEAD)
        g[b, h * rows : (h + 1) * rows, :] = grad_mixed[:, lanes]
    for c in swaps:
        c.wait()

    ones = jnp.ones((8, HEAD), f32)

    @pl.loop(0, 4)
    def _(t):
        for h in range(2):
            at_h = slice(h * rows, (h + 1) * rows)
            lanes = slice(h * HEAD, (h + 1) * HEAD)
            product = g[t, at_h, :].astype(f32) * attended[t, :, lanes].astype(f32)
            delta[t, :, at_h] = lax.dot_general(
                ones, product, (((1,), (1,)), ((), ())), precision=lax.Precision.HIGHEST,
                preferred_element_type=f32,
            )
        inv[t] = 1.0 / sums[t]

    query = lax.broadcasted_iota(jnp.int32, (rows, 2 * rows), 1) % rows
    causal = lax.broadcasted_iota(jnp.int32, (rows, 2 * rows), 0) <= query

    def step(t, k, v, total, slot, masked):
        q, gt = queries[t], g[t]
        th = jnp.tanh(dot_nt(k, q) * (1.0 / soft_cap))
        p = jnp.exp(soft_cap * th) * inv[t, 0:1, :]
        if masked:
            p = jnp.where(causal, p, 0.0)
        total[1, slot] += dot_nn(p.astype(bf16), gt)
        ds = (p * (dot_nt(v, gt) - delta[t, 0:1, :]) * (1.0 - th * th)).astype(bf16)
        total[0, slot] += dot_nn(ds, q)
        dq[t] += dot_tn(ds, k)

    dq[...] = jnp.zeros_like(dq)
    kv_own[...] = jnp.zeros_like(kv_own)

    def kv_copy(d):
        return copy(6 + d - 1, kv_send.at[d - 1], kv_got.at[d - 1], place.up(d))

    for d in range(1, planes):
        pass

    @pl.loop(1, planes)
    def _(d):
        zz = (z + d) % planes
        kv_far[...] = jnp.zeros_like(kv_far)
        step(1, kvp[zz, 0, 0], kvp[zz, 1, 0], kv_far, 0, False)

        @pl.when(zz < z)
        def _():
            step(0, kvp[zz, 0, 0], kvp[zz, 1, 0], kv_far, 0, False)
            step(1, kvp[zz, 0, 1], kvp[zz, 1, 1], kv_far, 1, False)

        @pl.loop(2, 4)
        def _(t):
            step(t, kvp[zz, 0, 0], kvp[zz, 1, 0], kv_far, 0, False)
            step(t, kvp[zz, 0, 1], kvp[zz, 1, 1], kv_far, 1, False)

        kv_send[d - 1] = kv_far[...].astype(bf16)
        for k in range(1, planes):

            @pl.when(d == k)
            def _(k=k):
                kv_copy(k).start()
                if k == 1:
                    feed_reduce.merge()
                    share_spread.gather()
                if k == 2:
                    feed_reduce.corner()
                    share_spread.plane()

    feed_reduce.finish()
    feed_spread.scatter()
    step(0, kvp[z, 0, 0], kvp[z, 1, 0], kv_own, 0, True)
    step(1, kvp[z, 0, 0], kvp[z, 1, 0], kv_own, 0, False)
    step(1, kvp[z, 0, 1], kvp[z, 1, 1], kv_own, 1, True)

    @pl.loop(2, 4)
    def _(t):
        step(t, kvc[0, t - 2], kvc[1, t - 2], kv_own, t, True)
        step(t, kvp[z, 0, 0], kvp[z, 1, 0], kv_own, 0, False)
        step(t, kvp[z, 0, 1], kvp[z, 1, 1], kv_own, 1, False)

    for c in loads:
        c.wait()
    feed_spread.gather()
    for d in range(1, planes):
        kv_copy(d).wait_recv()
        kv_own[:, 0:2] += kv_got[d - 1].astype(f32)
    half_head = HEAD // 2

    @pl.loop(0, 4)
    def _(t):
        at = span(t, rows)
        cos, sin = cosine[at, :], sine[at, :]
        masks = columns[at, :].astype(f32)

        def turned(pre, scale):
            first, second = pre[:, :half_head], pre[:, half_head:]
            one, two = first * cos + second * sin, second * cos - first * sin
            if scale != 1.0:
                one, two = one * scale, two * scale
            return jnp.concatenate([one, two], axis=1).astype(bf16)

        for h in range(2):
            grad_pre[at, h * HEAD : (h + 1) * HEAD] = turned(
                dq[t, h * rows : (h + 1) * rows, :], HEAD ** (-0.5)
            )
        grad_pre[at, 2 * HEAD : 3 * HEAD] = turned(kv_own[0, t], 1.0)
        grad_pre[at, 3 * HEAD :] = kv_own[1, t].astype(bf16)
        for i, (lanes, table) in enumerate(
            (
                (slice(0, 2 * HEAD), query_out),
                (slice(2 * HEAD, 3 * HEAD), key_out),
                (slice(3 * HEAD, 4 * HEAD), value_out),
            )
        ):
            back[at, i * LANES : (i + 1) * LANES] = (
                dot_nt(grad_pre[at, lanes], table[...]) * masks
            ).astype(bf16)

    share_spread.forward()
    for i, lanes in enumerate(
        (slice(0, 2 * HEAD), slice(2 * HEAD, 3 * HEAD), slice(3 * HEAD, 4 * HEAD))
    ):
        o_table[:, lanes] = dot_tn(
            narrow[:, i * LANES : (i + 1) * LANES], grad_pre[:, lanes]
        ).astype(bf16)
    out_swap.start()
    h_table[:, 3 * RANK :, :] = mix_table[...]

    @pl.loop(0, width // 384)
    def _(n):
        at = span(n, 384)
        got = dot_tn(back[...], normed_all[:, at]).astype(bf16)
        for i in range(3):
            for a in range(ADAPTERS):
                first = i * LANES + a * RANK
                h_table[a, i * RANK : (i + 1) * RANK, at] = got[first : first + RANK]

    head_reduce.begin()
    feed_spread.plane()

    def project(slot, target):
        at_rows = span(target, rows)

        @pl.loop(0, width // 384)
        def _(n):
            at = span(n, 384)
            part[slot, :, at] = (
                dot_nt(grad_pre[at_rows, :], wall[at, :])
                + dot_nn(back[at_rows, :], heads_in[:, at])
            ).astype(bf16)

    to_core = [copy(9 + i, part.at[i], from_core.at[i], place.pc) for i in range(2)]
    to_y = copy(11, part.at[2], from_y, place.py)
    project(0, place.b_yc)
    to_core[0].start()
    share_spread.corner()
    project(2, place.b_y)
    to_core[0].wait_recv()
    add_into(part.at[2], from_core.at[0], rows)
    to_y.start()
    head_reduce.merge()
    feed_spread.forward()
    out_swap.wait_recv()

    @pl.loop(0, lanes_half // 16)
    def _(i):
        at = span(i, 16)
        mine = pl.ds(pl.multiple_of(place.x * lanes_half + i * 16, 16), 16)
        o_total[at, :] = (o_table[mine, :].astype(f32) + o_got[at, :].astype(f32)).astype(bf16)

    out_spread.scatter()
    project(1, place.b_c)
    to_core[1].start()
    head_reduce.corner()
    feed_spread.corner()
    out_spread.gather()
    project(3, b)
    head_reduce.finish()
    head_spread.scatter()
    out_spread.plane()
    head_spread.gather()
    to_core[1].wait_recv()
    out_spread.forward()
    head_spread.plane()
    out_spread.corner()
    head_spread.forward()
    to_y.wait_recv()

    @pl.loop(0, rows // 32)
    def _(i):
        at = span(i, 32)
        grad_normed[at, :] = (
            part[3, at, :].astype(f32)
            + from_core[1, at, :].astype(f32)
            + from_y[at, :].astype(f32)
        ).astype(grad_normed.dtype)

    head_spread.corner()
    for spread in (share_spread, feed_spread, out_spread, head_spread):
        spread.finish()
    out_swap.wait_send()
    to_y.wait_send()
    for c in to_core:
        c.wait_send()
    for d in range(1, planes):
        kv_copy(d).wait_send()


def attention_backward(
    grad_mixed, kept, tables, columns, cosine, sine, mix_table, normed_all, wall, feed_table,
    feed_share,
):
    rows = grad_mixed.shape[0]
    width = wall.shape[0]
    planes = lax.axis_size("ulysses")
    m = feed_table.shape[1]
    fs, fw = feed_share.shape
    hm = 4 * RANK
    ow = 4 * HEAD
    om = LANES // 2
    count = 12 + 2 * TableReduce.COUNT + 4 * TableSpread.COUNT + 1

    def reduce_scratch(m):
        return [
            pltpu.VMEM((4, m, width), bf16),
            pltpu.VMEM((4, m, width), bf16),
            pltpu.VMEM((m, width), bf16),
            pltpu.VMEM((m, width), bf16),
            pltpu.VMEM((m, width), bf16),
            pltpu.VMEM((m, width), bf16),
        ]

    def spread_scratch(m, w):
        return [
            pltpu.VMEM((planes - 1, m // planes, w), bf16),
            pltpu.VMEM((m // planes, w), bf16),
        ]

    return pl.pallas_call(
        attention_backward_kernel,
        out_shape=(
            shape((rows, width), f32),
            shape((8, planes, m // planes, width), bf16),
            shape((8, planes, fs // planes, fw), bf16),
            shape((8, planes, hm // planes, width), bf16),
            shape((8, planes, om // planes, ow), bf16),
        ),
        in_specs=[VM] * 15 + [ANY] * 3 + [VM],
        out_specs=(VM, ANY, ANY, ANY, ANY),
        scratch_shapes=[
            pltpu.VMEM((4 * rows, width), bf16),
            pltpu.VMEM((width, 4 * HEAD), bf16),
            pltpu.VMEM((4, 2 * rows, HEAD), bf16),
            pltpu.VMEM((4, 8, 2 * rows), f32),
            pltpu.VMEM((4, 8, 2 * rows), f32),
            pltpu.VMEM((4, 2 * rows, HEAD), f32),
            pltpu.VMEM((2, 4, rows, HEAD), f32),
            pltpu.VMEM((2, 2, rows, HEAD), f32),
            pltpu.VMEM((planes - 1, 2, 2, rows, HEAD), bf16),
            pltpu.VMEM((planes - 1, 2, 2, rows, HEAD), bf16),
            pltpu.VMEM((4 * rows, 4 * HEAD), bf16),
            pltpu.VMEM((4 * rows, 3 * LANES), bf16),
            pltpu.VMEM((4, rows, width), bf16),
            pltpu.VMEM((2, rows, width), bf16),
            pltpu.VMEM((rows, width), bf16),
        ]
        + reduce_scratch(m)
        + spread_scratch(m, width)
        + spread_scratch(fs, fw)
        + [pltpu.VMEM((ADAPTERS, hm, width), bf16)]
        + reduce_scratch(hm)
        + spread_scratch(hm, width)
        + [
            pltpu.VMEM((LANES, ow), bf16),
            pltpu.VMEM((om, ow), bf16),
            pltpu.VMEM((om, ow), bf16),
        ]
        + spread_scratch(om, ow)
        + [
            pltpu.SemaphoreType.DMA((count,)),
            pltpu.SemaphoreType.DMA((count,)),
            pltpu.SemaphoreType.DMA((14,)),
        ],
        compiler_params=pltpu.CompilerParams(
            collective_id=4, has_side_effects=True, vmem_limit_bytes=62 << 20
        ),
        name="attention_backward",
    )(
        grad_mixed, *kept, *tables, columns, cosine, sine, mix_table, normed_all, wall, feed_table,
        feed_share,
    )


def take_columns(table, index, width):
    return lax.dynamic_slice_in_dim(table, index * width, width, axis=1)


def shards(
    tokens,
    query_weight,
    key_projection,
    value_projection,
    out_weight,
    gate_weight,
    up_weight,
    down_weight,
    attn_in_gain,
    attn_out_gain,
    feed_in_gain,
    feed_out_gain,
    adapt_heads_in,
    adapt_query_out,
    adapter_key_value_second,
    adapt_mix_in,
    adapt_mix_out,
    adapt_feed_in,
    adapt_feed_out,
    adapt_down_in,
    adapt_down_out,
    adapter_ids,
    cotangent,
):
    rows, width = tokens.shape
    blk_n = lax.axis_size("blk")
    z_n = lax.axis_size("ulysses")
    dp_n = lax.axis_size("dp")
    b = lax.axis_index("blk")
    z = lax.axis_index("ulysses")
    rank = lax.axis_index("dp") % 2 * blk_n + b
    ff = gate_weight.shape[1]
    share = ff // (2 * blk_n)
    weights = (
        query_weight, key_projection, value_projection, out_weight, gate_weight, up_weight,
        down_weight,
    )
    if dp_n > 2:
        weights = tuple(
            lax.dynamic_slice_in_dim(
                lax.all_gather(weight, PLANE, axis=0, tiled=True),
                rank * (weight.shape[0] * dp_n // 2),
                weight.shape[0] * dp_n // 2,
            )
            for weight in weights
        )
    down_rows = weights[6]

    block_first = (jnp.arange(blk_n, dtype=jnp.int32) * z_n + z) * rows
    sequence = jnp.where(block_first >= PROMPT, 1 + (block_first - PROMPT) // CONT, 0)
    all_ids = lax.all_gather(adapter_ids.astype(f32), "dp", axis=0, tiled=True).astype(jnp.int32)
    seq_ids = jnp.arange(CONTS + 1, dtype=jnp.int32)
    block_ids = jnp.sum(
        jnp.where(sequence[None, :, None] == seq_ids[None, None, :], all_ids[:, None, :], 0), axis=2
    )
    owner = jnp.arange(LANES, dtype=jnp.int32) // RANK
    block_masks = (block_ids[:, :, None] == owner).astype(f32)
    group_masks = lax.dynamic_index_in_dim(block_masks, lax.axis_index("dp"), 0, keepdims=False)
    own_mask = lax.dynamic_index_in_dim(group_masks, b, 0, keepdims=True)[0]
    group_columns = jnp.repeat(group_masks, rows, axis=0).astype(bf16)

    heads_in = jnp.transpose(adapt_heads_in, (1, 0, 2, 3)).reshape(3, LANES, width)
    query_out = take_columns(adapt_query_out.reshape(LANES, -1), b, 2 * HEAD)
    kv_out = jnp.transpose(adapter_key_value_second, (1, 0, 2, 3)).reshape(2, LANES, -1)
    key_out = take_columns(kv_out[0], b, HEAD)
    value_out = take_columns(kv_out[1], b, HEAD)
    mix_in = adapt_mix_in.reshape(LANES, -1)
    mix_out = adapt_mix_out.reshape(LANES, -1)
    feed_in = jnp.transpose(adapt_feed_in, (1, 0, 2, 3)).reshape(2, LANES, width)
    feed_out = jnp.transpose(adapt_feed_out, (1, 0, 2, 3)).reshape(2, LANES, ff)
    gate_out = take_columns(feed_out[0], rank, share)
    up_out = take_columns(feed_out[1], rank, share)
    down_in = take_columns(adapt_down_in.reshape(LANES, ff), rank, share)
    down_out = adapt_down_out.reshape(LANES, width)

    token_index = (block_first[:, None] + jnp.arange(rows, dtype=jnp.int32)).reshape(-1)
    positions = jnp.where(token_index >= PROMPT, PROMPT + (token_index - PROMPT) % CONT, token_index)
    half = HEAD // 2
    inverse = rope_base ** (-2.0 * jnp.arange(half, dtype=f32) / HEAD)
    angles = positions.astype(f32)[:, None] * inverse[None, :]
    cosine, sine = jnp.cos(angles), jnp.sin(angles)
    residual = tokens.astype(f32)
    (
        queries, kvp, kvc, attended, exp_sum, narrow_heads, mixed, narrow_mix, attn_out, middle,
        normed_feed, normed_all, head_weight, out_full, gate_share, up_share,
    ) = attention_forward(
        tokens,
        (attn_in_gain[None], attn_out_gain[None], feed_in_gain[None]),
        (heads_in.reshape(3 * LANES, width), query_out, key_out, value_out, mix_in, mix_out),
        group_columns,
        jnp.broadcast_to(own_mask, (rows, LANES)).astype(bf16),
        cosine,
        sine,
        weights[:6],
        share,
    )
    order = jnp.array([[0, 1], [4, 5], [6, 7], [2, 3]], dtype=jnp.int32)
    pair_masks = lax.dynamic_slice_in_dim(
        block_masks, lax.axis_index("dp") // 2 * 2, 2, axis=0
    ).reshape(8, LANES)
    plane_columns = jnp.repeat(
        jnp.take(pair_masks, (rank % 8) ^ order, axis=0), rows, axis=1
    ).reshape(4, 2 * rows, LANES).astype(bf16)
    feed_in2 = feed_in.reshape(2 * LANES, width)
    tables = (feed_in2, gate_out, up_out, down_in, down_out, plane_columns)
    branch, narrow_feed, feed_all, gate_up = feed_forward(
        normed_feed, *tables, gate_share, up_share, down_rows
    )
    layer_out = (middle + rms_scale(branch, feed_out_gain)).astype(bf16)
    grad_top = cotangent.astype(f32)
    grad_branch = norm_back(branch, feed_out_gain, grad_top).astype(bf16)
    grad_feed, back_feed, grad_feed_out, grad_down_in, grad_down_out = feed_backward(
        grad_branch, *tables, narrow_feed, gate_share, up_share, down_rows, gate_up
    )
    grad_feed = grad_feed.astype(f32)
    grad_feed_in = dot_tn(back_feed.reshape(-1, 2 * LANES), feed_all.reshape(-1, width))
    grad_middle = grad_top + norm_back(middle, feed_in_gain, grad_feed)
    grad_attn = norm_back(attn_out, attn_out_gain, grad_middle).astype(bf16)

    back_mix = (dot_nt(grad_attn, mix_out) * own_mask).astype(bf16)
    grad_mix_in, grad_mix_out = dot_tn(back_mix, mixed), dot_tn(narrow_mix, grad_attn)
    grad_mixed = (dot_nt(grad_attn, out_full) + dot_nn(back_mix, mix_in)).astype(bf16)
    def by_rank(table):
        return table.astype(bf16).reshape(-1, ADAPTERS, RANK, width).transpose(1, 0, 2, 3).reshape(
            ADAPTERS, -1, width
        )

    feed_table = by_rank(jnp.concatenate([grad_feed_in, grad_down_out, grad_mix_out]))
    feed_share = jnp.concatenate(
        [grad_feed_out.reshape(2 * LANES, share), grad_down_in]
    ).astype(bf16)
    mix_table = jnp.pad(
        grad_mix_in.astype(bf16).reshape(ADAPTERS, RANK, -1), ((0, 0), (0, 0), (0, width - mixed.shape[1]))
    )
    grad_normed, feed_rows, feed_columns, head_rows, head_columns = attention_backward(
        grad_mixed,
        (queries, kvp, kvc, attended, exp_sum, narrow_heads),
        (heads_in.reshape(3 * LANES, width), query_out, key_out, value_out),
        group_columns,
        cosine,
        sine,
        mix_table,
        normed_all,
        head_weight,
        feed_table,
        feed_share,
    )
    tokens_grad = grad_middle + norm_back(residual, attn_in_gain, grad_normed)

    feed_rows = feed_rows.reshape(ADAPTERS, 4, RANK, width)
    feed_columns = (
        feed_columns.reshape(8, 3, ADAPTERS, RANK, share)
        .transpose(2, 1, 3, 0, 4)
        .reshape(ADAPTERS, 3, RANK, ff)
    )
    head_rows = head_rows.reshape(ADAPTERS, 4, RANK, width)
    head_columns = (
        head_columns.reshape(2, 4, LANES // 2, 4 * HEAD)
        .transpose(0, 2, 1, 3)
        .reshape(ADAPTERS, RANK, 4, 4 * HEAD)
    )

    def joined(first, last):
        return head_columns[..., first:last].reshape(ADAPTERS, RANK, -1)

    summed = (
        head_rows[:, :3],
        joined(0, 2 * HEAD),
        jnp.stack([joined(2 * HEAD, 3 * HEAD), joined(3 * HEAD, 4 * HEAD)], axis=1),
        head_rows[:, 3, :, : mixed.shape[1]],
        feed_rows[:, 3],
        feed_rows[:, :2],
        feed_columns[:, :2],
        feed_columns[:, 2],
        feed_rows[:, 2],
    )
    summed = tuple(table.astype(f32) for table in summed)
    if dp_n > 2:
        summed = tuple(lax.psum(table * 0.5, "dp") for table in summed)
    return (layer_out, tokens_grad) + summed


def solution(mesh):
    sharded = P(EVERY, None)
    rowwise = P(PLANE, None)
    placed = (
        (sharded,) + (rowwise,) * 7 + (P(),) * 13 + (P("dp", None), sharded)
    )
    return jax.shard_map(
        shards,
        mesh=mesh,
        in_specs=placed,
        out_specs=(sharded, sharded) + (P(),) * 9,
        check_vma=False,
    )
```

time: 1650 us -> 781 us (0.47)
  waiting for transfers between devices: 1100 us -> 0 us
  Pallas kernels: 0 us -> 685 us
  matrix products: 289 us -> 14.6 us
  local copies, waits for them, and re-layouts: 98.8 us -> 39.2 us
  other arithmetic: 65.9 us -> 28.6 us
  blocking collectives: 39 us -> 5.09 us
  starting transfers between devices: 28.1 us -> 0 us
    pallas_call x0 -> x4, Pallas kernels: none -> 685 us  [the longest x1 251 us: attention_forward(): pl.pallas_call(attention_forward_kernel, out_shape=(shape((4, 2 * rows, H...]
    all_gather x9 -> x0, waiting for transfers between devices: 589 us -> none  [the longest x1 186 us: shards(): lax.all_gather(gate_weight, ('dp', 'blk'), axis=0, tiled=True)]
    psum x1 -> x0, waiting for transfers between devices: 396 us -> none  [shards(): lax.psum((gradients[0], gradients[1], gradients[2], gradients[3], gradien...]
    dot_general x63 -> x6, matrix products: 289 us -> 14.6 us  [the longest x3 7.46 us: dot_tn(): lax.dot_general(a, b, (((0,), (0,)), ((), ())), preferred_element_type=f32)]
    all_to_all x6 -> x0, waiting for transfers between devices: 67.7 us -> none  [the longest x1 26.1 us: shards(): lax.all_to_all(grad_mixed.reshape(sequence_local_rows, swap_count, -1), '...]
    reduce_scatter x2 -> x0, waiting for transfers between devices: 40 us -> none  [the longest x1 27 us: shards(): lax.psum_scatter(grad_value_all.reshape(cycle_count * block_rows, kv_loca...]
    all_to_all x2 -> x0, blocking collectives: 39 us -> none  [the longest x1 19.6 us: shards(): lax.all_to_all(key_rows, 'ulysses', split_axis=1, concat_axis=0, tiled=True)]
    unnamed x261 -> x61, local copies, waits for them, and re-layouts: 45.3 us -> 11.5 us
  transfers between devices with their start and end apart: 18 -> 0, of which waited for: 16 -> 0; matrix products, arithmetic and copies ran while one was open for 14% -> 0% of each run, Pallas kernels for 0% -> 0%
where the time goes in v1:
time: 781 us; the launch traced here: 774 us
  Pallas kernels  685 us (88%)
  local copies, waits for them, and re-layouts  39.2 us (5%)
  other arithmetic  28.6 us (4%)
  matrix products  14.6 us (2%)
    pallas_call x1, Pallas kernels, attention_forward(): pl.pallas_call(attention_forward_kernel, out_shape=(shape((4, 2 * rows, H...  251 us
    pallas_call x1, Pallas kernels, attention_backward(): pl.pallas_call(attention_backward_kernel, out_shape=(shape((rows, width),...  189 us
    pallas_call x1, Pallas kernels, feed_backward(): pl.pallas_call(feed_backward_kernel, out_shape=(shape((rows, width), bf16...  126 us
    pallas_call x1, Pallas kernels, feed_forward(): pl.pallas_call(feed_forward_kernel, out_shape=(shape((rows, width), f32),...  119 us

profile of v1, /device:TPU:0, one launch (start us, length us, event | category | flops | bytes accessed | tf_op | source)
XLA Modules:
  0.0 773.9 jit_solution(9363775722018202207)
XLA Ops:
  0.7 1.0 copy-done
  1.7 0.7 convert_bitcast_fusion.1
  2.4 5.1 all-gather
  7.5 0.7 compare_and_fusion
  8.2 0.1 select_reduce_fusion
  8.6 0.7 compare_select_fusion.1
  9.5 0.6 gather_fusion
  10.2 1.3 broadcast_in_dim.46.attn_in_gain
  11.5 1.3 broadcast_in_dim.47.attn_out_gain
  12.8 1.3 broadcast_in_dim.48.feed_in_gain
  14.1 0.6 broadcast_in_dim.82.own_columns
  14.8 0.7 constant_dynamic-slice_fusion.6.query_out
  15.4 0.7 broadcast_in_dim.81
  16.2 0.9 broadcast_in_dim.86
  17.0 1.2 fusion.27
  18.2 0.7 constant_dynamic-slice_fusion.4
  18.9 3.0 multiply_sine_fusion
  21.9 1.1 copy.71
  23.0 1.4 copy.70
  24.4 0.9 copy-done.11
  25.3 0.4 fusion.25
  25.8 1.8 constant_dynamic-slice_fusion
  27.6 0.7 constant_dynamic-slice_fusion.2.gate_out
  28.3 250.9 %attention_forward.1 = (bf16[4,512,256]{2,1,0:T(8,128)(2,1)}, bf16[4,2,2,256,256]{4,3,2,1,0:T(8,128)(2,1)}, bf16[2,2,256,256]{3,2,1,0:T(8,128)(2,1)}, bf16[4,256...) custom-call(bf16[256,2304]{1,0:T(8,128)(2,1)} %tokens.1, ...), custom_call_target="tpu_custom_call" | custom-call | tf_op jit(solution)/shard_map/attention_forward/pallas_call | solution.py:901
  279.2 119.0 %feed_forward.1 = (f32[256,2304]{1,0:T(8,128)}, bf16[4,3,512,128]{3,2,1,0:T(8,128)(2,1)}, bf16[4,512,2304]{2,1,0:T(8,128)(2,1)}, bf16[4,2,512,1152]{3,2,1,0:T(8,128)(2,1)}) custom-call(bf16[256,2304]{1,0:T(8,128)(2,1)} %get-tuple-element.42.own, bf16[256,2304]{1,0:T(8,128)(2,1)} %bitcast.84, bf16[128,1152]{1,0:T(8,128)(2,1)} %constant_dynamic-slice_fusion.2.gate_out, ...), custom_call_target="tpu_custom_call" | custom-call | tf_op jit(solution)/shard_map/feed_forward/pallas_call | solution.py:427
  398.3 2.4 fusion.6
  400.7 4.1 fusion.5
  404.8 126.1 %feed_backward.1 = (bf16[256,2304]{1,0:T(8,128)(2,1)}, bf16[4,512,256]{2,1,0:T(8,128)(2,1)}, f32[2,128,1152]{2,1,0:T(8,128)}, f32[128,1152]{1,0:T(8,128)}, f32[128,2304]{1,0:T(8,128)}) custom-call(bf16[256,2304]{1,0:T(8,128)(2,1)} %get-tuple-element.139.own, bf16[256,2304]{1,0:T(8,128)(2,1)} %bitcast.85, ...), custom_call_target="tpu_custom_call" | custom-call | tf_op jit(solution)/shard_map/feed_backward/pallas_call | solution.py:459
  531.0 6.8 fusion
  537.8 0.6 multiply_reduce_fusion.3
  538.4 1.0 copy-done.8
  539.4 1.1 multiply_reduce_fusion.1
  540.6 1.4 copy-done.2
  542.0 0.4 subtract_convert_fusion
  542.4 5.3 fusion.28
  547.7 0.5 fusion.12
  548.2 1.4 fusion.3.grad_mixed
  549.6 0.3 convolution_convert_fusion
  550.0 0.3 convolution_convert_fusion.1
  550.3 0.9 pad.4.mix_table
  551.3 0.2 pad_maximum_fusion
  551.5 1.6 copy.73
  553.2 1.0 pad_maximum_fusion.1.feed_share
  554.2 188.6 %attention_backward.1 = (f32[256,2304]{1,0:T(8,128)}, bf16[8,4,16,2304]{3,2,1,0:T(8,128)(2,1)}, bf16[8,4,96,1152]{3,2,1,0:T(8,128)(2,1)}, bf16[8,4,16,2304]{3,2,1,0:T(8,128)(2,1)}, bf16[8,4,16,1024]{3,2,1,0:T(8,128)(2,1)}) custom-call(bf16[256,2048]{1,0:T(8,128)(2,1)} %fusion.3.grad_mixed, bf16[4,512,256]{2,1,0:T(8,128)(2,1)} %get-tuple-element.51.queries, ...), custom_call_target="tpu_custom_call" | custom-call | tf_op jit(solution)/shard_map/attention_backward/pallas_call | solution.py:1441
  742.8 1.3 copy.74
  744.2 7.2 copy.83
  751.4 0.5 fusion.7
  751.9 1.1 copy-done.3
  753.0 2.0 fusion.10
  755.1 0.1 convert_bitcast_fusion
  755.2 1.1 copy.82
  756.3 0.2 copy.76
  756.5 0.2 stack_reshape.6
  756.6 0.2 copy.77
  756.9 0.2 stack_reshape.7
  757.1 1.0 copy.79
  758.2 0.5 copy-done.14
  758.6 1.1 bitcast_convert_fusion.2
  759.7 2.2 slice_convert_fusion.1
  761.9 1.6 slice_convert_fusion.2
  763.6 1.6 bitcast_convert_fusion
  765.2 2.7 fusion.11
  767.9 1.1 slice_convert_fusion
  769.0 4.4 copy.80
  (79 shorter events, 1.1 us)
Async XLA Ops:
  0.6 1.1 copy-start
  0.7 21.3 %copy-start.17 = (bf16[8,2,16,2304]{3,2,1,0:T(8,128)(2,1)S(1)}, bf16[8,2,16,2304]{3,2,1,0:T(8,128)(2,1)}, u32[]{:S(2)}) copy-start(bf16[8,2,16,2304]{3,2,1,0:T(8,128)(2,1)} %param.41) | copy-start | bytes 3538948
  17.0 6.0 copy-start.16
  21.9 3.4 copy-start.11
  279.2 119.1 %copy-start.6 = (bf16[256,2304]{1,0:T(8,128)(2,1)S(1)}, bf16[256,2304]{1,0:T(8,128)(2,1)}, u32[]{:S(2)}) copy-start(bf16[256,2304]{1,0:T(8,128)(2,1)} %param.46) | copy-start | bytes 3538948
  279.2 119.1 %copy-start.26 = (f32[2304]{0:T(1024)S(1)}, f32[2304]{0:T(1024)}, u32[]{:S(2)}) copy-start(f32[2304]{0:T(1024)} %param.35) | copy-start | bytes 27652
  398.2 2.4 copy-start.4
  530.9 6.8 copy-start.5
  530.9 6.8 copy-start.10
  530.9 6.8 copy-start.23
  537.8 1.7 copy-start.8
  537.8 1.7 copy-start.22
  540.6 1.4 copy-start.2
  542.4 5.3 copy-start.13
  542.4 5.8 copy-start.15
  547.7 1.9 copy-start.25
  548.2 1.8 copy-start.20
  549.6 1.6 copy-start.21
  549.6 1.6 copy-start.19
  551.5 1.6 copy-start.18
  744.1 7.3 copy-start.7
  744.1 7.2 copy-start.9
  744.1 7.2 copy-start.24
  751.4 1.7 copy-start.3
  756.6 2.0 copy-start.14
  757.1 8.1 %slice-start = ((s8[7077888]{0:T(1024)(128)(4,1)}), s8[4194304]{0:T(1024)(128)(4,1)S(1)}, s32[]{:S(2)}) async-start(s8[7077888]{0:T(1024)(128)(4,1)} %bitcast.78), calls=%async_computation | async-start | bytes 8388608
  758.6 3.3 copy-start.12
  759.7 5.5 slice-start.1
  769.0 4.4 copy-start.1

commit v2 on v1

--- a/solution.py
+++ b/solution.py
@@ -1,3 +1,5 @@
+import math
+
 import jax
 import jax.numpy as jnp
 from jax import lax
@@ -36,13 +38,7 @@
     return lax.dot_general(a, b, (((0,), (0,)), ((), ())), preferred_element_type=f32)
 
 
-def rms_scale(values, gain_row):
-    return (
-        values * lax.rsqrt(jnp.mean(values * values, axis=-1, keepdims=True) + epsilon) * gain_row
-    )
-
-
-def norm_back(values, gain_row, grad_out):
+def norm_grad(values, gain_row, grad_out):
     scale = lax.rsqrt(jnp.mean(values * values, axis=-1, keepdims=True) + epsilon)
     weighted = grad_out * gain_row
     return scale * weighted - values * (
@@ -149,6 +145,36 @@
     def finish(self):
         for c in self.c:
             c.wait_send()
+
+
+def plane_masks(masks, i, rows):
+    group = (i + 1) // 2 % 2
+    near = (lax.axis_index("blk") + 2 * (i // 2)) % 4
+    far = near + 1 - 2 * (near % 2)
+    first = masks[group, pl.ds(near, 1), :]
+    second = masks[group, pl.ds(far, 1), :]
+    return jnp.where(
+        lax.broadcasted_iota(jnp.int32, (2 * rows, LANES), 0) < rows, first, second
+    )
+
+
+def feed_table_copies(rank, share, feed_in_hbm, feed_out_hbm, down_in_hbm, feed_in, feed_out, down_in):
+    lanes = pl.ds(pl.multiple_of(rank * share, 128), share)
+    return [
+        (feed_in_hbm.at[:, 0], feed_in.at[0]),
+        (feed_in_hbm.at[:, 1], feed_in.at[1]),
+        (feed_out_hbm.at[:, 0, :, lanes], feed_out.at[0]),
+        (feed_out_hbm.at[:, 1, :, lanes], feed_out.at[1]),
+        (down_in_hbm.at[:, :, lanes], down_in),
+    ]
+
+
+def feed_table_scratch(width, share):
+    return [
+        pltpu.VMEM((2, ADAPTERS, RANK, width), bf16),
+        pltpu.VMEM((2, ADAPTERS, RANK, share), bf16),
+        pltpu.VMEM((ADAPTERS, RANK, share), bf16),
+    ]
 
 
 class PlaneReduce:
@@ -200,7 +226,7 @@
                     self.d[0].start()
                     self.d[1].start()
 
-    def finish(self, out):
+    def finish(self, write, between=None):
         h, h0, h1 = self.h, pl.ds(0, self.h), pl.ds(self.h, self.h)
         self.merge(3)
         self.e[1].start()
@@ -210,6 +236,8 @@
         self.d[1].wait_recv()
         add_into(self.part.at[1, h1], self.diag.at[h1], h)
         self.e[2].start()
+        if between is not None:
+            between()
         self.merge(0)
         for e in self.e:
             e.wait_recv()
@@ -217,11 +245,12 @@
         @pl.loop(0, self.rows // 32)
         def _(i):
             at = pl.ds(pl.multiple_of(i * 32, 32), 32)
-            out[at, :] = (
+            write(
+                at,
                 self.part[0, at, :].astype(f32)
                 + self.from_x[at, :].astype(f32)
-                + self.from_y[at, :].astype(f32)
-            ).astype(out.dtype)
+                + self.from_y[at, :].astype(f32),
+            )
 
         for c in self.core[2:] + self.d + self.e:
             c.wait_send()
@@ -231,14 +260,19 @@
 GELU_CUBE = 0.044715
 
 
+def plane_rank():
+    return lax.axis_index("dp") % 2 * 4 + lax.axis_index("blk")
+
+
 def span(i, size):
     return pl.ds(pl.multiple_of(i * size, size), size)
 
 
 def feed_forward_kernel(
-    own, feed_in, gate_out, up_out, down_in, down_out, columns, gate_hbm, up_hbm, down_hbm,
-    branch, narrow, feed_all, gate_up,
-    gate, up, down, land, hidden, saved, part, odd, from_core, from_x, from_y, diag,
+    own, middle, cotangent, gains, masks, down_out, feed_in_hbm, feed_out_hbm, down_in_hbm,
+    gate_hbm, up_hbm, down_hbm,
+    layer_out, grad_branch, narrow, feed_all, gate_up,
+    feed_in, feed_out, down_in, gate, up, down, land, hidden, saved, part, odd, from_core, from_x, from_y, diag,
     send, recv, load, store,
 ):
     rows = own.shape[0]
@@ -247,7 +281,13 @@
     tile = 384
     loads = [
         pltpu.make_async_copy(s, d, load.at[i])
-        for i, (s, d) in enumerate(((gate_hbm, gate), (up_hbm, up), (down_hbm, down)))
+        for i, (s, d) in enumerate(
+            [(gate_hbm, gate), (up_hbm, up), (down_hbm, down)]
+            + feed_table_copies(
+                plane_rank(), share, feed_in_hbm, feed_out_hbm, down_in_hbm, feed_in, feed_out,
+                down_in,
+            )
+        )
     ]
     for c in loads:
         c.start()
@@ -279,18 +319,15 @@
             for c in keep(i - 2):
                 c.wait()
 
-        masks = columns[i].astype(f32)
-        low = dot_nt(land[i], feed_in[...])
-        low_gate = (low[:, :LANES] * masks).astype(bf16)
-        low_up = (low[:, LANES:] * masks).astype(bf16)
-        narrow[i, 0] = low_gate
-        narrow[i, 1] = low_up
+        mask = plane_masks(masks, i, rows)
+        for k in range(2):
+            narrow[i, k] = (dot_nt(land[i], flat(feed_in[k])) * mask).astype(bf16)
 
         @pl.loop(0, share // tile)
         def _(n):
             at = span(n, tile)
-            g = dot_nn(land[i], gate[:, at]) + dot_nn(narrow[i, 0], gate_out[:, at])
-            u = dot_nn(land[i], up[:, at]) + dot_nn(narrow[i, 1], up_out[:, at])
+            g = dot_nn(land[i], gate[:, at]) + dot_nn(narrow[i, 0], flat(feed_out[0, :, :, at]))
+            u = dot_nn(land[i], up[:, at]) + dot_nn(narrow[i, 1], flat(feed_out[1, :, :, at]))
             saved[slot, 0, :, at] = g.astype(bf16)
             saved[slot, 1, :, at] = u.astype(bf16)
             th = jnp.tanh(GELU_SLOPE * (g + GELU_CUBE * g * g * g))
@@ -298,7 +335,7 @@
 
         for c in keep(i):
             c.start()
-        narrow[i, 2] = (dot_nt(hidden[...], down_in[...]) * masks).astype(bf16)
+        narrow[i, 2] = (dot_nt(hidden[...], flat(down_in[...])) * mask).astype(bf16)
         reduce.before(i)
 
         @pl.loop(0, width // tile)
@@ -311,7 +348,13 @@
 
         reduce.after(i)
 
-    reduce.finish(branch)
+    def write(at, branch):
+        scale = lax.rsqrt(jnp.mean(branch * branch, axis=-1, keepdims=True) + epsilon)
+        gain = gains[3:4, :]
+        layer_out[at, :] = (middle[at, :].astype(f32) + branch * scale * gain).astype(bf16)
+        grad_branch[at, :] = norm_grad(branch, gain, cotangent[at, :].astype(f32)).astype(bf16)
+
+    reduce.finish(write)
     gather.finish()
     for i in (2, 3):
         for c in keep(i):
@@ -319,10 +362,11 @@
 
 
 def feed_backward_kernel(
-    own, feed_in, gate_out, up_out, down_in, down_out, columns, narrow,
-    gate_hbm, up_hbm, down_hbm, gate_up,
-    grad_feed, both, t_feed_out, t_down_in, t_down_out,
-    gate, up, down, land, saved, gg, gu, part, odd, from_core, from_x, from_y, diag,
+    own, masks, down_out, narrow, feed_in_hbm, feed_out_hbm, down_in_hbm,
+    gate_hbm, up_hbm, down_hbm, gate_up, feed_all,
+    grad_feed, feed_table, share_sum,
+    both, t_feed_out, t_down_in, t_down_out, share_table, share_in, share_piece,
+    feed_in, feed_out, down_in, gate, up, down, land, saved, gg, gu, part, odd, from_core, from_x, from_y, diag,
     send, recv, load, fetch,
 ):
     rows = own.shape[0]
@@ -331,7 +375,13 @@
     tile = 384
     loads = [
         pltpu.make_async_copy(s, d, load.at[i])
-        for i, (s, d) in enumerate(((down_hbm, down), (gate_hbm, gate), (up_hbm, up)))
+        for i, (s, d) in enumerate(
+            [(down_hbm, down), (gate_hbm, gate), (up_hbm, up)]
+            + feed_table_copies(
+                plane_rank(), share, feed_in_hbm, feed_out_hbm, down_in_hbm, feed_in, feed_out,
+                down_in,
+            )
+        )
     ]
 
     def bring(i):
@@ -340,8 +390,13 @@
     for c in loads:
         c.start()
     bring(0).start()
-    greet(neighbours())
+    place = Places()
+    greet(list(neighbours()) + [place.up(d) for d in range(1, place.planes)])
     copy = sender(send, recv)
+    spread = TableSum(
+        place, copy, PlaneGather.COUNT + PlaneReduce.COUNT, share_table, share_in, share_piece,
+        lambda z: share_sum.at[z], fetch.at[1],
+    )
     gather = PlaneGather(copy, own, land, rows)
     reduce = PlaneReduce(
         copy, part, odd, from_core, from_x, from_y, diag, rows, PlaneGather.COUNT
@@ -358,13 +413,13 @@
     def _(i):
         gather.before(i)
         bring(i).wait()
-        masks = columns[i].astype(f32)
-        back = (dot_nt(land[i], down_out[...]) * masks).astype(bf16)
+        mask = plane_masks(masks, i, rows)
+        back = (dot_nt(land[i], down_out[...]) * mask).astype(bf16)
 
         @pl.loop(0, share // tile)
         def _(n):
             at = span(n, tile)
-            gh = dot_nt(land[i], down[at, :]) + dot_nn(back, down_in[:, at])
+            gh = dot_nt(land[i], down[at, :]) + dot_nn(back, flat(down_in[:, :, at]))
             g = saved[0, :, at].astype(f32)
             u = saved[1, :, at].astype(f32)
             th = jnp.tanh(GELU_SLOPE * (g + GELU_CUBE * g * g * g))
@@ -380,9 +435,8 @@
         def _():
             bring(i + 1).start()
 
-        back_gate = (dot_nt(gg[...], gate_out[...]) * masks).astype(bf16)
-        back_up = (dot_nt(gu[...], up_out[...]) * masks).astype(bf16)
-        both[i] = jnp.concatenate([back_gate, back_up], axis=1)
+        both[i, :, :LANES] = (dot_nt(gg[...], flat(feed_out[0])) * mask).astype(bf16)
+        both[i, :, LANES:] = (dot_nt(gu[...], flat(feed_out[1])) * mask).astype(bf16)
         reduce.before(i)
 
         @pl.loop(0, width // tile)
@@ -391,7 +445,8 @@
             got = (
                 dot_nt(gg[...], gate[at, :])
                 + dot_nt(gu[...], up[at, :])
-                + dot_nn(both[i], feed_in[:, at])
+                + dot_nn(both[i, :, :LANES], flat(feed_in[0, :, :, at]))
+                + dot_nn(both[i, :, LANES:], flat(feed_in[1, :, :, at]))
             ).astype(bf16)
             part[i, :, at] = got[:rows]
             odd[i % 2, :, at] = got[rows:]
@@ -401,11 +456,41 @@
         t_feed_out[1] += dot_tn(narrow[i, 1], gu[...])
         t_down_out[...] += dot_tn(narrow[i, 2], land[i])
 
-    reduce.finish(grad_feed)
+    share_table[: 2 * LANES] = t_feed_out[...].reshape(2 * LANES, share).astype(bf16)
+    share_table[2 * LANES :] = t_down_in[...].astype(bf16)
+    spread.scatter()
     gather.finish()
-
-
-def feed_scratch(rows, width):
+    reload = [pltpu.make_async_copy(feed_all.at[i], land.at[i], fetch.at[2 + i]) for i in range(4)]
+    for c in reload:
+        c.start()
+
+    def tables():
+        spread.gather()
+        for c in reload:
+            c.wait()
+        backs = both[...].reshape(8 * rows, 2 * LANES)
+
+        @pl.loop(0, width // 256)
+        def _(n):
+            at = span(n, 256)
+            got = dot_tn(backs, land[:, :, at].reshape(8 * rows, 256)).astype(bf16)
+            last = t_down_out[:, at].astype(bf16)
+            for a in range(ADAPTERS):
+                first = slice(a * RANK, (a + 1) * RANK)
+                second = slice(LANES + a * RANK, LANES + (a + 1) * RANK)
+                feed_table[a, :RANK, at] = got[first]
+                feed_table[a, RANK : 2 * RANK, at] = got[second]
+                feed_table[a, 2 * RANK :, at] = last[first]
+
+    def write(at, total):
+        grad_feed[at, :] = total.astype(grad_feed.dtype)
+
+    reduce.finish(write, tables)
+    spread.finish()
+
+
+def feed_scratch(rows, width, extra=0):
+    count = PlaneGather.COUNT + PlaneReduce.COUNT + extra
     return [
         pltpu.VMEM((4, rows, width), bf16),
         pltpu.VMEM((2, rows, width), bf16),
@@ -413,28 +498,30 @@
         pltpu.VMEM((rows, width), bf16),
         pltpu.VMEM((rows, width), bf16),
         pltpu.VMEM((rows, width), bf16),
-        pltpu.SemaphoreType.DMA((PlaneGather.COUNT + PlaneReduce.COUNT,)),
-        pltpu.SemaphoreType.DMA((PlaneGather.COUNT + PlaneReduce.COUNT,)),
+        pltpu.SemaphoreType.DMA((count,)),
+        pltpu.SemaphoreType.DMA((count,)),
     ]
 
 
 ANY = pl.BlockSpec(memory_space=pl.ANY)
 
 
-def feed_forward(own, feed_in, gate_out, up_out, down_in, down_out, columns, gate, up, down):
+def feed_forward(own, middle, cotangent, gains, masks, down_out, tables, gate, up, down):
     rows, width = own.shape
     share = gate.shape[1]
     return pl.pallas_call(
         feed_forward_kernel,
         out_shape=(
-            shape((rows, width), f32),
+            shape((rows, width), bf16),
+            shape((rows, width), bf16),
             shape((4, 3, 2 * rows, LANES), bf16),
             shape((4, 2 * rows, width), bf16),
             shape((4, 2, 2 * rows, share), bf16),
         ),
-        in_specs=[VM] * 7 + [ANY] * 3,
-        out_specs=(VM, VM, ANY, ANY),
-        scratch_shapes=[
+        in_specs=[VM] * 6 + [ANY] * 6,
+        out_specs=(VM, VM, VM, ANY, ANY),
+        scratch_shapes=feed_table_scratch(width, share)
+        + [
             pltpu.VMEM(gate.shape, bf16),
             pltpu.VMEM(up.shape, bf16),
             pltpu.VMEM(down.shape, bf16),
@@ -443,31 +530,39 @@
             pltpu.VMEM((2, 2, 2 * rows, share), bf16),
         ]
         + feed_scratch(rows, width)
-        + [pltpu.SemaphoreType.DMA((3,)), pltpu.SemaphoreType.DMA((4,))],
+        + [pltpu.SemaphoreType.DMA((8,)), pltpu.SemaphoreType.DMA((4,))],
         compiler_params=pltpu.CompilerParams(
             collective_id=1, has_side_effects=True, vmem_limit_bytes=62 << 20
         ),
         name="feed_forward",
-    )(own, feed_in, gate_out, up_out, down_in, down_out, columns, gate, up, down)
-
-
-def feed_backward(
-    own, feed_in, gate_out, up_out, down_in, down_out, columns, narrow, gate, up, down, gate_up
-):
+    )(own, middle, cotangent, gains, masks, down_out, *tables, gate, up, down)
+
+
+def feed_backward(own, masks, down_out, narrow, tables, gate, up, down, gate_up, feed_all):
     rows, width = own.shape
     share = gate.shape[1]
+    planes = lax.axis_size("ulysses")
+    piece = 3 * LANES // planes
     return pl.pallas_call(
         feed_backward_kernel,
         out_shape=(
             shape((rows, width), bf16),
-            shape((4, 2 * rows, 2 * LANES), bf16),
-            shape((2, LANES, share), f32),
-            shape((LANES, share), f32),
-            shape((LANES, width), f32),
+            shape((ADAPTERS, 3 * RANK, width), bf16),
+            shape((planes, piece, share), bf16),
         ),
-        in_specs=[VM] * 8 + [ANY] * 4,
-        out_specs=(VM,) * 5,
+        in_specs=[VM] * 4 + [ANY] * 8,
+        out_specs=(VM, VM, ANY),
         scratch_shapes=[
+            pltpu.VMEM((4, 2 * rows, 2 * LANES), bf16),
+            pltpu.VMEM((2, LANES, share), f32),
+            pltpu.VMEM((LANES, share), f32),
+            pltpu.VMEM((LANES, width), f32),
+            pltpu.VMEM((3 * LANES, share), bf16),
+            pltpu.VMEM((planes - 1, piece, share), bf16),
+            pltpu.VMEM((piece, share), bf16),
+        ]
+        + feed_table_scratch(width, share)
+        + [
             pltpu.VMEM(gate.shape, bf16),
             pltpu.VMEM(up.shape, bf16),
             pltpu.VMEM(down.shape, bf16),
@@ -476,18 +571,49 @@
             pltpu.VMEM((2 * rows, share), bf16),
             pltpu.VMEM((2 * rows, share), bf16),
         ]
-        + feed_scratch(rows, width)
-        + [pltpu.SemaphoreType.DMA((3,)), pltpu.SemaphoreType.DMA((1,))],
+        + feed_scratch(rows, width, TableSum.COUNT)
+        + [pltpu.SemaphoreType.DMA((8,)), pltpu.SemaphoreType.DMA((6,))],
         compiler_params=pltpu.CompilerParams(
             collective_id=2, has_side_effects=True, vmem_limit_bytes=62 << 20
         ),
         name="feed_backward",
-    )(
-        own, feed_in, gate_out, up_out, down_in, down_out, columns, narrow, gate, up, down, gate_up
-    )
-
-
-def rms_rows(source, gain, target, rows, add=None, keep=None):
+    )(own, masks, down_out, narrow, *tables, gate, up, down, gate_up, feed_all)
+
+
+def flat(table):
+    return table.reshape(LANES, table.shape[-1])
+
+
+def head_table_copies(
+    b, heads_hbm, query_out_hbm, kv_out_hbm, heads_in, query_out, key_out, value_out
+):
+    lanes = pl.ds(pl.multiple_of(b * 2 * HEAD, 128), 2 * HEAD)
+    lane = pl.ds(pl.multiple_of(b * HEAD, 128), HEAD)
+    return [(heads_hbm.at[:, i], heads_in.at[i]) for i in range(3)] + [
+        (query_out_hbm.at[:, :, lanes], query_out),
+        (kv_out_hbm.at[:, 0, :, lane], key_out),
+        (kv_out_hbm.at[:, 1, :, lane], value_out),
+    ]
+
+
+def head_table_scratch(width):
+    return [
+        pltpu.VMEM((3, ADAPTERS, RANK, width), bf16),
+        pltpu.VMEM((ADAPTERS, RANK, 2 * HEAD), bf16),
+        pltpu.VMEM((ADAPTERS, RANK, HEAD), bf16),
+        pltpu.VMEM((ADAPTERS, RANK, HEAD), bf16),
+    ]
+
+
+def adapter_mask(ids, t, z, planes, rows):
+    sequence = 0 if t * planes * rows < PROMPT else 1 + ((t * planes + z) * rows - PROMPT) // CONT
+    owner = lax.broadcasted_iota(jnp.int32, (1, LANES), 1) // RANK
+    return jnp.where(owner == ids[0, sequence], 1.0, 0.0)
+
+
+def rms_rows(source, gains, which, target, rows, add=None):
+    gain = gains.at[pl.ds(which, 1)]
+
     @pl.loop(0, rows // 32)
     def _(i):
         at = span(i, 32)
@@ -499,11 +625,12 @@
 
 
 def attention_forward_kernel(
-    tokens, attn_in_gain, attn_out_gain, feed_in_gain, heads_in, query_out, key_out, value_out,
-    mix_in, mix_out, columns, own_columns, cosine, sine,
+    tokens, gains, ids, mix_in, mix_out, heads_hbm, query_out_hbm, kv_out_hbm,
     query_hbm, key_hbm, value_hbm, out_hbm, gate_hbm, up_hbm,
-    queries, values_prompt, values_cont, attended, sums, narrow, mixed_out, narrow_mix, attn_out,
-    middle, normed_feed, normed_out, wall_out, out_out, gate_share, up_share,
+    queries, values_prompt, values_cont, attended, sums, narrow, mixed_out, narrow_mix,
+    attn_out_out, middle_out, normed_feed, cosine, sine, masks_out, normed_out, wall_out, out_out, gate_share,
+    up_share,
+    heads_in, query_out, key_out, value_out, masks, masks_got, attn_out, middle,
     normed_all, wall, wo, kvp, kvc, acc, total, mixed, send, recv, local,
 ):
     rows, width = tokens.shape
@@ -545,13 +672,21 @@
         for i, (ref, size, to) in enumerate(heads)
     ]
     own_loads.append(pltpu.make_async_copy(out_hbm, wo.at[out_rows(rank)], local.at[3]))
+    table_loads = [
+        pltpu.make_async_copy(src, dst, local.at[12 + i])
+        for i, (src, dst) in enumerate(
+            head_table_copies(
+                b, heads_hbm, query_out_hbm, kv_out_hbm, heads_in, query_out, key_out, value_out
+            )
+        )
+    ]
     own_rows = [
         pltpu.make_async_copy(
             columns_of(ref, rank, share), out.at[weight_rows(rank)], local.at[4 + i]
         )
         for i, (ref, out) in enumerate(((gate_hbm, gate_share), (up_hbm, up_share)))
     ]
-    for cp in own_loads:
+    for cp in own_loads + table_loads:
         cp.start()
 
     barrier = pltpu.get_barrier_semaphore()
@@ -560,7 +695,11 @@
     ):
         pl.semaphore_signal(barrier, inc=1, device_id=peer, device_id_type=MESH)
 
-    rms_rows(tokens, attn_in_gain, normed_all.at[block(b)], rows)
+    rms_rows(tokens, gains, 0, normed_all.at[block(b)], rows)
+    masks[...] = jnp.zeros_like(masks)
+    for t in range(4):
+        masks[t : t + 1, :] = adapter_mask(ids, t, z, planes, rows)
+    masks_out[0] = masks[...]
     pl.semaphore_wait(barrier, 6 + planes)
 
     stage = []
@@ -589,6 +728,8 @@
     for cp in stage[3:]:
         cp.start()
     token_copies[1].start()
+    mask_copy = copy(34, masks, masks_got, px)
+    mask_copy.start()
     for cp in own_loads[:3]:
         cp.wait()
     across[0].start()
@@ -603,6 +744,22 @@
     across[3].start()
     token_copies[0].wait_recv()
     token_copies[2].start()
+    lane = lax.broadcasted_iota(jnp.int32, (rows, HEAD // 2), 1).astype(f32)
+    inverse = jnp.exp(lane * (-2.0 / HEAD * math.log(rope_base)))
+
+    @pl.loop(0, 4)
+    def _(t):
+        at = block(t)
+        token = (t * planes + z) * rows + lax.broadcasted_iota(jnp.int32, (rows, HEAD // 2), 0)
+        position = jnp.where(token >= PROMPT, PROMPT + (token - PROMPT) % CONT, token)
+        angle = position.astype(f32) * inverse
+        cosine[at, :] = jnp.cos(angle)
+        sine[at, :] = jnp.sin(angle)
+
+    for cp in table_loads:
+        cp.wait()
+    mask_copy.wait()
+    masks_out[1] = masks_got[...]
 
     half = part // 2
     rx, ry, rxy = (1 - x) * 4 + b, x * 4 + b_y, (1 - x) * 4 + b_y
@@ -626,10 +783,61 @@
     ]
     wo_first = [copy(i, ref, ref, peer) for i, ref, peer in wo_first]
     wo_next = [copy(i, ref, ref, peer) for i, ref, peer in wo_next]
+    swaps = [
+        copy(26 + i, columns_of(ref, x * 4 + b_c, share), out.at[weight_rows(rank)], pc)
+        for i, (ref, out) in enumerate(((gate_hbm, gate_share), (up_hbm, up_share)))
+    ]
+    chips = (
+        ((px, rx), (pxc, (1 - x) * 4 + b_c)),
+        ((py, ry), (pyc, x * 4 + b_yc)),
+        ((pxy, rxy), (pxyc, (1 - x) * 4 + b_yc)),
+    )
+    got_ranks = (
+        (1 - x) * 4 + y * 2 + z % 2, x * 4 + (1 - y) * 2 + z % 2, (1 - x) * 4 + (1 - y) * 2 + z % 2,
+    )
+    direct, relay, whole = {}, {}, []
+    for n, targets in enumerate(chips):
+        for i, (ref, out) in enumerate(((gate_hbm, gate_share), (up_hbm, up_share))):
+            kind = 2 * n + i
+            if kind in (0, 2):
+                whole += [
+                    copy(63 + kind + j, columns_of(ref, pr, share), out.at[weight_rows(rank)], peer)
+                    for j, (peer, pr) in enumerate(targets)
+                ]
+                continue
+            direct[kind] = [
+                pltpu.make_async_remote_copy(
+                    columns_of(ref, pr, share),
+                    out.at[weight_rows(rank)],
+                    send.at[51 + 2 * kind + j],
+                    recv.at[51 + kind],
+                    device_id=peer,
+                    device_id_type=MESH,
+                )
+                for j, (peer, pr) in enumerate(targets)
+            ]
+            got = out.at[weight_rows(got_ranks[n])]
+            relay[kind] = copy(28 + kind, got, got, pz)
+
+    def send_direct(kinds):
+        @pl.when(c == z % 2)
+        def _():
+            for kind in kinds:
+                for cp in direct[kind]:
+                    cp.start()
+
+    def pass_along(kinds):
+        for kind in kinds:
+            direct[kind][0].wait_recv()
+            relay[kind].start()
+
     own_loads[3].wait()
     for cp in across:
         cp.wait_recv()
     for cp in wo_first:
+        cp.start()
+    send_direct((4, 5))
+    for cp in swaps + own_rows:
         cp.start()
     token_copies[1].wait_recv()
     token_copies[2].wait_recv()
@@ -650,12 +858,12 @@
     @pl.loop(0, 4)
     def _(t):
         at = block(t)
-        masks = columns[at, :].astype(f32)
+        mask = masks[pl.ds(t, 1), :]
         cos, sin = cosine[at, :], sine[at, :]
         a = normed_all[at, :]
         for i in range(3):
             lanes = slice(i * LANES, (i + 1) * LANES)
-            narrow[at, lanes] = (dot_nt(a, heads_in[lanes, :]) * masks).astype(bf16)
+            narrow[at, lanes] = (dot_nt(a, flat(heads_in[i])) * mask).astype(bf16)
 
         def turned(pre, scale):
             first, second = pre[:, :half_head], pre[:, half_head:]
@@ -666,14 +874,18 @@
 
         for h in range(2):
             lanes = slice(h * HEAD, (h + 1) * HEAD)
-            pre = dot_nn(a, wall[:, lanes]) + dot_nn(narrow[at, :LANES], query_out[:, lanes])
+            pre = dot_nn(a, wall[:, lanes]) + dot_nn(
+                narrow[at, :LANES], flat(query_out[:, :, lanes])
+            )
             queries[t, h * rows : (h + 1) * rows, :] = turned(pre, HEAD ** (-0.5))
         pre = dot_nn(a, wall[:, 2 * HEAD : 3 * HEAD]) + dot_nn(
-            narrow[at, LANES : 2 * LANES], key_out[...]
+            narrow[at, LANES : 2 * LANES], flat(key_out[...])
         )
         key = turned(pre, 1.0)
         value = (
-            dot_nn(a, wall[:, 3 * HEAD :]) + dot_nn(narrow[at, 2 * LANES :], value_out[...])
+            dot_nn(a, wall[:, 3 * HEAD :]) + dot_nn(
+                narrow[at, 2 * LANES :], flat(value_out[...])
+            )
         ).astype(bf16)
 
         @pl.when(t < 2)
@@ -701,6 +913,7 @@
     pass_on(1, 0)
     pass_on(-1, 0)
 
+    send_direct((1, 3))
     acc[...] = jnp.zeros_like(acc)
     total[...] = jnp.zeros_like(total)
     row = lax.broadcasted_iota(jnp.int32, (2 * rows, rows), 0) % rows
@@ -726,55 +939,22 @@
         step(t, kvp[z, 0, 0], kvp[z, 1, 0], False)
         step(t, kvp[z, 0, 1], kvp[z, 1, 1], False)
 
+    for cp in whole:
+        cp.start()
     wo_first[0].wait_recv()
     wo_next[0].start()
     wo_first[1].wait_recv()
     wo_next[1].start()
-
-    swaps = []
-    at = 26
-    for peer, pr in (
-        (px, rx), (py, ry), (pxc, (1 - x) * 4 + b_c), (pyc, x * 4 + b_yc), (pc, x * 4 + b_c),
-    ):
-        for ref, out in ((gate_hbm, gate_share), (up_hbm, up_share)):
-            swaps.append(
-                copy(at, columns_of(ref, pr, share), out.at[weight_rows(rank)], peer)
-            )
-            at += 1
-    far = []
-    for i, (ref, out) in enumerate(((gate_hbm, gate_share), (up_hbm, up_share))):
-        for j, (peer, pr) in enumerate(((pxy, rxy), (pxyc, (1 - x) * 4 + b_yc))):
-            far.append(
-                pltpu.make_async_remote_copy(
-                    columns_of(ref, pr, share),
-                    out.at[weight_rows(rank)],
-                    send.at[36 + 2 * j + i],
-                    recv.at[36 + i],
-                    device_id=peer,
-                    device_id_type=MESH,
-                )
-            )
-    got_rank = (1 - x) * 4 + (1 - y) * 2 + z % 2
-    relay = [
-        copy(40 + i, out.at[weight_rows(got_rank)], out.at[weight_rows(got_rank)], pz)
-        for i, out in enumerate((gate_share, up_share))
-    ]
-
-    @pl.when(c == z % 2)
-    def _():
-        for cp in far:
-            cp.start()
-
-    for cp in swaps:
-        cp.start()
-    for cp in own_rows:
-        cp.start()
 
     @pl.loop(0, 2 * (planes - 1))
     def _(i):
         d = i // 2 + 1
         direction = 1 - 2 * (i % 2)
         zz = z - d * direction
+
+        @pl.when(i == 2)
+        def _():
+            pass_along((4, 5))
 
         @pl.when((zz >= 0) & (zz < planes))
         def _():
@@ -834,6 +1014,7 @@
     for cp in mixes:
         cp.start()
     mixed[:, lanes] = attended[b]
+    pass_along((1, 3))
     wo_first[2].wait_recv()
     wo_next[2].start()
     wo_first[3].wait_recv()
@@ -848,29 +1029,28 @@
         cp.wait_recv()
     outs[2].start()
     outs[5].start()
-    narrow_mix[...] = (dot_nt(mixed[...], mix_in[...]) * own_columns[...].astype(f32)).astype(bf16)
+    narrow_mix[...] = (dot_nt(mixed[...], mix_in[...]) * masks[pl.ds(b, 1), :]).astype(bf16)
 
     @pl.loop(0, width // 384)
     def _(n):
         at = span(n, 384)
         attn_out[:, at] = dot_nn(mixed[...], wo[:, at]) + dot_nn(narrow_mix[...], mix_out[:, at])
 
-    rms_rows(attn_out, attn_out_gain, middle, rows, add=tokens)
-    rms_rows(middle, feed_in_gain, normed_feed, rows)
-
-    for cp in far[:1] + far[2:3]:
-        cp.wait_recv()
-    for cp in relay:
-        cp.start()
-    for cp in swaps:
+    rms_rows(attn_out, gains, 1, middle, rows, add=tokens)
+    rms_rows(middle, gains, 2, normed_feed, rows)
+    attn_out_out[...] = attn_out[...].astype(bf16)
+    middle_out[...] = middle[...].astype(bf16)
+
+    for cp in swaps + whole:
         cp.wait()
-    for cp in relay:
+    for cp in relay.values():
         cp.wait()
 
     @pl.when(c == z % 2)
     def _():
-        for cp in far:
-            cp.wait_send()
+        for pair in direct.values():
+            for cp in pair:
+                cp.wait_send()
 
     for cp in own_rows + outs:
         cp.wait()
@@ -893,9 +1073,7 @@
             ).wait_send()
 
 
-def attention_forward(
-    tokens, gains, tables, columns, own_columns, cosine, sine, weights, share
-):
+def attention_forward(tokens, gains, ids, mix_in, mix_out, tables, weights, share):
     rows, width = tokens.shape
     planes = lax.axis_size("ulysses")
     return pl.pallas_call(
@@ -909,18 +1087,26 @@
             shape((4 * rows, 3 * LANES), bf16),
             shape((rows, 8 * HEAD), bf16),
             shape((rows, LANES), bf16),
-            shape((rows, width), f32),
-            shape((rows, width), f32),
             shape((rows, width), bf16),
+            shape((rows, width), bf16),
+            shape((rows, width), bf16),
+            shape((4 * rows, HEAD // 2), f32),
+            shape((4 * rows, HEAD // 2), f32),
+            shape((2, 16, LANES), f32),
             shape((4 * rows, width), bf16),
             shape((width, 4 * HEAD), bf16),
             shape((8 * HEAD, width), bf16),
             shape((width, share), bf16),
             shape((width, share), bf16),
         ),
-        in_specs=[VM] * 14 + [ANY] * 6,
-        out_specs=(VM, ANY, ANY, VM, VM, VM, ANY, VM, VM, VM, VM, ANY, ANY, ANY, ANY, ANY),
-        scratch_shapes=[
+        in_specs=[VM, VM, pl.BlockSpec(memory_space=pltpu.SMEM), VM, VM] + [ANY] * 9,
+        out_specs=(VM, ANY, ANY, VM, VM, VM, ANY) + (VM,) * 7 + (ANY,) * 5,
+        scratch_shapes=head_table_scratch(width)
+        + [
+            pltpu.VMEM((16, LANES), f32),
+            pltpu.VMEM((16, LANES), f32),
+            pltpu.VMEM((rows, width), f32),
+            pltpu.VMEM((rows, width), f32),
             pltpu.VMEM((4 * rows, width), bf16),
             pltpu.VMEM((width, 4 * HEAD), bf16),
             pltpu.VMEM((8 * HEAD, width), bf16),
@@ -929,15 +1115,15 @@
             pltpu.VMEM((4, 2 * rows, HEAD), f32),
             pltpu.VMEM((4, 2 * rows, 128), f32),
             pltpu.VMEM((rows, 8 * HEAD), bf16),
-            pltpu.SemaphoreType.DMA((51,)),
-            pltpu.SemaphoreType.DMA((51,)),
-            pltpu.SemaphoreType.DMA((12,)),
+            pltpu.SemaphoreType.DMA((67,)),
+            pltpu.SemaphoreType.DMA((67,)),
+            pltpu.SemaphoreType.DMA((18,)),
         ],
         compiler_params=pltpu.CompilerParams(
             collective_id=3, has_side_effects=True, vmem_limit_bytes=62 << 20
         ),
         name="attention_forward",
-    )(tokens, *gains, *tables, columns, own_columns, cosine, sine, *weights)
+    )(tokens, gains, ids, mix_in, mix_out, *tables, *weights)
 
 
 class Places:
@@ -967,48 +1153,20 @@
         return (self.dp, self.b, self.along(d))
 
 
-class TableSpread:
-    COUNT = 16
-
-    def __init__(self, place, copy, first, source, arrived, piece, gathered, local):
+class TableSum:
+    COUNT = 6
+
+    def __init__(self, place, copy, first, source, arrived, piece, target, local):
         self.place, self.source, self.arrived, self.piece = place, source, arrived, piece
-        self.gathered = gathered
         n = place.planes
         self.q = piece.shape[0]
-        half = n // 2
-
-        def region(rank, h):
-            return gathered.at[rank, pl.ds(h * half, half)]
-
         self.out = [
             copy(first + d - 1, source.at[span(place.along(d), self.q)], arrived.at[d - 1], place.up(d))
             for d in range(1, n)
         ]
-        self.own = pltpu.make_async_copy(piece, gathered.at[place.rank, place.z], local)
+        self.own = pltpu.make_async_copy(piece, target(place.z), local)
         self.back = [
-            copy(first + 2 + d, piece, gathered.at[place.rank, place.z], place.up(d))
-            for d in range(1, n)
-        ]
-        own, rx, rxy, ry = place.near
-        at = first + 6
-
-        def same(i, ref, peer):
-            return copy(at + i, ref, ref, peer)
-
-        px, py, pc = place.px, place.py, place.pc
-        self.first = [
-            same(0, region(own, 0), px),
-            same(1, region(own, 1), py),
-            same(2, region(own, 1), px),
-            same(3, region(own, 0), py),
-            same(4, gathered.at[own], pc),
-        ]
-        self.next = [
-            same(5, region(rx, 0), py),
-            same(6, region(ry, 1), px),
-            same(7, gathered.at[rx], pc),
-            same(8, gathered.at[ry], pc),
-            same(9, gathered.at[rxy], pc),
+            copy(first + 2 + d, piece, target(place.z), place.up(d)) for d in range(1, n)
         ]
 
     def scatter(self):
@@ -1026,22 +1184,58 @@
         for c in self.back:
             c.start()
 
-    def plane(self):
+    def ready(self):
         for c in self.back:
             c.wait_recv()
         self.own.wait()
+
+    def finish(self):
+        self.ready()
+        self.close()
+
+    def close(self):
+        for c in self.out + self.back:
+            c.wait_send()
+
+
+class PlaneSpread:
+    COUNT = 10
+
+    def __init__(self, place, copy, first, own, gathered):
+        half = place.planes // 2
+        parts = (pl.ds(0, half), pl.ds(half, half))
+        mine, rx, rxy, ry = place.near
+        px, py, pc = place.px, place.py, place.pc
+
+        def same(i, ref, peer):
+            return copy(first + i, ref, ref, peer)
+
+        def send(i, part, peer):
+            return copy(first + i, own.at[part], gathered.at[mine, part], peer)
+
+        self.first = [
+            send(0, parts[0], px),
+            send(1, parts[1], py),
+            send(2, parts[1], px),
+            send(3, parts[0], py),
+            copy(first + 4, own, gathered.at[mine], pc),
+        ]
+        self.next = [
+            same(5, gathered.at[rx, parts[0]], py),
+            same(6, gathered.at[ry, parts[1]], px),
+            same(7, gathered.at[rx], pc),
+            same(8, gathered.at[ry], pc),
+            same(9, gathered.at[rxy], pc),
+        ]
+
+    def plane(self):
         for c in self.first:
             c.start()
 
     def forward(self):
-        self.first[0].wait_recv()
-        self.next[0].start()
-        self.first[1].wait_recv()
-        self.next[1].start()
-        self.first[2].wait_recv()
-        self.next[2].start()
-        self.first[3].wait_recv()
-        self.next[3].start()
+        for i in range(4):
+            self.first[i].wait_recv()
+            self.next[i].start()
 
     def corner(self):
         self.next[0].wait_recv()
@@ -1052,8 +1246,29 @@
         self.first[4].wait_recv()
         for c in self.next[2:]:
             c.wait_recv()
-        for c in self.out + self.back + self.first + self.next:
+        for c in self.first + self.next:
             c.wait_send()
+
+
+class TableSpread:
+    COUNT = TableSum.COUNT + PlaneSpread.COUNT
+
+    def __init__(self, place, copy, first, source, arrived, piece, gathered, local):
+        own = gathered.at[place.rank]
+        self.sum = TableSum(
+            place, copy, first, source, arrived, piece, lambda z: gathered.at[place.rank, z], local
+        )
+        self.spread = PlaneSpread(place, copy, first + TableSum.COUNT, own, gathered)
+        self.scatter, self.gather = self.sum.scatter, self.sum.gather
+        self.forward, self.corner = self.spread.forward, self.spread.corner
+
+    def plane(self):
+        self.sum.ready()
+        self.spread.plane()
+
+    def finish(self):
+        self.sum.close()
+        self.spread.finish()
 
 
 class TableReduce:
@@ -1124,28 +1339,42 @@
 
 
 def attention_backward_kernel(
-    grad_mixed, queries, kvp, kvc, attended, sums, narrow, heads_in, query_out, key_out, value_out,
-    columns, cosine, sine, mix_table,
-    normed_hbm, wall_hbm, feed_table, feed_share,
-    grad_normed, g_feed_table, g_feed_share, g_head_table, g_head_share,
-    normed_all, wall, g, delta, inv, dq, kv_own, kv_far, kv_send, kv_got, grad_pre, back, part,
+    middle, attn_out, cotangent, gains, masks, mixed, narrow_mix, mix_in, mix_out,
+    queries, kvp, kvc, attended, sums, narrow, cosine, sine,
+    grad_feed_hbm, tokens_hbm, heads_hbm, query_out_hbm, kv_out_hbm, out_hbm, normed_hbm, wall_hbm, feed_hbm, feed_share,
+    tokens_grad, g_feed_table, g_feed_share, g_head_table, g_head_share,
+    heads_in, query_out, key_out, value_out, wo, wall, grad_attn, grad_mixed,
+    g, delta, inv, dq, kv_own, kv_far, kv_send, kv_got, grad_pre, back,
     from_core, from_y,
-    a_part, a_core, a_x, a_y, a_diag, a_total, a_in, a_piece,
-    s_in, s_piece,
+    feed_table, a_part, a_core, a_x, a_y, a_diag, a_total, a_in, a_piece,
     h_table, h_part, h_core, h_x, h_y, h_diag, h_total, h_in, h_piece,
     o_table, o_got, o_total, o_in, o_piece,
     send, recv, local,
 ):
-    rows, width = grad_normed.shape
+    rows, width = tokens_grad.shape
     place = Places()
     b, z, planes = place.b, place.z, place.planes
     copy = sender(send, recv)
+    normed_all = wo.at[pl.ds(0, 4 * rows)]
+    part = [wo.at[pl.ds((4 + i) * rows, rows)] for i in range(4)]
+    own_share = pltpu.make_async_copy(feed_share, g_feed_share.at[place.rank], local.at[0])
     loads = [
-        pltpu.make_async_copy(normed_hbm, normed_all, local.at[0]),
-        pltpu.make_async_copy(wall_hbm, wall, local.at[1]),
+        pltpu.make_async_copy(src, dst, local.at[14 + i])
+        for i, (src, dst) in enumerate(
+            [(out_hbm, wo)]
+            + head_table_copies(
+                b, heads_hbm, query_out_hbm, kv_out_hbm, heads_in, query_out, key_out, value_out
+            )
+            + [(wall_hbm, wall), (feed_hbm, feed_table.at[:, pl.ds(0, 3 * RANK)])]
+        )
     ]
+    grad_feed = from_y
+    bring_feed = pltpu.make_async_copy(grad_feed_hbm, grad_feed, local.at[24])
+    bring_feed.start()
+    late = pltpu.make_async_copy(normed_hbm, normed_all, local.at[1])
     for c in loads:
         c.start()
+    own_share.start()
     barrier = pltpu.get_barrier_semaphore()
     peers = list(place.plane) + [place.up(d) for d in range(1, planes)]
     for peer in peers:
@@ -1166,8 +1395,6 @@
                     peer,
                 )
             )
-    for c in swaps:
-        c.start()
     at = 12
     feed_reduce = TableReduce(
         place, copy, at, feed_table, a_part, a_core, a_x, a_y, a_diag, a_total,
@@ -1176,10 +1403,8 @@
     at += TableReduce.COUNT
     feed_spread = TableSpread(place, copy, at, a_total, a_in, a_piece, g_feed_table, local.at[6])
     at += TableSpread.COUNT
-    share_spread = TableSpread(
-        place, copy, at, feed_share, s_in, s_piece, g_feed_share, local.at[7]
-    )
-    at += TableSpread.COUNT
+    share_spread = PlaneSpread(place, copy, at, feed_share, g_feed_share)
+    at += PlaneSpread.COUNT
     head_reduce = TableReduce(
         place, copy, at, h_table, h_part, h_core, h_x, h_y, h_diag, h_total,
         lambda i: local.at[8 + i],
@@ -1194,11 +1419,58 @@
         at, o_table.at[span(1 - place.x, lanes_half)], o_got, place.px
     )
 
-    share_spread.scatter()
+    share_spread.plane()
+
+    bring_feed.wait()
+
+    @pl.loop(0, rows // 32)
+    def _(i):
+        at = span(i, 32)
+        grad = cotangent[at, :].astype(f32) + norm_grad(
+            middle[at, :].astype(f32), gains[2:3, :], grad_feed[at, :].astype(f32)
+        )
+        tokens_grad[at, :] = grad
+        grad_attn[at, :] = norm_grad(attn_out[at, :].astype(f32), gains[1:2, :], grad).astype(bf16)
+
+    back_mix = (dot_nt(grad_attn[...], mix_out[...]) * masks[0, pl.ds(b, 1), :]).astype(bf16)
+    loads[0].wait()
+    for j, pb in enumerate((place.b_y, place.b_yc, place.b_c, b)):
+
+        @pl.loop(0, 2)
+        def _(h):
+            at = span(pb * 2 + h, HEAD)
+            grad_mixed[:, at] = (
+                dot_nt(grad_attn[...], wo[at, :]) + dot_nn(back_mix, mix_in[:, at])
+            ).astype(bf16)
+
+        if j < 3:
+            for c in swaps[2 * j : 2 * j + 2]:
+                c.start()
+    late.start()
+    for c in loads[1:]:
+        c.wait()
+    for n in range(8):
+        lanes = slice(n * HEAD, (n + 1) * HEAD)
+        got = dot_tn(back_mix, mixed[:, lanes]).astype(bf16)
+        for a in range(ADAPTERS):
+            h_table[a, 3 * RANK :, lanes] = got[a * RANK : (a + 1) * RANK]
+    h_table[:, 3 * RANK :, 8 * HEAD :] = jnp.zeros((ADAPTERS, RANK, width - 8 * HEAD), bf16)
+
+    @pl.loop(0, width // 256)
+    def _(n):
+        at = span(n, 256)
+        got = dot_tn(narrow_mix[...], grad_attn[:, at]).astype(bf16)
+        for a in range(ADAPTERS):
+            feed_table[a, 3 * RANK :, at] = got[a * RANK : (a + 1) * RANK]
+
+    tokens = grad_attn
+    bring_tokens = pltpu.make_async_copy(tokens_hbm, tokens, local.at[23])
+    bring_tokens.start()
     feed_reduce.begin()
     for h in range(2):
         lanes = pl.ds(pl.multiple_of(b * 2 * HEAD + h * HEAD, 128), HEAD)
         g[b, h * rows : (h + 1) * rows, :] = grad_mixed[:, lanes]
+    share_spread.forward()
     for c in swaps:
         c.wait()
 
@@ -1236,9 +1508,6 @@
     def kv_copy(d):
         return copy(6 + d - 1, kv_send.at[d - 1], kv_got.at[d - 1], place.up(d))
 
-    for d in range(1, planes):
-        pass
-
     @pl.loop(1, planes)
     def _(d):
         zz = (z + d) % planes
@@ -1263,10 +1532,9 @@
                 kv_copy(k).start()
                 if k == 1:
                     feed_reduce.merge()
-                    share_spread.gather()
+                    share_spread.corner()
                 if k == 2:
                     feed_reduce.corner()
-                    share_spread.plane()
 
     feed_reduce.finish()
     feed_spread.scatter()
@@ -1280,8 +1548,7 @@
         step(t, kvp[z, 0, 0], kvp[z, 1, 0], kv_own, 0, False)
         step(t, kvp[z, 0, 1], kvp[z, 1, 1], kv_own, 1, False)
 
-    for c in loads:
-        c.wait()
+    late.wait()
     feed_spread.gather()
     for d in range(1, planes):
         kv_copy(d).wait_recv()
@@ -1292,7 +1559,7 @@
     def _(t):
         at = span(t, rows)
         cos, sin = cosine[at, :], sine[at, :]
-        masks = columns[at, :].astype(f32)
+        mask = masks[0, pl.ds(t, 1), :]
 
         def turned(pre, scale):
             first, second = pre[:, :half_head], pre[:, half_head:]
@@ -1315,10 +1582,9 @@
             )
         ):
             back[at, i * LANES : (i + 1) * LANES] = (
-                dot_nt(grad_pre[at, lanes], table[...]) * masks
+                dot_nt(grad_pre[at, lanes], flat(table[...])) * mask
             ).astype(bf16)
 
-    share_spread.forward()
     for i, lanes in enumerate(
         (slice(0, 2 * HEAD), slice(2 * HEAD, 3 * HEAD), slice(3 * HEAD, 4 * HEAD))
     ):
@@ -1326,11 +1592,10 @@
             narrow[:, i * LANES : (i + 1) * LANES], grad_pre[:, lanes]
         ).astype(bf16)
     out_swap.start()
-    h_table[:, 3 * RANK :, :] = mix_table[...]
-
-    @pl.loop(0, width // 384)
+
+    @pl.loop(0, width // 256)
     def _(n):
-        at = span(n, 384)
+        at = span(n, 256)
         got = dot_tn(back[...], normed_all[:, at]).astype(bf16)
         for i in range(3):
             for a in range(ADAPTERS):
@@ -1343,22 +1608,21 @@
     def project(slot, target):
         at_rows = span(target, rows)
 
-        @pl.loop(0, width // 384)
+        @pl.loop(0, width // 256)
         def _(n):
-            at = span(n, 384)
-            part[slot, :, at] = (
+            at = span(n, 256)
+            part[slot][:, at] = (
                 dot_nt(grad_pre[at_rows, :], wall[at, :])
-                + dot_nn(back[at_rows, :], heads_in[:, at])
+                + dot_nn(back[at_rows, :], heads_in[:, :, :, at].reshape(3 * LANES, 256))
             ).astype(bf16)
 
-    to_core = [copy(9 + i, part.at[i], from_core.at[i], place.pc) for i in range(2)]
-    to_y = copy(11, part.at[2], from_y, place.py)
+    to_core = [copy(9 + i, part[i], from_core.at[i], place.pc) for i in range(2)]
+    to_y = copy(11, part[2], from_y, place.py)
     project(0, place.b_yc)
     to_core[0].start()
-    share_spread.corner()
     project(2, place.b_y)
     to_core[0].wait_recv()
-    add_into(part.at[2], from_core.at[0], rows)
+    add_into(part[2], from_core.at[0], rows)
     to_y.start()
     head_reduce.merge()
     feed_spread.forward()
@@ -1387,19 +1651,22 @@
     out_spread.corner()
     head_spread.forward()
     to_y.wait_recv()
+    bring_tokens.wait()
 
     @pl.loop(0, rows // 32)
     def _(i):
         at = span(i, 32)
-        grad_normed[at, :] = (
-            part[3, at, :].astype(f32)
+        grad = (
+            part[3][at, :].astype(f32)
             + from_core[1, at, :].astype(f32)
             + from_y[at, :].astype(f32)
-        ).astype(grad_normed.dtype)
+        )
+        tokens_grad[at, :] += norm_grad(tokens[at, :].astype(f32), gains[0:1, :], grad)
 
     head_spread.corner()
     for spread in (share_spread, feed_spread, out_spread, head_spread):
         spread.finish()
+    own_share.wait()
     out_swap.wait_send()
     to_y.wait_send()
     for c in to_core:
@@ -1408,22 +1675,18 @@
         kv_copy(d).wait_send()
 
 
-def attention_backward(
-    grad_mixed, kept, tables, columns, cosine, sine, mix_table, normed_all, wall, feed_table,
-    feed_share,
-):
-    rows = grad_mixed.shape[0]
-    width = wall.shape[0]
+def attention_backward(rows_in, kept, grad_feed, tokens, tables, weights, feed_table, feed_share):
+    rows, width = rows_in[0].shape
     planes = lax.axis_size("ulysses")
-    m = feed_table.shape[1]
-    fs, fw = feed_share.shape
+    m = 4 * RANK
     hm = 4 * RANK
     ow = 4 * HEAD
     om = LANES // 2
-    count = 12 + 2 * TableReduce.COUNT + 4 * TableSpread.COUNT + 1
+    count = 12 + 2 * TableReduce.COUNT + 3 * TableSpread.COUNT + PlaneSpread.COUNT + 1
 
     def reduce_scratch(m):
         return [
+            pltpu.VMEM((ADAPTERS, m, width), bf16),
             pltpu.VMEM((4, m, width), bf16),
             pltpu.VMEM((4, m, width), bf16),
             pltpu.VMEM((m, width), bf16),
@@ -1443,15 +1706,18 @@
         out_shape=(
             shape((rows, width), f32),
             shape((8, planes, m // planes, width), bf16),
-            shape((8, planes, fs // planes, fw), bf16),
+            shape((8,) + feed_share.shape, bf16),
             shape((8, planes, hm // planes, width), bf16),
             shape((8, planes, om // planes, ow), bf16),
         ),
-        in_specs=[VM] * 15 + [ANY] * 3 + [VM],
+        in_specs=[VM] * 17 + [ANY] * 10,
         out_specs=(VM, ANY, ANY, ANY, ANY),
-        scratch_shapes=[
-            pltpu.VMEM((4 * rows, width), bf16),
+        scratch_shapes=head_table_scratch(width)
+        + [
+            pltpu.VMEM((8 * HEAD, width), bf16),
             pltpu.VMEM((width, 4 * HEAD), bf16),
+            pltpu.VMEM((rows, width), bf16),
+            pltpu.VMEM((rows, 8 * HEAD), bf16),
             pltpu.VMEM((4, 2 * rows, HEAD), bf16),
             pltpu.VMEM((4, 8, 2 * rows), f32),
             pltpu.VMEM((4, 8, 2 * rows), f32),
@@ -1462,14 +1728,11 @@
             pltpu.VMEM((planes - 1, 2, 2, rows, HEAD), bf16),
             pltpu.VMEM((4 * rows, 4 * HEAD), bf16),
             pltpu.VMEM((4 * rows, 3 * LANES), bf16),
-            pltpu.VMEM((4, rows, width), bf16),
             pltpu.VMEM((2, rows, width), bf16),
             pltpu.VMEM((rows, width), bf16),
         ]
         + reduce_scratch(m)
         + spread_scratch(m, width)
-        + spread_scratch(fs, fw)
-        + [pltpu.VMEM((ADAPTERS, hm, width), bf16)]
         + reduce_scratch(hm)
         + spread_scratch(hm, width)
         + [
@@ -1481,20 +1744,13 @@
         + [
             pltpu.SemaphoreType.DMA((count,)),
             pltpu.SemaphoreType.DMA((count,)),
-            pltpu.SemaphoreType.DMA((14,)),
+            pltpu.SemaphoreType.DMA((25,)),
         ],
         compiler_params=pltpu.CompilerParams(
-            collective_id=4, has_side_effects=True, vmem_limit_bytes=62 << 20
+            collective_id=4, has_side_effects=True, vmem_limit_bytes=63 << 20
         ),
         name="attention_backward",
-    )(
-        grad_mixed, *kept, *tables, columns, cosine, sine, mix_table, normed_all, wall, feed_table,
-        feed_share,
-    )
-
-
-def take_columns(table, index, width):
-    return lax.dynamic_slice_in_dim(table, index * width, width, axis=1)
+    )(*rows_in, *kept, grad_feed, tokens, *tables, *weights, feed_table, feed_share)
 
 
 def shards(
@@ -1522,13 +1778,10 @@
     adapter_ids,
     cotangent,
 ):
-    rows, width = tokens.shape
+    width = tokens.shape[1]
     blk_n = lax.axis_size("blk")
-    z_n = lax.axis_size("ulysses")
     dp_n = lax.axis_size("dp")
-    b = lax.axis_index("blk")
-    z = lax.axis_index("ulysses")
-    rank = lax.axis_index("dp") % 2 * blk_n + b
+    rank = lax.axis_index("dp") % 2 * blk_n + lax.axis_index("blk")
     ff = gate_weight.shape[1]
     share = ff // (2 * blk_n)
     weights = (
@@ -1545,107 +1798,36 @@
             for weight in weights
         )
     down_rows = weights[6]
-
-    block_first = (jnp.arange(blk_n, dtype=jnp.int32) * z_n + z) * rows
-    sequence = jnp.where(block_first >= PROMPT, 1 + (block_first - PROMPT) // CONT, 0)
-    all_ids = lax.all_gather(adapter_ids.astype(f32), "dp", axis=0, tiled=True).astype(jnp.int32)
-    seq_ids = jnp.arange(CONTS + 1, dtype=jnp.int32)
-    block_ids = jnp.sum(
-        jnp.where(sequence[None, :, None] == seq_ids[None, None, :], all_ids[:, None, :], 0), axis=2
-    )
-    owner = jnp.arange(LANES, dtype=jnp.int32) // RANK
-    block_masks = (block_ids[:, :, None] == owner).astype(f32)
-    group_masks = lax.dynamic_index_in_dim(block_masks, lax.axis_index("dp"), 0, keepdims=False)
-    own_mask = lax.dynamic_index_in_dim(group_masks, b, 0, keepdims=True)[0]
-    group_columns = jnp.repeat(group_masks, rows, axis=0).astype(bf16)
-
-    heads_in = jnp.transpose(adapt_heads_in, (1, 0, 2, 3)).reshape(3, LANES, width)
-    query_out = take_columns(adapt_query_out.reshape(LANES, -1), b, 2 * HEAD)
-    kv_out = jnp.transpose(adapter_key_value_second, (1, 0, 2, 3)).reshape(2, LANES, -1)
-    key_out = take_columns(kv_out[0], b, HEAD)
-    value_out = take_columns(kv_out[1], b, HEAD)
-    mix_in = adapt_mix_in.reshape(LANES, -1)
-    mix_out = adapt_mix_out.reshape(LANES, -1)
-    feed_in = jnp.transpose(adapt_feed_in, (1, 0, 2, 3)).reshape(2, LANES, width)
-    feed_out = jnp.transpose(adapt_feed_out, (1, 0, 2, 3)).reshape(2, LANES, ff)
-    gate_out = take_columns(feed_out[0], rank, share)
-    up_out = take_columns(feed_out[1], rank, share)
-    down_in = take_columns(adapt_down_in.reshape(LANES, ff), rank, share)
-    down_out = adapt_down_out.reshape(LANES, width)
-
-    token_index = (block_first[:, None] + jnp.arange(rows, dtype=jnp.int32)).reshape(-1)
-    positions = jnp.where(token_index >= PROMPT, PROMPT + (token_index - PROMPT) % CONT, token_index)
-    half = HEAD // 2
-    inverse = rope_base ** (-2.0 * jnp.arange(half, dtype=f32) / HEAD)
-    angles = positions.astype(f32)[:, None] * inverse[None, :]
-    cosine, sine = jnp.cos(angles), jnp.sin(angles)
-    residual = tokens.astype(f32)
+    gains = jnp.stack([attn_in_gain, attn_out_gain, feed_in_gain, feed_out_gain])
+    mix_in, mix_out, down_out = flat(adapt_mix_in), flat(adapt_mix_out), flat(adapt_down_out)
+    head_tables = (adapt_heads_in, adapt_query_out, adapter_key_value_second)
+    feed_tables = (adapt_feed_in, adapt_feed_out, adapt_down_in)
     (
         queries, kvp, kvc, attended, exp_sum, narrow_heads, mixed, narrow_mix, attn_out, middle,
-        normed_feed, normed_all, head_weight, out_full, gate_share, up_share,
+        normed_feed, cosine, sine, masks, normed_all, head_weight, out_full, gate_share, up_share,
     ) = attention_forward(
+        tokens, gains, adapter_ids, mix_in, mix_out, head_tables, weights[:6], share
+    )
+    layer_out, grad_branch, narrow_feed, feed_all, gate_up = feed_forward(
+        normed_feed, middle, cotangent, gains, masks, down_out, feed_tables, gate_share, up_share,
+        down_rows,
+    )
+    grad_feed, feed_table, share_sum = feed_backward(
+        grad_branch, masks, down_out, narrow_feed, feed_tables, gate_share, up_share, down_rows,
+        gate_up, feed_all,
+    )
+    tokens_grad, feed_rows, feed_columns, head_rows, head_columns = attention_backward(
+        (
+            middle, attn_out, cotangent, gains, masks, mixed, narrow_mix, mix_in, mix_out,
+        ),
+        (queries, kvp, kvc, attended, exp_sum, narrow_heads, cosine, sine),
+        grad_feed,
         tokens,
-        (attn_in_gain[None], attn_out_gain[None], feed_in_gain[None]),
-        (heads_in.reshape(3 * LANES, width), query_out, key_out, value_out, mix_in, mix_out),
-        group_columns,
-        jnp.broadcast_to(own_mask, (rows, LANES)).astype(bf16),
-        cosine,
-        sine,
-        weights[:6],
-        share,
-    )
-    order = jnp.array([[0, 1], [4, 5], [6, 7], [2, 3]], dtype=jnp.int32)
-    pair_masks = lax.dynamic_slice_in_dim(
-        block_masks, lax.axis_index("dp") // 2 * 2, 2, axis=0
-    ).reshape(8, LANES)
-    plane_columns = jnp.repeat(
-        jnp.take(pair_masks, (rank % 8) ^ order, axis=0), rows, axis=1
-    ).reshape(4, 2 * rows, LANES).astype(bf16)
-    feed_in2 = feed_in.reshape(2 * LANES, width)
-    tables = (feed_in2, gate_out, up_out, down_in, down_out, plane_columns)
-    branch, narrow_feed, feed_all, gate_up = feed_forward(
-        normed_feed, *tables, gate_share, up_share, down_rows
-    )
-    layer_out = (middle + rms_scale(branch, feed_out_gain)).astype(bf16)
-    grad_top = cotangent.astype(f32)
-    grad_branch = norm_back(branch, feed_out_gain, grad_top).astype(bf16)
-    grad_feed, back_feed, grad_feed_out, grad_down_in, grad_down_out = feed_backward(
-        grad_branch, *tables, narrow_feed, gate_share, up_share, down_rows, gate_up
-    )
-    grad_feed = grad_feed.astype(f32)
-    grad_feed_in = dot_tn(back_feed.reshape(-1, 2 * LANES), feed_all.reshape(-1, width))
-    grad_middle = grad_top + norm_back(middle, feed_in_gain, grad_feed)
-    grad_attn = norm_back(attn_out, attn_out_gain, grad_middle).astype(bf16)
-
-    back_mix = (dot_nt(grad_attn, mix_out) * own_mask).astype(bf16)
-    grad_mix_in, grad_mix_out = dot_tn(back_mix, mixed), dot_tn(narrow_mix, grad_attn)
-    grad_mixed = (dot_nt(grad_attn, out_full) + dot_nn(back_mix, mix_in)).astype(bf16)
-    def by_rank(table):
-        return table.astype(bf16).reshape(-1, ADAPTERS, RANK, width).transpose(1, 0, 2, 3).reshape(
-            ADAPTERS, -1, width
-        )
-
-    feed_table = by_rank(jnp.concatenate([grad_feed_in, grad_down_out, grad_mix_out]))
-    feed_share = jnp.concatenate(
-        [grad_feed_out.reshape(2 * LANES, share), grad_down_in]
-    ).astype(bf16)
-    mix_table = jnp.pad(
-        grad_mix_in.astype(bf16).reshape(ADAPTERS, RANK, -1), ((0, 0), (0, 0), (0, width - mixed.shape[1]))
-    )
-    grad_normed, feed_rows, feed_columns, head_rows, head_columns = attention_backward(
-        grad_mixed,
-        (queries, kvp, kvc, attended, exp_sum, narrow_heads),
-        (heads_in.reshape(3 * LANES, width), query_out, key_out, value_out),
-        group_columns,
-        cosine,
-        sine,
-        mix_table,
-        normed_all,
-        head_weight,
+        head_tables,
+        (out_full, normed_all, head_weight),
         feed_table,
-        feed_share,
-    )
-    tokens_grad = grad_middle + norm_back(residual, attn_in_gain, grad_normed)
+        share_sum,
+    )
 
     feed_rows = feed_rows.reshape(ADAPTERS, 4, RANK, width)
     feed_columns = (

time: 781 us -> 690 us (0.88)
  Pallas kernels: 685 us -> 651 us
  local copies, waits for them, and re-layouts: 39.2 us -> 19.7 us
  other arithmetic: 28.6 us -> 11.2 us
  matrix products: 14.6 us -> 0 us
    pallas_call x1, Pallas kernels: 251 us -> 205 us  [attention_forward(): pl.pallas_call(attention_forward_kernel, out_shape=(shape((4, 2 * rows, H...]
    dot_general x6 -> x0, matrix products: 14.6 us -> none  [the longest x3 7.46 us: dot_tn(): lax.dot_general(a, b, (((0,), (0,)), ((), ())), preferred_element_type=f32)]
where the time goes in v2:
time: 690 us; the launch traced here: 683 us
  Pallas kernels  651 us (94%)
  local copies, waits for them, and re-layouts  19.7 us (3%)
  other arithmetic  11.2 us (2%)
    pallas_call x1, Pallas kernels, attention_forward(): pl.pallas_call(attention_forward_kernel, out_shape=(shape((4, 2 * rows, H...  205 us
    pallas_call x1, Pallas kernels, attention_backward(): pl.pallas_call(attention_backward_kernel, out_shape=(shape((rows, width),...  193 us
    pallas_call x1, Pallas kernels, feed_backward(): pl.pallas_call(feed_backward_kernel, out_shape=(shape((rows, width), bf16...  129 us
    pallas_call x1, Pallas kernels, feed_forward(): pl.pallas_call(feed_forward_kernel, out_shape=(shape((rows, width), bf16)...  125 us

profile of v2, /device:TPU:0, one launch (start us, length us, event | category | flops | bytes accessed | tf_op | source)
XLA Modules:
  0.0 683.1 jit_solution(16403297348987450398)
XLA Ops:
  0.6 0.7 stack.18
  1.4 0.7 stack.19
  2.1 0.7 stack.20
  2.8 0.7 stack.21
  3.5 0.7 pad_maximum_fusion.gains
  4.2 204.7 %attention_forward.1 = (bf16[4,512,256]{2,1,0:T(8,128)(2,1)}, bf16[4,2,2,256,256]{4,3,2,1,0:T(8,128)(2,1)}, bf16[2,2,256,256]{3,2,1,0:T(8,128)(2,1)}, bf16[4,256...) custom-call(bf16[256,2304]{1,0:T(8,128)(2,1)} %tokens_hbm.1, ...), custom_call_target="tpu_custom_call" | custom-call | tf_op jit(solution)/shard_map/attention_forward/pallas_call | solution.py:1079
  208.9 124.7 %feed_forward.1 = (bf16[256,2304]{1,0:T(8,128)(2,1)}, bf16[256,2304]{1,0:T(8,128)(2,1)}, bf16[4,3,512,128]{3,2,1,0:T(8,128)(2,1)}, bf16[4,512,2304]{2,1,0:T(8,128)(2,1)}, bf16[4,2,512,1152]{3,2,1,0:T(8,128)(2,1)}) custom-call(bf16[256,2304]{1,0:T(8,128)(2,1)} %get-tuple-element.43.own, bf16[256,2304]{1,0:T(8,128)(2,1)} %get-tuple-element.44.middle, ...), custom_call_target="tpu_custom_call" | custom-call | tf_op jit(solution)/shard_map/feed_forward/pallas_call | solution.py:512
  333.6 128.6 %feed_backward.1 = (bf16[256,2304]{1,0:T(8,128)(2,1)}, bf16[8,48,2304]{2,1,0:T(8,128)(2,1)}, bf16[4,96,1152]{2,1,0:T(8,128)(2,1)}) custom-call(bf16[256,2304]{1,0:T(8,128)(2,1)} %get-tuple-element.60.own, f32[2,16,128]{2,1,0:T(8,128)} %get-tuple-element.45.masks, bf16[128,2304]{1,0:T(8,128)(2,1)} %bitcast.37, ...), custom_call_target="tpu_custom_call" | custom-call | tf_op jit(solution)/shard_map/feed_backward/pallas_call | solution.py:546
  462.2 193.0 %attention_backward.1 = (f32[256,2304]{1,0:T(8,128)}, bf16[8,4,16,2304]{3,2,1,0:T(8,128)(2,1)}, bf16[8,4,96,1152]{3,2,1,0:T(8,128)(2,1)}, bf16[8,4,16,2304]{3,2,1,0:T(8,128)(2,1)}, bf16[8,4,16,1024]{3,2,1,0:T(8,128)(2,1)}) custom-call(bf16[256,2304]{1,0:T(8,128)(2,1)} %get-tuple-element.44.middle, bf16[256,2304]{1,0:T(8,128)(2,1)} %get-tuple-element.49.attn_out, ...), custom_call_target="tpu_custom_call" | custom-call | tf_op jit(solution)/shard_map/attention_backward/pallas_call | solution.py:1704
  655.2 1.3 copy.39
  656.6 0.1 convert_bitcast_fusion
  656.7 1.1 copy.46
  657.8 0.2 copy.41
  658.0 0.2 stack_reshape.6
  658.2 0.0 copy-start.2
  658.2 0.2 copy.42
  658.4 0.2 stack_reshape.7
  658.6 0.1 maximum_convert_fusion
  658.7 1.1 copy.44
  659.7 0.4 copy-done.2
  660.1 1.1 bitcast_convert_fusion.2
  661.2 0.0 copy-start
  661.2 2.2 slice_convert_fusion.1
  663.4 0.2 copy-done
  663.6 1.6 slice_convert_fusion.2
  665.2 1.6 bitcast_convert_fusion
  666.9 4.1 copy.47
  671.0 2.7 fusion
  673.6 1.1 slice_convert_fusion
  674.7 0.0 copy-start.3
  674.8 4.4 copy.45
  679.1 0.0 copy-done.3
  679.1 0.0 copy-start.1
  679.1 1.0 copy.50
  680.2 1.1 copy-done.1
  681.2 1.4 copy.51
  (1 shorter events, 0.0 us)
Async XLA Ops:
  658.2 1.9 copy-start.2
  661.2 2.4 copy-start
  674.7 4.4 copy-start.3
  679.1 2.1 copy-start.1

commit v3 on v2

--- a/solution.py
+++ b/solution.py
@@ -98,18 +98,18 @@
         self.c = [
             copy(0, own, land.at[0, far], pc),
             copy(1, own.at[h0], land.at[1, h0], px),
-            copy(2, own.at[h1], land.at[3, h1], py),
-            copy(3, own.at[h1], land.at[1, h1], px),
-            copy(4, own.at[h0], land.at[3, h0], py),
+            copy(2, own.at[h1], land.at[1, h1], py),
+            copy(3, own.at[h1], land.at[3, h0], px),
+            copy(4, own.at[h0], land.at[3, h1], py),
             copy(5, land.at[1, h0], land.at[2, h0], py),
-            copy(6, land.at[3, h1], land.at[2, h1], px),
+            copy(6, land.at[1, h1], land.at[2, h1], px),
             copy(7, land.at[1, near], land.at[1, far], pc),
             copy(8, land.at[3, near], land.at[3, far], pc),
             copy(9, land.at[2, near], land.at[2, far], pc),
         ]
 
     def begin(self):
-        for i in range(5):
+        for i in range(3):
             self.c[i].start()
 
     def before(self, i):
@@ -125,10 +125,9 @@
             c[5].start()
             c[2].wait_recv()
             c[6].start()
-            c[3].wait_recv()
             c[7].start()
-            c[4].wait_recv()
-            c[8].start()
+            for k in (3, 4):
+                c[k].start()
             c[7].wait_recv()
 
         @pl.when(i == 2)
@@ -140,6 +139,9 @@
 
         @pl.when(i == 3)
         def _():
+            c[3].wait_recv()
+            c[4].wait_recv()
+            c[8].start()
             c[8].wait_recv()
 
     def finish(self):
@@ -148,14 +150,17 @@
 
 
 def plane_masks(masks, i, rows):
-    group = (i + 1) // 2 % 2
-    near = (lax.axis_index("blk") + 2 * (i // 2)) % 4
-    far = near + 1 - 2 * (near % 2)
-    first = masks[group, pl.ds(near, 1), :]
-    second = masks[group, pl.ds(far, 1), :]
-    return jnp.where(
-        lax.broadcasted_iota(jnp.int32, (2 * rows, LANES), 0) < rows, first, second
-    )
+    b = lax.axis_index("blk")
+    diagonal = i // 2 * (1 - i % 2)
+    away = (i + 2) // 3
+    out = jnp.zeros((2 * rows, LANES), f32)
+    place = lax.broadcasted_iota(jnp.int32, (2 * rows, LANES), 0) // (rows // 2)
+    for half, (group, shift) in enumerate(((away, diagonal), (diagonal, away))):
+        near = (b + 2 * shift) % 4
+        far = near + 1 - 2 * (near % 2)
+        out = jnp.where(place == half, masks[group, pl.ds(near, 1), :], out)
+        out = jnp.where(place == 2 + half, masks[group, pl.ds(far, 1), :], out)
+    return out
 
 
 def feed_table_copies(rank, share, feed_in_hbm, feed_out_hbm, down_in_hbm, feed_in, feed_out, down_in):
@@ -197,9 +202,9 @@
         ]
         self.e = [
             copy(first + 6, part.at[1, h0], from_x.at[h0], px),
-            copy(first + 7, part.at[3, h1], from_y.at[h1], py),
-            copy(first + 8, part.at[1, h1], from_x.at[h1], px),
-            copy(first + 9, part.at[3, h0], from_y.at[h0], py),
+            copy(first + 7, part.at[1, h1], from_y.at[h1], py),
+            copy(first + 8, part.at[3, h0], from_x.at[h1], px),
+            copy(first + 9, part.at[3, h1], from_y.at[h0], py),
         ]
 
     def merge(self, i):
@@ -222,6 +227,7 @@
                 if k == 2:
                     self.merge(1)
                     self.e[0].start()
+                    self.e[1].start()
                     self.merge(2)
                     self.d[0].start()
                     self.d[1].start()
@@ -229,12 +235,11 @@
     def finish(self, write, between=None):
         h, h0, h1 = self.h, pl.ds(0, self.h), pl.ds(self.h, self.h)
         self.merge(3)
-        self.e[1].start()
         self.d[0].wait_recv()
-        add_into(self.part.at[3, h0], self.diag.at[h0], h)
+        add_into(self.part.at[3, h1], self.diag.at[h0], h)
         self.e[3].start()
         self.d[1].wait_recv()
-        add_into(self.part.at[1, h1], self.diag.at[h1], h)
+        add_into(self.part.at[3, h0], self.diag.at[h1], h)
         self.e[2].start()
         if between is not None:
             between()
@@ -268,21 +273,32 @@
     return pl.ds(pl.multiple_of(i * size, size), size)
 
 
+def woven(gate_hbm, up_hbm, both):
+    out = []
+    for j in range(gate_hbm.shape[1] // 128):
+        for k, ref in enumerate((gate_hbm, up_hbm)):
+            out.append(
+                (ref.at[:, pl.ds(j * 128, 128)], both.at[:, pl.ds(j * 256 + k * 128, 128)])
+            )
+    return out
+
+
 def feed_forward_kernel(
     own, middle, cotangent, gains, masks, down_out, feed_in_hbm, feed_out_hbm, down_in_hbm,
     gate_hbm, up_hbm, down_hbm,
     layer_out, grad_branch, narrow, feed_all, gate_up,
-    feed_in, feed_out, down_in, gate, up, down, land, hidden, saved, part, odd, from_core, from_x, from_y, diag,
+    feed_in, feed_out, down_in, weave, down, land, hidden, saved, part, odd, from_core, from_x, from_y, diag,
     send, recv, load, store,
 ):
     rows = own.shape[0]
-    share = gate.shape[1]
+    share = gate_hbm.shape[1]
     width = own.shape[1]
-    tile = 384
+    tile = 256
     loads = [
         pltpu.make_async_copy(s, d, load.at[i])
         for i, (s, d) in enumerate(
-            [(gate_hbm, gate), (up_hbm, up), (down_hbm, down)]
+            woven(gate_hbm, up_hbm, weave)
+            + [(down_hbm, down)]
             + feed_table_copies(
                 plane_rank(), share, feed_in_hbm, feed_out_hbm, down_in_hbm, feed_in, feed_out,
                 down_in,
@@ -323,11 +339,12 @@
         for k in range(2):
             narrow[i, k] = (dot_nt(land[i], flat(feed_in[k])) * mask).astype(bf16)
 
-        @pl.loop(0, share // tile)
+        @pl.loop(0, share // 128)
         def _(n):
-            at = span(n, tile)
-            g = dot_nn(land[i], gate[:, at]) + dot_nn(narrow[i, 0], flat(feed_out[0, :, :, at]))
-            u = dot_nn(land[i], up[:, at]) + dot_nn(narrow[i, 1], flat(feed_out[1, :, :, at]))
+            at = span(n, 128)
+            pre = dot_nn(land[i], weave[:, span(n, 256)])
+            g = pre[:, :128] + dot_nn(narrow[i, 0], flat(feed_out[0, :, :, at]))
+            u = pre[:, 128:] + dot_nn(narrow[i, 1], flat(feed_out[1, :, :, at]))
             saved[slot, 0, :, at] = g.astype(bf16)
             saved[slot, 1, :, at] = u.astype(bf16)
             th = jnp.tanh(GELU_SLOPE * (g + GELU_CUBE * g * g * g))
@@ -365,18 +382,19 @@
     own, masks, down_out, narrow, feed_in_hbm, feed_out_hbm, down_in_hbm,
     gate_hbm, up_hbm, down_hbm, gate_up, feed_all,
     grad_feed, feed_table, share_sum,
-    both, t_feed_out, t_down_in, t_down_out, share_table, share_in, share_piece,
-    feed_in, feed_out, down_in, gate, up, down, land, saved, gg, gu, part, odd, from_core, from_x, from_y, diag,
+    back, both, t_feed_out, t_down_in, t_down_out, share_table, share_in, share_piece,
+    feed_in, feed_out, down_in, weave, down, land, saved, gg, part, odd, from_core, from_x, from_y, diag,
     send, recv, load, fetch,
 ):
     rows = own.shape[0]
-    share = gate.shape[1]
+    share = gate_hbm.shape[1]
     width = own.shape[1]
-    tile = 384
+    tile = 256
     loads = [
         pltpu.make_async_copy(s, d, load.at[i])
         for i, (s, d) in enumerate(
-            [(down_hbm, down), (gate_hbm, gate), (up_hbm, up)]
+            woven(gate_hbm, up_hbm, weave)
+            + [(down_hbm, down)]
             + feed_table_copies(
                 plane_rank(), share, feed_in_hbm, feed_out_hbm, down_in_hbm, feed_in, feed_out,
                 down_in,
@@ -414,37 +432,48 @@
         gather.before(i)
         bring(i).wait()
         mask = plane_masks(masks, i, rows)
-        back = (dot_nt(land[i], down_out[...]) * mask).astype(bf16)
-
-        @pl.loop(0, share // tile)
+        back[...] = (dot_nt(land[i], down_out[...]) * mask).astype(bf16)
+
+        @pl.loop(0, 2)
         def _(n):
-            at = span(n, tile)
-            gh = dot_nt(land[i], down[at, :]) + dot_nn(back, flat(down_in[:, :, at]))
-            g = saved[0, :, at].astype(f32)
-            u = saved[1, :, at].astype(f32)
+            at = span(n, rows)
+            gh = dot_nt(land[i, at, :], down[...]) + dot_nn(back[at, :], flat(down_in[...]))
+            g = saved[0, at, :].astype(f32)
+            u = saved[1, at, :].astype(f32)
             th = jnp.tanh(GELU_SLOPE * (g + GELU_CUBE * g * g * g))
             gelu = 0.5 * g * (1.0 + th)
             slope = 0.5 * (1.0 + th) + 0.5 * g * (1.0 - th * th) * GELU_SLOPE * (
                 1.0 + 3.0 * GELU_CUBE * g * g
             )
-            t_down_in[:, at] += dot_tn(back, (gelu * u).astype(bf16))
-            gg[:, at] = (gh * u * slope).astype(bf16)
-            gu[:, at] = (gh * gelu).astype(bf16)
+            saved[0, at, :] = (gelu * u).astype(bf16)
+            left = (gh * u * slope).astype(bf16)
+            right = (gh * gelu).astype(bf16)
+            for j in range(share // 128):
+                lanes = slice(j * 128, (j + 1) * 128)
+                gg[at, j * 256 : j * 256 + 128] = left[:, lanes]
+                gg[at, j * 256 + 128 : (j + 1) * 256] = right[:, lanes]
+
+        t_down_in[...] += dot_tn(back[...], saved[0])
 
         @pl.when(i < 3)
         def _():
             bring(i + 1).start()
 
-        both[i, :, :LANES] = (dot_nt(gg[...], flat(feed_out[0])) * mask).astype(bf16)
-        both[i, :, LANES:] = (dot_nt(gu[...], flat(feed_out[1])) * mask).astype(bf16)
+        for k in range(2):
+            low = jnp.zeros((2 * rows, LANES), f32)
+            for j in range(share // 128):
+                at = j * 256 + k * 128
+                low = low + dot_nt(
+                    gg[:, at : at + 128], flat(feed_out[k, :, :, j * 128 : (j + 1) * 128])
+                )
+            both[i, :, k * LANES : (k + 1) * LANES] = (low * mask).astype(bf16)
         reduce.before(i)
 
         @pl.loop(0, width // tile)
         def _(n):
             at = span(n, tile)
             got = (
-                dot_nt(gg[...], gate[at, :])
-                + dot_nt(gu[...], up[at, :])
+                dot_nt(gg[...], weave[at, :])
                 + dot_nn(both[i, :, :LANES], flat(feed_in[0, :, :, at]))
                 + dot_nn(both[i, :, LANES:], flat(feed_in[1, :, :, at]))
             ).astype(bf16)
@@ -452,8 +481,12 @@
             odd[i % 2, :, at] = got[rows:]
 
         reduce.after(i)
-        t_feed_out[0] += dot_tn(narrow[i, 0], gg[...])
-        t_feed_out[1] += dot_tn(narrow[i, 1], gu[...])
+        for k in range(2):
+            for j in range(share // 128):
+                at = j * 256 + k * 128
+                t_feed_out[k, :, j * 128 : (j + 1) * 128] += dot_tn(
+                    narrow[i, k], gg[:, at : at + 128]
+                )
         t_down_out[...] += dot_tn(narrow[i, 2], land[i])
 
     share_table[: 2 * LANES] = t_feed_out[...].reshape(2 * LANES, share).astype(bf16)
@@ -522,15 +555,14 @@
         out_specs=(VM, VM, VM, ANY, ANY),
         scratch_shapes=feed_table_scratch(width, share)
         + [
-            pltpu.VMEM(gate.shape, bf16),
-            pltpu.VMEM(up.shape, bf16),
+            pltpu.VMEM((width, 2 * share), bf16),
             pltpu.VMEM(down.shape, bf16),
             pltpu.VMEM((4, 2 * rows, width), bf16),
             pltpu.VMEM((2 * rows, share), bf16),
             pltpu.VMEM((2, 2, 2 * rows, share), bf16),
         ]
         + feed_scratch(rows, width)
-        + [pltpu.SemaphoreType.DMA((8,)), pltpu.SemaphoreType.DMA((4,))],
+        + [pltpu.SemaphoreType.DMA((6 + share // 64,)), pltpu.SemaphoreType.DMA((4,))],
         compiler_params=pltpu.CompilerParams(
             collective_id=1, has_side_effects=True, vmem_limit_bytes=62 << 20
         ),
@@ -553,6 +585,7 @@
         in_specs=[VM] * 4 + [ANY] * 8,
         out_specs=(VM, VM, ANY),
         scratch_shapes=[
+            pltpu.VMEM((2 * rows, LANES), bf16),
             pltpu.VMEM((4, 2 * rows, 2 * LANES), bf16),
             pltpu.VMEM((2, LANES, share), f32),
             pltpu.VMEM((LANES, share), f32),
@@ -563,16 +596,14 @@
         ]
         + feed_table_scratch(width, share)
         + [
-            pltpu.VMEM(gate.shape, bf16),
-            pltpu.VMEM(up.shape, bf16),
+            pltpu.VMEM((width, 2 * share), bf16),
             pltpu.VMEM(down.shape, bf16),
             pltpu.VMEM((4, 2 * rows, width), bf16),
             pltpu.VMEM((2, 2 * rows, share), bf16),
-            pltpu.VMEM((2 * rows, share), bf16),
-            pltpu.VMEM((2 * rows, share), bf16),
+            pltpu.VMEM((2 * rows, 2 * share), bf16),
         ]
         + feed_scratch(rows, width, TableSum.COUNT)
-        + [pltpu.SemaphoreType.DMA((8,)), pltpu.SemaphoreType.DMA((6,))],
+        + [pltpu.SemaphoreType.DMA((6 + share // 64,)), pltpu.SemaphoreType.DMA((6,))],
         compiler_params=pltpu.CompilerParams(
             collective_id=2, has_side_effects=True, vmem_limit_bytes=62 << 20
         ),
@@ -1419,8 +1450,6 @@
         at, o_table.at[span(1 - place.x, lanes_half)], o_got, place.px
     )
 
-    share_spread.plane()
-
     bring_feed.wait()
 
     @pl.loop(0, rows // 32)
@@ -1470,9 +1499,9 @@
     for h in range(2):
         lanes = pl.ds(pl.multiple_of(b * 2 * HEAD + h * HEAD, 128), HEAD)
         g[b, h * rows : (h + 1) * rows, :] = grad_mixed[:, lanes]
-    share_spread.forward()
     for c in swaps:
         c.wait()
+    share_spread.plane()
 
     ones = jnp.ones((8, HEAD), f32)
 
@@ -1532,9 +1561,11 @@
                 kv_copy(k).start()
                 if k == 1:
                     feed_reduce.merge()
-                    share_spread.corner()
                 if k == 2:
                     feed_reduce.corner()
+                    share_spread.forward()
+                if k == 3:
+                    share_spread.corner()
 
     feed_reduce.finish()
     feed_spread.scatter()
@@ -1585,6 +1616,7 @@
                 dot_nt(grad_pre[at, lanes], flat(table[...])) * mask
             ).astype(bf16)
 
+    feed_spread.plane()
     for i, lanes in enumerate(
         (slice(0, 2 * HEAD), slice(2 * HEAD, 3 * HEAD), slice(3 * HEAD, 4 * HEAD))
     ):
@@ -1603,7 +1635,6 @@
                 h_table[a, i * RANK : (i + 1) * RANK, at] = got[first : first + RANK]
 
     head_reduce.begin()
-    feed_spread.plane()
 
     def project(slot, target):
         at_rows = span(target, rows)
@@ -1620,12 +1651,13 @@
     to_y = copy(11, part[2], from_y, place.py)
     project(0, place.b_yc)
     to_core[0].start()
+    head_reduce.merge()
+    feed_spread.forward()
     project(2, place.b_y)
+    head_reduce.corner()
     to_core[0].wait_recv()
     add_into(part[2], from_core.at[0], rows)
     to_y.start()
-    head_reduce.merge()
-    feed_spread.forward()
     out_swap.wait_recv()
 
     @pl.loop(0, lanes_half // 16)
@@ -1634,22 +1666,22 @@
         mine = pl.ds(pl.multiple_of(place.x * lanes_half + i * 16, 16), 16)
         o_total[at, :] = (o_table[mine, :].astype(f32) + o_got[at, :].astype(f32)).astype(bf16)
 
+    feed_spread.corner()
     out_spread.scatter()
+    head_reduce.finish()
+    head_spread.scatter()
     project(1, place.b_c)
     to_core[1].start()
-    head_reduce.corner()
-    feed_spread.corner()
+    head_spread.gather()
     out_spread.gather()
     project(3, b)
-    head_reduce.finish()
-    head_spread.scatter()
+    head_spread.plane()
     out_spread.plane()
-    head_spread.gather()
+    head_spread.forward()
+    out_spread.forward()
     to_core[1].wait_recv()
-    out_spread.forward()
-    head_spread.plane()
+    head_spread.corner()
     out_spread.corner()
-    head_spread.forward()
     to_y.wait_recv()
     bring_tokens.wait()
 
@@ -1663,7 +1695,6 @@
         )
         tokens_grad[at, :] += norm_grad(tokens[at, :].astype(f32), gains[0:1, :], grad)
 
-    head_spread.corner()
     for spread in (share_spread, feed_spread, out_spread, head_spread):
         spread.finish()
     own_share.wait()

time: 690 us -> 629 us (0.912)
  Pallas kernels: 651 us -> 597 us
    pallas_call x1, Pallas kernels: 193 us -> 160 us  [attention_backward(): pl.pallas_call(attention_backward_kernel, out_shape=(shape((rows, width),...]
    pallas_call x1, Pallas kernels: 125 us -> 108 us  [feed_forward(): pl.pallas_call(feed_forward_kernel, out_shape=(shape((rows, width), bf16)...]
where the time goes in v3:
time: 629 us; the launch traced here: 628 us
  Pallas kernels  597 us (95%)
  local copies, waits for them, and re-layouts  19.7 us (3%)
  other arithmetic  11.2 us (2%)
    pallas_call x1, Pallas kernels, attention_forward(): pl.pallas_call(attention_forward_kernel, out_shape=(shape((4, 2 * rows, H...  205 us
    pallas_call x1, Pallas kernels, attention_backward(): pl.pallas_call(attention_backward_kernel, out_shape=(shape((rows, width),...  160 us
    pallas_call x1, Pallas kernels, feed_backward(): pl.pallas_call(feed_backward_kernel, out_shape=(shape((rows, width), bf16...  124 us
    pallas_call x1, Pallas kernels, feed_forward(): pl.pallas_call(feed_forward_kernel, out_shape=(shape((rows, width), bf16)...  108 us

profile of v3, /device:TPU:0, one launch (start us, length us, event | category | flops | bytes accessed | tf_op | source)
XLA Modules:
  0.0 628.2 jit_solution(13091954494096453726)
XLA Ops:
  0.6 0.7 stack.18
  1.4 0.7 stack.19
  2.1 0.7 stack.20
  2.8 0.7 stack.21
  3.5 0.7 pad_maximum_fusion.gains
  4.2 204.7 %attention_forward.1 = (bf16[4,512,256]{2,1,0:T(8,128)(2,1)}, bf16[4,2,2,256,256]{4,3,2,1,0:T(8,128)(2,1)}, bf16[2,2,256,256]{3,2,1,0:T(8,128)(2,1)}, bf16[4,256...) custom-call(bf16[256,2304]{1,0:T(8,128)(2,1)} %tokens_hbm.1, ...), custom_call_target="tpu_custom_call" | custom-call | tf_op jit(solution)/shard_map/attention_forward/pallas_call | solution.py:1110
  208.9 107.6 %feed_forward.1 = (bf16[256,2304]{1,0:T(8,128)(2,1)}, bf16[256,2304]{1,0:T(8,128)(2,1)}, bf16[4,3,512,128]{3,2,1,0:T(8,128)(2,1)}, bf16[4,512,2304]{2,1,0:T(8,128)(2,1)}, bf16[4,2,512,1152]{3,2,1,0:T(8,128)(2,1)}) custom-call(bf16[256,2304]{1,0:T(8,128)(2,1)} %get-tuple-element.43.own, bf16[256,2304]{1,0:T(8,128)(2,1)} %get-tuple-element.44.middle, ...), custom_call_target="tpu_custom_call" | custom-call | tf_op jit(solution)/shard_map/feed_forward/pallas_call | solution.py:545
  316.5 124.3 %feed_backward.1 = (bf16[256,2304]{1,0:T(8,128)(2,1)}, bf16[8,48,2304]{2,1,0:T(8,128)(2,1)}, bf16[4,96,1152]{2,1,0:T(8,128)(2,1)}) custom-call(bf16[256,2304]{1,0:T(8,128)(2,1)} %get-tuple-element.60.own, f32[2,16,128]{2,1,0:T(8,128)} %get-tuple-element.45.masks, bf16[128,2304]{1,0:T(8,128)(2,1)} %bitcast.37, ...), custom_call_target="tpu_custom_call" | custom-call | tf_op jit(solution)/shard_map/feed_backward/pallas_call | solution.py:578
  440.8 159.9 %attention_backward.1 = (f32[256,2304]{1,0:T(8,128)}, bf16[8,4,16,2304]{3,2,1,0:T(8,128)(2,1)}, bf16[8,4,96,1152]{3,2,1,0:T(8,128)(2,1)}, bf16[8,4,16,2304]{3,2,1,0:T(8,128)(2,1)}, bf16[8,4,16,1024]{3,2,1,0:T(8,128)(2,1)}) custom-call(bf16[256,2304]{1,0:T(8,128)(2,1)} %get-tuple-element.44.middle, bf16[256,2304]{1,0:T(8,128)(2,1)} %get-tuple-element.49.attn_out, ...), custom_call_target="tpu_custom_call" | custom-call | tf_op jit(solution)/shard_map/attention_backward/pallas_call | solution.py:1735
  600.8 1.3 copy.39
  602.1 0.1 convert_bitcast_fusion
  602.3 1.1 copy.46
  603.3 0.2 copy.41
  603.5 0.2 stack_reshape.6
  603.7 0.0 copy-start.2
  603.7 0.2 copy.42
  603.9 0.2 stack_reshape.7
  604.1 0.1 maximum_convert_fusion
  604.2 1.1 copy.44
  605.3 0.4 copy-done.2
  605.6 1.1 bitcast_convert_fusion.2
  606.7 0.0 copy-start
  606.7 2.2 slice_convert_fusion.1
  608.9 0.2 copy-done
  609.1 1.6 slice_convert_fusion.2
  610.8 1.6 bitcast_convert_fusion
  612.4 4.1 copy.47
  616.5 2.7 fusion
  619.2 1.1 slice_convert_fusion
  620.3 0.0 copy-start.3
  620.3 4.4 copy.45
  624.7 0.0 copy-done.3
  624.7 0.0 copy-start.1
  624.7 1.0 copy.50
  625.7 1.1 copy-done.1
  626.8 1.4 copy.51
  (1 shorter events, 0.0 us)
Async XLA Ops:
  603.7 1.9 copy-start.2
  606.7 2.4 copy-start
  620.3 4.4 copy-start.3
  624.7 2.1 copy-start.1

commit v4 on v3

--- a/solution.py
+++ b/solution.py
@@ -755,7 +755,6 @@
     ]
     for cp in stage[:3]:
         cp.start()
-    token_copies[0].start()
     for cp in stage[3:]:
         cp.start()
     token_copies[1].start()
@@ -764,17 +763,6 @@
     for cp in own_loads[:3]:
         cp.wait()
     across[0].start()
-    for cp in stage[6:]:
-        cp.wait_recv()
-    across[1].start()
-    for cp in stage[:3]:
-        cp.wait_recv()
-    across[2].start()
-    for cp in stage[3:6]:
-        cp.wait_recv()
-    across[3].start()
-    token_copies[0].wait_recv()
-    token_copies[2].start()
     lane = lax.broadcasted_iota(jnp.int32, (rows, HEAD // 2), 1).astype(f32)
     inverse = jnp.exp(lane * (-2.0 / HEAD * math.log(rope_base)))
 
@@ -787,6 +775,18 @@
         cosine[at, :] = jnp.cos(angle)
         sine[at, :] = jnp.sin(angle)
 
+    for cp in stage[6:]:
+        cp.wait_recv()
+    across[1].start()
+    for cp in stage[:3]:
+        cp.wait_recv()
+    token_copies[0].start()
+    across[2].start()
+    for cp in stage[3:6]:
+        cp.wait_recv()
+    across[3].start()
+    token_copies[0].wait_recv()
+    token_copies[2].start()
     for cp in table_loads:
         cp.wait()
     mask_copy.wait()
@@ -886,49 +886,39 @@
 
     half_head = HEAD // 2
 
-    @pl.loop(0, 4)
-    def _(t):
-        at = block(t)
-        mask = masks[pl.ds(t, 1), :]
+    def turned(pre, at, scale):
         cos, sin = cosine[at, :], sine[at, :]
-        a = normed_all[at, :]
-        for i in range(3):
-            lanes = slice(i * LANES, (i + 1) * LANES)
-            narrow[at, lanes] = (dot_nt(a, flat(heads_in[i])) * mask).astype(bf16)
-
-        def turned(pre, scale):
-            first, second = pre[:, :half_head], pre[:, half_head:]
-            one, two = first * cos - second * sin, second * cos + first * sin
-            if scale != 1.0:
-                one, two = one * scale, two * scale
-            return jnp.concatenate([one, two], axis=1).astype(bf16)
-
-        for h in range(2):
-            lanes = slice(h * HEAD, (h + 1) * HEAD)
-            pre = dot_nn(a, wall[:, lanes]) + dot_nn(
-                narrow[at, :LANES], flat(query_out[:, :, lanes])
-            )
-            queries[t, h * rows : (h + 1) * rows, :] = turned(pre, HEAD ** (-0.5))
-        pre = dot_nn(a, wall[:, 2 * HEAD : 3 * HEAD]) + dot_nn(
+        first, second = pre[:, :half_head], pre[:, half_head:]
+        one, two = first * cos - second * sin, second * cos + first * sin
+        if scale != 1.0:
+            one, two = one * scale, two * scale
+        return jnp.concatenate([one, two], axis=1).astype(bf16)
+
+    def keys_values(p):
+        at = pl.ds(2 * p * rows, 2 * rows)
+        first = lax.broadcasted_iota(jnp.int32, (2 * rows, 3 * LANES), 0) < rows
+        both = [jnp.concatenate([masks[pl.ds(2 * p + k, 1), :]] * 3, axis=1) for k in range(2)]
+        mask = jnp.where(first, both[0], both[1])
+        low = dot_nt(normed_all[at, :], heads_in[...].reshape(3 * LANES, width))
+        narrow[at, :] = (low * mask).astype(bf16)
+        pre = dot_nn(normed_all[at, :], wall[:, 2 * HEAD : 3 * HEAD]) + dot_nn(
             narrow[at, LANES : 2 * LANES], flat(key_out[...])
         )
-        key = turned(pre, 1.0)
+        key = turned(pre, at, 1.0)
         value = (
-            dot_nn(a, wall[:, 3 * HEAD :]) + dot_nn(
-                narrow[at, 2 * LANES :], flat(value_out[...])
-            )
+            dot_nn(normed_all[at, :], wall[:, 3 * HEAD :])
+            + dot_nn(narrow[at, 2 * LANES :], flat(value_out[...]))
         ).astype(bf16)
-
-        @pl.when(t < 2)
-        def _():
-            kvp[z, 0, t] = key
-            kvp[z, 1, t] = value
-
-        @pl.when(t >= 2)
-        def _():
-            kvc[0, t - 2] = key
-            kvc[1, t - 2] = value
-
+        for k in range(2):
+            part_rows = slice(k * rows, (k + 1) * rows)
+            if p == 0:
+                kvp[z, 0, k] = key[part_rows]
+                kvp[z, 1, k] = value[part_rows]
+            else:
+                kvc[0, k] = key[part_rows]
+                kvc[1, k] = value[part_rows]
+
+    keys_values(0)
     def hop(direction, d):
         index = 42 + d if direction > 0 else 45 + d
         zz = z - d * direction
@@ -943,6 +933,19 @@
 
     pass_on(1, 0)
     pass_on(-1, 0)
+    keys_values(1)
+
+    @pl.loop(0, 2)
+    def _(p):
+        at = span(p, 2 * rows)
+        for h in range(2):
+            lanes = slice(h * HEAD, (h + 1) * HEAD)
+            pre = dot_nn(normed_all[at, :], wall[:, lanes]) + dot_nn(
+                narrow[at, :LANES], flat(query_out[:, :, lanes])
+            )
+            got = turned(pre, at, HEAD ** (-0.5))
+            for k in range(2):
+                queries[2 * p + k, h * rows : (h + 1) * rows, :] = got[k * rows : (k + 1) * rows]
 
     send_direct((1, 3))
     acc[...] = jnp.zeros_like(acc)
@@ -970,8 +973,6 @@
         step(t, kvp[z, 0, 0], kvp[z, 1, 0], False)
         step(t, kvp[z, 0, 1], kvp[z, 1, 1], False)
 
-    for cp in whole:
-        cp.start()
     wo_first[0].wait_recv()
     wo_next[0].start()
     wo_first[1].wait_recv()
@@ -982,10 +983,6 @@
         d = i // 2 + 1
         direction = 1 - 2 * (i % 2)
         zz = z - d * direction
-
-        @pl.when(i == 2)
-        def _():
-            pass_along((4, 5))
 
         @pl.when((zz >= 0) & (zz < planes))
         def _():
@@ -1044,7 +1041,10 @@
     ]
     for cp in mixes:
         cp.start()
+    for cp in whole:
+        cp.start()
     mixed[:, lanes] = attended[b]
+    pass_along((4, 5))
     pass_along((1, 3))
     wo_first[2].wait_recv()
     wo_next[2].start()
@@ -1782,6 +1782,71 @@
         ),
         name="attention_backward",
     )(*rows_in, *kept, grad_feed, tokens, *tables, *weights, feed_table, feed_share)
+
+
+def lay_out_kernel(
+    feed_rows, feed_columns, head_rows, head_columns,
+    heads_in, query_out, kv_out, t_mix_in, t_mix_out, feed_in, feed_out, t_down_in, t_down_out,
+):
+    rows = feed_rows[0]
+    feed_in[0, 0] = rows[0].astype(f32)
+    feed_in[0, 1] = rows[1].astype(f32)
+    t_down_out[0] = rows[2].astype(f32)
+    t_mix_out[0] = rows[3].astype(f32)
+    rows = head_rows[0]
+    for i in range(3):
+        heads_in[0, i] = rows[i].astype(f32)
+    t_mix_in[0] = rows[3, :, : t_mix_in.shape[2]].astype(f32)
+    share = feed_out.shape[3]
+    table = feed_columns[0].reshape(3, ADAPTERS, RANK, share)
+    for a in range(ADAPTERS):
+        feed_out[a, 0] = table[0, a].astype(f32)
+        feed_out[a, 1] = table[1, a].astype(f32)
+        t_down_in[a] = table[2, a].astype(f32)
+    for a in range(head_columns.shape[1]):
+        got = head_columns[0, a].astype(f32)
+        query_out[a] = got[:, : 2 * HEAD]
+        kv_out[a, 0] = got[:, 2 * HEAD : 3 * HEAD]
+        kv_out[a, 1] = got[:, 3 * HEAD :]
+
+
+def lay_out(feed_rows, feed_columns, head_rows, head_columns):
+    planes, _, width = feed_rows.shape[1:]
+    share = feed_columns.shape[3]
+    ff = 8 * share
+
+    def whole(array):
+        return pl.BlockSpec((1,) + array.shape[1:], lambda r: (r, 0, 0, 0))
+
+    return pl.pallas_call(
+        lay_out_kernel,
+        grid=(8,),
+        out_shape=(
+            shape((ADAPTERS, 3, RANK, width), f32),
+            shape((ADAPTERS, RANK, 8 * HEAD), f32),
+            shape((ADAPTERS, 2, RANK, 4 * HEAD), f32),
+            shape((ADAPTERS, RANK, 8 * HEAD), f32),
+            shape((ADAPTERS, RANK, width), f32),
+            shape((ADAPTERS, 2, RANK, width), f32),
+            shape((ADAPTERS, 2, RANK, ff), f32),
+            shape((ADAPTERS, RANK, ff), f32),
+            shape((ADAPTERS, RANK, width), f32),
+        ),
+        in_specs=[whole(x) for x in (feed_rows, feed_columns, head_rows, head_columns)],
+        out_specs=(
+            pl.BlockSpec((1, 3, RANK, width), lambda r: (r, 0, 0, 0)),
+            pl.BlockSpec((planes, RANK, 2 * HEAD), lambda r: (r // 4, 0, r % 4)),
+            pl.BlockSpec((planes, 2, RANK, HEAD), lambda r: (r // 4, 0, 0, r % 4)),
+            pl.BlockSpec((1, RANK, 8 * HEAD), lambda r: (r, 0, 0)),
+            pl.BlockSpec((1, RANK, width), lambda r: (r, 0, 0)),
+            pl.BlockSpec((1, 2, RANK, width), lambda r: (r, 0, 0, 0)),
+            pl.BlockSpec((ADAPTERS, 2, RANK, share), lambda r: (0, 0, 0, r)),
+            pl.BlockSpec((ADAPTERS, RANK, share), lambda r: (0, 0, r)),
+            pl.BlockSpec((1, RANK, width), lambda r: (r, 0, 0)),
+        ),
+        compiler_params=pltpu.CompilerParams(vmem_limit_bytes=62 << 20),
+        name="lay_out",
+    )(feed_rows, feed_columns, head_rows, head_columns)
 
 
 def shards(
@@ -1860,34 +1925,7 @@
         share_sum,
     )
 
-    feed_rows = feed_rows.reshape(ADAPTERS, 4, RANK, width)
-    feed_columns = (
-        feed_columns.reshape(8, 3, ADAPTERS, RANK, share)
-        .transpose(2, 1, 3, 0, 4)
-        .reshape(ADAPTERS, 3, RANK, ff)
-    )
-    head_rows = head_rows.reshape(ADAPTERS, 4, RANK, width)
-    head_columns = (
-        head_columns.reshape(2, 4, LANES // 2, 4 * HEAD)
-        .transpose(0, 2, 1, 3)
-        .reshape(ADAPTERS, RANK, 4, 4 * HEAD)
-    )
-
-    def joined(first, last):
-        return head_columns[..., first:last].reshape(ADAPTERS, RANK, -1)
-
-    summed = (
-        head_rows[:, :3],
-        joined(0, 2 * HEAD),
-        jnp.stack([joined(2 * HEAD, 3 * HEAD), joined(3 * HEAD, 4 * HEAD)], axis=1),
-        head_rows[:, 3, :, : mixed.shape[1]],
-        feed_rows[:, 3],
-        feed_rows[:, :2],
-        feed_columns[:, :2],
-        feed_columns[:, 2],
-        feed_rows[:, 2],
-    )
-    summed = tuple(table.astype(f32) for table in summed)
+    summed = lay_out(feed_rows, feed_columns, head_rows, head_columns)
     if dp_n > 2:
         summed = tuple(lax.psum(table * 0.5, "dp") for table in summed)
     return (layer_out, tokens_grad) + summed

time: 629 us -> 599 us (0.952)
  local copies, waits for them, and re-layouts: 19.7 us -> 6.34 us
  other arithmetic: 11.2 us -> 0.65 us
    pallas_call x1, Pallas kernels: 205 us -> 184 us  [attention_forward(): pl.pallas_call(attention_forward_kernel, out_shape=(shape((4, 2 * rows, H...]
    pallas_call x0 -> x1, Pallas kernels: none -> 14.4 us  [lay_out(): pl.pallas_call(lay_out_kernel, grid=(8,), out_shape=(shape((ADAPTERS, 3,...]
    convert_element_type x7 -> x0, other arithmetic: 10.4 us -> none  [shards(): summed = tuple((table.astype(f32) for table in summed))]
where the time goes in v4:
time: 599 us
  Pallas kernels  591 us (99%)
  local copies, waits for them, and re-layouts  6.34 us (1%)
    pallas_call x1, Pallas kernels, attention_forward(): pl.pallas_call(attention_forward_kernel, out_shape=(shape((4, 2 * rows, H...  184 us
    pallas_call x1, Pallas kernels, attention_backward(): pl.pallas_call(attention_backward_kernel, out_shape=(shape((rows, width),...  164 us
    pallas_call x1, Pallas kernels, feed_backward(): pl.pallas_call(feed_backward_kernel, out_shape=(shape((rows, width), bf16...  120 us
    pallas_call x1, Pallas kernels, feed_forward(): pl.pallas_call(feed_forward_kernel, out_shape=(shape((rows, width), bf16)...  109 us
    pallas_call x1, Pallas kernels, lay_out(): pl.pallas_call(lay_out_kernel, grid=(8,), out_shape=(shape((ADAPTERS, 3,...  14.4 us

profile of v4, /device:TPU:0, one launch (start us, length us, event | category | flops | bytes accessed | tf_op | source)
XLA Modules:
  0.0 598.7 jit_solution(9195659717977249959)
XLA Ops:
  0.6 0.7 stack.15
  1.4 0.7 stack.16
  2.1 0.7 stack.17
  2.8 0.7 stack.18
  3.5 0.7 pad_maximum_fusion.gains
  4.2 183.8 %attention_forward.1 = (bf16[4,512,256]{2,1,0:T(8,128)(2,1)}, bf16[4,2,2,256,256]{4,3,2,1,0:T(8,128)(2,1)}, bf16[2,2,256,256]{3,2,1,0:T(8,128)(2,1)}, bf16[4,256...) custom-call(bf16[256,2304]{1,0:T(8,128)(2,1)} %tokens_hbm.1, ...), custom_call_target="tpu_custom_call" | custom-call | tf_op jit(solution)/shard_map/attention_forward/pallas_call | solution.py:1110
  188.0 108.8 %feed_forward.1 = (bf16[256,2304]{1,0:T(8,128)(2,1)}, bf16[256,2304]{1,0:T(8,128)(2,1)}, bf16[4,3,512,128]{3,2,1,0:T(8,128)(2,1)}, bf16[4,512,2304]{2,1,0:T(8,128)(2,1)}, bf16[4,2,512,1152]{3,2,1,0:T(8,128)(2,1)}) custom-call(bf16[256,2304]{1,0:T(8,128)(2,1)} %get-tuple-element.52.own, bf16[256,2304]{1,0:T(8,128)(2,1)} %get-tuple-element.53.middle, ...), custom_call_target="tpu_custom_call" | custom-call | tf_op jit(solution)/shard_map/feed_forward/pallas_call | solution.py:545
  296.8 119.7 %feed_backward.1 = (bf16[256,2304]{1,0:T(8,128)(2,1)}, bf16[8,48,2304]{2,1,0:T(8,128)(2,1)}, bf16[4,96,1152]{2,1,0:T(8,128)(2,1)}) custom-call(bf16[256,2304]{1,0:T(8,128)(2,1)} %get-tuple-element.69.own, f32[2,16,128]{2,1,0:T(8,128)} %get-tuple-element.54.masks, bf16[128,2304]{1,0:T(8,128)(2,1)} %bitcast.6, ...), custom_call_target="tpu_custom_call" | custom-call | tf_op jit(solution)/shard_map/feed_backward/pallas_call | solution.py:578
  416.5 164.2 %attention_backward.1 = (f32[256,2304]{1,0:T(8,128)}, bf16[8,4,16,2304]{3,2,1,0:T(8,128)(2,1)}, bf16[8,4,96,1152]{3,2,1,0:T(8,128)(2,1)}, bf16[8,4,16,2304]{3,2,1,0:T(8,128)(2,1)}, bf16[8,4,16,1024]{3,2,1,0:T(8,128)(2,1)}) custom-call(bf16[256,2304]{1,0:T(8,128)(2,1)} %get-tuple-element.53.middle, bf16[256,2304]{1,0:T(8,128)(2,1)} %get-tuple-element.58.attn_out, ...), custom_call_target="tpu_custom_call" | custom-call | tf_op jit(solution)/shard_map/attention_backward/pallas_call | solution.py:1735
  580.7 0.0 copy-start.1
  580.7 14.4 %lay_out.1 = (f32[8,3,16,2304]{3,2,1,0:T(8,128)}, f32[8,16,2048]{2,1,0:T(8,128)}, f32[8,2,16,1024]{3,2,1,0:T(8,128)}, f32[8,16,2048]{2,1,0:T(8,128)}, f32[8,16,2...) custom-call(bf16[8,4,16,2304]{3,2,1,0:T(8,128)(2,1)} %get-tuple-elem, ...), custom_call_target="tpu_custom_call" | custom-call | tf_op jit(solution)/shard_map/lay_out/pallas_call | solution.py:1821
  595.2 0.0 copy-start
  595.2 0.0 copy-done.1
  595.2 1.0 copy.36
  596.2 1.1 copy-done
  597.3 1.4 copy.37
Async XLA Ops:
  580.7 14.5 %copy-start.1 = (bf16[256,2304]{1,0:T(8,128)(2,1)S(1)}, bf16[256,2304]{1,0:T(8,128)(2,1)}, u32[]{:S(2)}) copy-start(bf16[256,2304]{1,0:T(8,128)(2,1)} %get-tuple-element.104) | copy-start | bytes 3538948
  595.2 2.1 copy-start

commit v5 on v4

--- a/solution.py
+++ b/solution.py
@@ -283,11 +283,19 @@
     return out
 
 
+def weave_table(feed_out, woven_out):
+    woven_out[...] = jnp.zeros_like(woven_out)
+    for j in range(feed_out.shape[3] // 128):
+        for k in range(2):
+            at = j * 256 + k * 128
+            woven_out[k, :, :, at : at + 128] = feed_out[k, :, :, j * 128 : (j + 1) * 128]
+
+
 def feed_forward_kernel(
     own, middle, cotangent, gains, masks, down_out, feed_in_hbm, feed_out_hbm, down_in_hbm,
     gate_hbm, up_hbm, down_hbm,
     layer_out, grad_branch, narrow, feed_all, gate_up,
-    feed_in, feed_out, down_in, weave, down, land, hidden, saved, part, odd, from_core, from_x, from_y, diag,
+    narrow_two, woven_out, feed_in, feed_out, down_in, weave, down, land, hidden, saved, part, odd, from_core, from_x, from_y, diag,
     send, recv, load, store,
 ):
     rows = own.shape[0]
@@ -317,6 +325,7 @@
     land[0, :rows, :] = own[...]
     for c in loads:
         c.wait()
+    weave_table(feed_out, woven_out)
 
     def keep(i):
         slot = i % 2
@@ -336,15 +345,20 @@
                 c.wait()
 
         mask = plane_masks(masks, i, rows)
+        low = dot_nt(land[i], feed_in[...].reshape(2 * LANES, width))
         for k in range(2):
-            narrow[i, k] = (dot_nt(land[i], flat(feed_in[k])) * mask).astype(bf16)
+            lanes = slice(k * LANES, (k + 1) * LANES)
+            narrow_two[:, lanes] = (low[:, lanes] * mask).astype(bf16)
+            narrow[i, k] = narrow_two[:, lanes]
 
         @pl.loop(0, share // 128)
         def _(n):
             at = span(n, 128)
-            pre = dot_nn(land[i], weave[:, span(n, 256)])
-            g = pre[:, :128] + dot_nn(narrow[i, 0], flat(feed_out[0, :, :, at]))
-            u = pre[:, 128:] + dot_nn(narrow[i, 1], flat(feed_out[1, :, :, at]))
+            pair = span(n, 256)
+            pre = dot_nn(land[i], weave[:, pair]) + dot_nn(
+                narrow_two[...], woven_out[:, :, :, pair].reshape(2 * LANES, 256)
+            )
+            g, u = pre[:, :128], pre[:, 128:]
             saved[slot, 0, :, at] = g.astype(bf16)
             saved[slot, 1, :, at] = u.astype(bf16)
             th = jnp.tanh(GELU_SLOPE * (g + GELU_CUBE * g * g * g))
@@ -383,7 +397,7 @@
     gate_hbm, up_hbm, down_hbm, gate_up, feed_all,
     grad_feed, feed_table, share_sum,
     back, both, t_feed_out, t_down_in, t_down_out, share_table, share_in, share_piece,
-    feed_in, feed_out, down_in, weave, down, land, saved, gg, part, odd, from_core, from_x, from_y, diag,
+    woven_out, feed_in, feed_out, down_in, weave, down, land, saved, gg, part, odd, from_core, from_x, from_y, diag,
     send, recv, load, fetch,
 ):
     rows = own.shape[0]
@@ -426,6 +440,7 @@
     t_down_out[...] = jnp.zeros_like(t_down_out)
     for c in loads:
         c.wait()
+    weave_table(feed_out, woven_out)
 
     @pl.loop(0, 4)
     def _(i):
@@ -459,14 +474,10 @@
         def _():
             bring(i + 1).start()
 
+        low = dot_nt(gg[...], woven_out[...].reshape(2 * LANES, 2 * share))
         for k in range(2):
-            low = jnp.zeros((2 * rows, LANES), f32)
-            for j in range(share // 128):
-                at = j * 256 + k * 128
-                low = low + dot_nt(
-                    gg[:, at : at + 128], flat(feed_out[k, :, :, j * 128 : (j + 1) * 128])
-                )
-            both[i, :, k * LANES : (k + 1) * LANES] = (low * mask).astype(bf16)
+            lanes = slice(k * LANES, (k + 1) * LANES)
+            both[i, :, lanes] = (low[:, lanes] * mask).astype(bf16)
         reduce.before(i)
 
         @pl.loop(0, width // tile)
@@ -474,8 +485,7 @@
             at = span(n, tile)
             got = (
                 dot_nt(gg[...], weave[at, :])
-                + dot_nn(both[i, :, :LANES], flat(feed_in[0, :, :, at]))
-                + dot_nn(both[i, :, LANES:], flat(feed_in[1, :, :, at]))
+                + dot_nn(both[i], feed_in[:, :, :, at].reshape(2 * LANES, 256))
             ).astype(bf16)
             part[i, :, at] = got[:rows]
             odd[i % 2, :, at] = got[rows:]
@@ -553,7 +563,11 @@
         ),
         in_specs=[VM] * 6 + [ANY] * 6,
         out_specs=(VM, VM, VM, ANY, ANY),
-        scratch_shapes=feed_table_scratch(width, share)
+        scratch_shapes=[
+            pltpu.VMEM((2 * rows, 2 * LANES), bf16),
+            pltpu.VMEM((2, ADAPTERS, RANK, 2 * share), bf16),
+        ]
+        + feed_table_scratch(width, share)
         + [
             pltpu.VMEM((width, 2 * share), bf16),
             pltpu.VMEM(down.shape, bf16),
@@ -593,6 +607,7 @@
             pltpu.VMEM((3 * LANES, share), bf16),
             pltpu.VMEM((planes - 1, piece, share), bf16),
             pltpu.VMEM((piece, share), bf16),
+            pltpu.VMEM((2, ADAPTERS, RANK, 2 * share), bf16),
         ]
         + feed_table_scratch(width, share)
         + [
@@ -1434,6 +1449,8 @@
     at += TableReduce.COUNT
     feed_spread = TableSpread(place, copy, at, a_total, a_in, a_piece, g_feed_table, local.at[6])
     at += TableSpread.COUNT
+    kv_second = at
+    at += 3
     share_spread = PlaneSpread(place, copy, at, feed_share, g_feed_share)
     at += PlaneSpread.COUNT
     head_reduce = TableReduce(
@@ -1534,13 +1551,23 @@
     dq[...] = jnp.zeros_like(dq)
     kv_own[...] = jnp.zeros_like(kv_own)
 
-    def kv_copy(d):
-        return copy(6 + d - 1, kv_send.at[d - 1], kv_got.at[d - 1], place.up(d))
+    def kv_copy(d, n):
+        index = 6 + d - 1 if n == 0 else kv_second + d - 1
+        return copy(index, kv_send.at[d - 1, :, n], kv_got.at[d - 1, :, n], place.up(d))
 
     @pl.loop(1, planes)
     def _(d):
         zz = (z + d) % planes
         kv_far[...] = jnp.zeros_like(kv_far)
+        def ship(n):
+            for kind in range(2):
+                kv_send[d - 1, kind, n] = kv_far[kind, n].astype(bf16)
+            for k in range(1, planes):
+
+                @pl.when(d == k)
+                def _(k=k):
+                    kv_copy(k, n).start()
+
         step(1, kvp[zz, 0, 0], kvp[zz, 1, 0], kv_far, 0, False)
 
         @pl.when(zz < z)
@@ -1551,14 +1578,18 @@
         @pl.loop(2, 4)
         def _(t):
             step(t, kvp[zz, 0, 0], kvp[zz, 1, 0], kv_far, 0, False)
+
+        ship(0)
+
+        @pl.loop(2, 4)
+        def _(t):
             step(t, kvp[zz, 0, 1], kvp[zz, 1, 1], kv_far, 1, False)
 
-        kv_send[d - 1] = kv_far[...].astype(bf16)
+        ship(1)
         for k in range(1, planes):
 
             @pl.when(d == k)
             def _(k=k):
-                kv_copy(k).start()
                 if k == 1:
                     feed_reduce.merge()
                 if k == 2:
@@ -1568,7 +1599,6 @@
                     share_spread.corner()
 
     feed_reduce.finish()
-    feed_spread.scatter()
     step(0, kvp[z, 0, 0], kvp[z, 1, 0], kv_own, 0, True)
     step(1, kvp[z, 0, 0], kvp[z, 1, 0], kv_own, 0, False)
     step(1, kvp[z, 0, 1], kvp[z, 1, 1], kv_own, 1, True)
@@ -1580,9 +1610,9 @@
         step(t, kvp[z, 0, 1], kvp[z, 1, 1], kv_own, 1, False)
 
     late.wait()
-    feed_spread.gather()
     for d in range(1, planes):
-        kv_copy(d).wait_recv()
+        for n in range(2):
+            kv_copy(d, n).wait_recv()
         kv_own[:, 0:2] += kv_got[d - 1].astype(f32)
     half_head = HEAD // 2
 
@@ -1616,7 +1646,6 @@
                 dot_nt(grad_pre[at, lanes], flat(table[...])) * mask
             ).astype(bf16)
 
-    feed_spread.plane()
     for i, lanes in enumerate(
         (slice(0, 2 * HEAD), slice(2 * HEAD, 3 * HEAD), slice(3 * HEAD, 4 * HEAD))
     ):
@@ -1635,6 +1664,7 @@
                 h_table[a, i * RANK : (i + 1) * RANK, at] = got[first : first + RANK]
 
     head_reduce.begin()
+    feed_spread.scatter()
 
     def project(slot, target):
         at_rows = span(target, rows)
@@ -1652,7 +1682,6 @@
     project(0, place.b_yc)
     to_core[0].start()
     head_reduce.merge()
-    feed_spread.forward()
     project(2, place.b_y)
     head_reduce.corner()
     to_core[0].wait_recv()
@@ -1666,20 +1695,23 @@
         mine = pl.ds(pl.multiple_of(place.x * lanes_half + i * 16, 16), 16)
         o_total[at, :] = (o_table[mine, :].astype(f32) + o_got[at, :].astype(f32)).astype(bf16)
 
-    feed_spread.corner()
+    feed_spread.gather()
     out_spread.scatter()
     head_reduce.finish()
     head_spread.scatter()
     project(1, place.b_c)
     to_core[1].start()
+    feed_spread.plane()
     head_spread.gather()
     out_spread.gather()
     project(3, b)
     head_spread.plane()
     out_spread.plane()
+    feed_spread.forward()
     head_spread.forward()
     out_spread.forward()
     to_core[1].wait_recv()
+    feed_spread.corner()
     head_spread.corner()
     out_spread.corner()
     to_y.wait_recv()
@@ -1703,7 +1735,8 @@
     for c in to_core:
         c.wait_send()
     for d in range(1, planes):
-        kv_copy(d).wait_send()
+        for n in range(2):
+            kv_copy(d, n).wait_send()
 
 
 def attention_backward(rows_in, kept, grad_feed, tokens, tables, weights, feed_table, feed_share):
@@ -1713,7 +1746,7 @@
     hm = 4 * RANK
     ow = 4 * HEAD
     om = LANES // 2
-    count = 12 + 2 * TableReduce.COUNT + 3 * TableSpread.COUNT + PlaneSpread.COUNT + 1
+    count = 12 + 2 * TableReduce.COUNT + 3 * TableSpread.COUNT + PlaneSpread.COUNT + 4
 
     def reduce_scratch(m):
         return [
@@ -1894,7 +1927,7 @@
             for weight in weights
         )
     down_rows = weights[6]
-    gains = jnp.stack([attn_in_gain, attn_out_gain, feed_in_gain, feed_out_gain])
+    gains = jnp.concatenate([attn_in_gain, attn_out_gain, feed_in_gain, feed_out_gain]).reshape(4, -1)
     mix_in, mix_out, down_out = flat(adapt_mix_in), flat(adapt_mix_out), flat(adapt_down_out)
     head_tables = (adapt_heads_in, adapt_query_out, adapter_key_value_second)
     feed_tables = (adapt_feed_in, adapt_feed_out, adapt_down_in)

time: 599 us -> 586 us (0.978)
  Pallas kernels: 591 us -> 580 us
    pallas_call x1, Pallas kernels: 164 us -> 157 us  [attention_backward(): pl.pallas_call(attention_backward_kernel, out_shape=(shape((rows, width),...]
where the time goes in v5:
time: 586 us
  Pallas kernels  580 us (99%)
    pallas_call x1, Pallas kernels, attention_forward(): pl.pallas_call(attention_forward_kernel, out_shape=(shape((4, 2 * rows, H...  184 us
    pallas_call x1, Pallas kernels, attention_backward(): pl.pallas_call(attention_backward_kernel, out_shape=(shape((rows, width),...  157 us
    pallas_call x1, Pallas kernels, feed_backward(): pl.pallas_call(feed_backward_kernel, out_shape=(shape((rows, width), bf16...  118 us
    pallas_call x1, Pallas kernels, feed_forward(): pl.pallas_call(feed_forward_kernel, out_shape=(shape((rows, width), bf16)...  107 us
    pallas_call x1, Pallas kernels, lay_out(): pl.pallas_call(lay_out_kernel, grid=(8,), out_shape=(shape((ADAPTERS, 3,...  14.4 us

profile of v5, /device:TPU:0, one launch (start us, length us, event | category | flops | bytes accessed | tf_op | source)
XLA Modules:
  0.0 586.0 jit_solution(13462782713125353025)
XLA Ops:
  0.6 0.8 pad_maximum_fusion
  1.4 0.6 reshape.34.gains
  2.0 183.8 %attention_forward.1 = (bf16[4,512,256]{2,1,0:T(8,128)(2,1)}, bf16[4,2,2,256,256]{4,3,2,1,0:T(8,128)(2,1)}, bf16[2,2,256,256]{3,2,1,0:T(8,128)(2,1)}, bf16[4,256...) custom-call(bf16[256,2304]{1,0:T(8,128)(2,1)} %tokens_hbm.1, ...), custom_call_target="tpu_custom_call" | custom-call | tf_op jit(solution)/shard_map/attention_forward/pallas_call | solution.py:1125
  185.9 107.2 %feed_forward.1 = (bf16[256,2304]{1,0:T(8,128)(2,1)}, bf16[256,2304]{1,0:T(8,128)(2,1)}, bf16[4,3,512,128]{3,2,1,0:T(8,128)(2,1)}, bf16[4,512,2304]{2,1,0:T(8,128)(2,1)}, bf16[4,2,512,1152]{3,2,1,0:T(8,128)(2,1)}) custom-call(bf16[256,2304]{1,0:T(8,128)(2,1)} %get-tuple-element.52.own, bf16[256,2304]{1,0:T(8,128)(2,1)} %get-tuple-element.53.middle, ...), custom_call_target="tpu_custom_call" | custom-call | tf_op jit(solution)/shard_map/feed_forward/pallas_call | solution.py:555
  293.0 118.5 %feed_backward.1 = (bf16[256,2304]{1,0:T(8,128)(2,1)}, bf16[8,48,2304]{2,1,0:T(8,128)(2,1)}, bf16[4,96,1152]{2,1,0:T(8,128)(2,1)}) custom-call(bf16[256,2304]{1,0:T(8,128)(2,1)} %get-tuple-element.69.own, f32[2,16,128]{2,1,0:T(8,128)} %get-tuple-element.54.masks, bf16[128,2304]{1,0:T(8,128)(2,1)} %bitcast.6, ...), custom_call_target="tpu_custom_call" | custom-call | tf_op jit(solution)/shard_map/feed_backward/pallas_call | solution.py:592
  411.5 156.5 %attention_backward.1 = (f32[256,2304]{1,0:T(8,128)}, bf16[8,4,16,2304]{3,2,1,0:T(8,128)(2,1)}, bf16[8,4,96,1152]{3,2,1,0:T(8,128)(2,1)}, bf16[8,4,16,2304]{3,2,1,0:T(8,128)(2,1)}, bf16[8,4,16,1024]{3,2,1,0:T(8,128)(2,1)}) custom-call(bf16[256,2304]{1,0:T(8,128)(2,1)} %get-tuple-element.53.middle, bf16[256,2304]{1,0:T(8,128)(2,1)} %get-tuple-element.58.attn_out, ...), custom_call_target="tpu_custom_call" | custom-call | tf_op jit(solution)/shard_map/attention_backward/pallas_call | solution.py:1768
  568.1 0.0 copy-start.1
  568.1 14.4 %lay_out.1 = (f32[8,3,16,2304]{3,2,1,0:T(8,128)}, f32[8,16,2048]{2,1,0:T(8,128)}, f32[8,2,16,1024]{3,2,1,0:T(8,128)}, f32[8,16,2048]{2,1,0:T(8,128)}, f32[8,16,2...) custom-call(bf16[8,4,16,2304]{3,2,1,0:T(8,128)(2,1)} %get-tuple-elem, ...), custom_call_target="tpu_custom_call" | custom-call | tf_op jit(solution)/shard_map/lay_out/pallas_call | solution.py:1854
  582.5 0.0 copy-start
  582.5 0.0 copy-done.1
  582.6 1.0 copy.36
  583.6 1.1 copy-done
  584.6 1.4 copy.37
Async XLA Ops:
  568.1 14.5 %copy-start.1 = (bf16[256,2304]{1,0:T(8,128)(2,1)S(1)}, bf16[256,2304]{1,0:T(8,128)(2,1)}, u32[]{:S(2)}) copy-start(bf16[256,2304]{1,0:T(8,128)(2,1)} %get-tuple-element.104) | copy-start | bytes 3538948
  582.5 2.1 copy-start
